TPU v7x, 32 devices: a whole 2x2x4 slice. The times are simulated.
32 devices in a mesh: sub: 8 (over z, y), grp: 4 (over x, core).
Axes of the slice: x: 2, y: 2, z: 4, core: 2. Of those that a mesh axis runs over, the one named last changes fastest.
Arguments:
- multipliers: float32 [128, 32, 512], P(('sub', 'grp')), may hold values from -6 to 6
- residual: float32 [128, 32, 512], P(('sub', 'grp')), may hold values from -40 to 40
- old_direction: float32 [128, 32, 512], P(('sub', 'grp')), may hold values from -6 to 6
- old_norms: float32 [32], replicated, may hold values from 65536 to 524288
- matching: int32 [128, 512], P(('sub', 'grp')), may hold values from 0 to 511, each once within a row
- factor_inverse: bfloat16 [128, 1024, 1024], P(('sub', 'grp')), may hold values from -1 to 1.5, as said below
- rigid_modes: float32 [128, 6, 1024], P(('sub', 'grp')), may hold values from -0.4375 to 0.4375
- coarse_inverse: float32 [768, 768], P(('sub', 'grp')), may hold values from -1 to 1.6, as said below
Outputs:
- new_multipliers: float32 [128, 32, 512], P(('sub', 'grp'))
- new_residual: float32 [128, 32, 512], P(('sub', 'grp'))
- direction: float32 [128, 32, 512], P(('sub', 'grp'))
Inputs may be any that keep to these rules, and one draw needn't show every extreme that they name: `matching`: each row is a permutation of 0 to 511. `factor_inverse`: lower triangular with a positive diagonal. `coarse_inverse`: symmetric.
All inputs are finite; a program needn't handle non-finite values.
Results may differ from a plain program's by a relative error of at most 0.0021.
Values sent between devices are 32-bit elements; how exact they have to be, the bound alone decides.
No kernel may reach another device: no remote copies, remote signals or barrier semaphores. Data moves between devices by JAX's collectives and lax.ppermute only.
A program may use at most 64 MiB of HBM per device.

v0:
```python
import jax
import jax.numpy as jnp
from jax import lax
from jax.sharding import PartitionSpec as P


def shifted(block, axis, distance):
    devices = range(lax.axis_size(axis))
    route = [(i - distance, i) for i in devices if i - distance in devices]
    return lax.ppermute(block, axis, route)


def before_faces(values):
    incoming = shifted(values[values.shape[0] - 1 :], ("sub", "grp"), 1)
    return jnp.concatenate([incoming, values[:-1]], 0)


def interface(values, match_table, retain):
    before = before_faces(values)
    leftward = -jnp.einsum("sck,sjk->scj", before, match_table, precision=lax.Precision.HIGHEST)
    return jnp.concatenate([leftward, values * retain[:, None, None]], 2)


def assemble(local_sol, match_table, retain):
    middle = local_sol.shape[2] // 2
    leftpart = local_sol[:, :, :middle]
    returned = jnp.einsum("sci,sik->sck", leftpart, match_table, precision=lax.Precision.HIGHEST)
    incoming = shifted(returned[:1], ("sub", "grp"), -1)
    following = jnp.concatenate([returned[1:], incoming], 0)
    return (local_sol[:, :, middle:] - following) * retain[:, None, None]


def inner_sums(first_field, second_field):
    return lax.psum(jnp.sum(first_field * second_field, axis=(0, 2)), ("sub", "grp"))


def on_device(
    multipliers,
    residual,
    old_direction,
    old_norms,
    matching,
    factor_inverse,
    rigid_modes,
    coarse_inverse,
):
    count = multipliers.shape[0]
    cases = multipliers.shape[1]
    ranks = rigid_modes.shape[1]
    half_width = matching.shape[1]
    own_rows = count * ranks
    global_ids = lax.axis_index(("sub", "grp")) * count + jnp.arange(count, dtype=jnp.int32)
    total_subs = count * lax.axis_size(("sub", "grp"))
    retain = (global_ids != total_subs - 1).astype(jnp.float32)
    positions = lax.broadcasted_iota(jnp.int32, (1, 1, half_width), 2)
    match_table = (matching[:, :, None] == positions).astype(jnp.float32)
    masked = residual * retain[:, None, None]
    xres = interface(masked, match_table, retain)
    modes = jnp.einsum("smj,scj->smc", rigid_modes, xres, precision=lax.Precision.HIGHEST)
    modes = modes.reshape(own_rows, cases)
    coeffs = jnp.dot(
        coarse_inverse,
        lax.all_gather(modes, ("sub", "grp"), axis=0, tiled=True),
        precision=lax.Precision.HIGHEST,
    )
    coeffs = coeffs.reshape(count, ranks, cases)
    spread = jnp.einsum("smj,smc->scj", rigid_modes, coeffs, precision=lax.Precision.HIGHEST)
    projected = masked - assemble(spread, match_table, retain)
    norms = inner_sums(projected, projected)
    direction = (
        projected + (norms / old_norms)[None, :, None] * old_direction * retain[:, None, None]
    )
    xdir = interface(direction, match_table, retain).astype(jnp.bfloat16)
    inner = jnp.einsum(
        "scj,sij->sci", xdir, factor_inverse, preferred_element_type=jnp.float32
    ).astype(jnp.bfloat16)
    solved = jnp.einsum("sci,sij->scj", inner, factor_inverse, preferred_element_type=jnp.float32)
    image = assemble(solved, match_table, retain)
    curvature = inner_sums(direction, image)
    step_len = (norms / curvature)[None, :, None]
    return (multipliers + step_len * direction, masked - step_len * image, direction)


def solution(mesh):
    placed = (
        P(("sub", "grp"), None, None),
        P(("sub", "grp"), None, None),
        P(("sub", "grp"), None, None),
        P(),
        P(("sub", "grp"), None),
        P(("sub", "grp"), None, None),
        P(("sub", "grp"), None, None),
        P(("sub", "grp"), None),
    )
    return jax.shard_map(
        on_device,
        mesh=mesh,
        in_specs=placed,
        out_specs=(
            P(("sub", "grp"), None, None),
            P(("sub", "grp"), None, None),
            P(("sub", "grp"), None, None),
        ),
        check_vma=False,
    )
```

profile of v0, /device:TPU:0, one launch (start us, length us, event | category | flops | bytes accessed | tf_op | source)
XLA Modules:
  0.0 168.0 jit_solution(7167217824628758073)
XLA Ops:
  0.6 0.0 copy-start
  0.6 0.0 copy-start.4
  0.7 0.0 copy-start.5
  0.7 0.0 copy-start.3
  0.7 1.1 broadcast_multiply_fusion
  1.8 2.4 %collective-permute-start = (f32[1,32,512]{2,1,0:T(8,128)S(1)}, f32[1,32,512]{2,1,0:T(8,128)S(1)}, u32[]{:S(2)}, u32[]{:S(2)}) collective-permute-start(f32[1,32,512]{2,1,0:T(8,128)S(1)} %slice.48), channel_id=1, source_target_pairs={{0,1},{1,2},{2,3},{3,4},{4,5},{5,6},{6,7},{7,8},{8,9},{9,10},{10,1... | collective-permute-start | bytes 196616 | tf_op jit(solution)/shard_map/ppermute | solution.py:10
  4.2 0.9 collective-permute-done
  5.1 2.8 %fusion.8 = f32[4,32,512]{2,1,0:T(8,128)S(1)} fusion(s32[4,512]{1,0:T(4,128)} %param.12, f32[3,32,512]{2,1,0:T(8,128)S(1)} %slice.49, f32[1,32,512]{2,1,0:T(8,128)S(1)} %collective-permute-done), kind=kOutput, calls=%fused_computation.10 | convolution fusion | flops 403832832 | bytes 532480 | tf_op jit(solution)/shard_map/sck,sjk->scj/dot_general | solution.py:20
  7.9 0.0 copy-done
  7.9 0.6 convolution_bitcast_fusion
  8.5 46.6 %all_gather.3 = f32[768,32]{1,0:T(8,128)S(1)} all-gather(f32[24,32]{1,0:T(8,128)S(1)} %reshape.21), channel_id=1, replica_groups=mesh['sub'=8,'grp'=4] {'sub','grp'}, dimensions={0}, use_global_device_ids=true | all-gather | bytes 101376 | tf_op jit(solution)/shard_map/all_gather | solution.py:63
  55.1 1.2 convolution_bitcast_fusion.1
  56.4 0.7 fusion.32
  57.0 0.0 copy-done.4
  57.0 1.8 %fusion.2 = f32[4,32,512]{2,1,0:T(8,128)S(1)} fusion(s32[4,512]{1,0:T(4,128)S(1)} %copy-done.4, f32[4,32,1024]{2,1,0:T(8,128)S(1)} %fusion.32), kind=kOutput, calls=%fused_computation.3 | convolution fusion | flops 403701760 | bytes 532480 | tf_op jit(solution)/shard_map/sci,sik->sck/dot_general | solution.py:27
  58.9 1.3 collective-permute-start.1
  60.2 1.8 %collective-permute-done.1 = f32[1,32,512]{2,1,0:T(8,128)S(1)} collective-permute-done((f32[1,32,512]{2,1,0:T(8,128)S(1)}, f32[1,32,512]{2,1,0:T(8,128)S(1)}, u32[]{:S(2)}, u32[]{:S(2)}) %collective-permute-start.1) | collective-permute-done | bytes 65568 | tf_op jit(solution)/shard_map/ppermute | solution.py:10
  62.0 0.2 multiply_reduce_fusion.1
  62.2 37.7 %psum.14 = f32[32]{0:T(128)S(1)} all-reduce(f32[32]{0:T(128)S(1)} %get-tuple-element.5), channel_id=1, replica_groups=mesh['sub'=8,'grp'=4] {'sub','grp'}, use_global_device_ids=true, to_apply=%region_1.0 | all-reduce | flops 32 | bytes 256 | tf_op jit(solution)/shard_map/psum | solution.py:34
  99.9 0.0 copy-done.5
  99.9 0.0 copy-done.3
  99.9 0.1 multiply_convert_fusion
  100.0 0.0 copy-start.1
  100.1 1.3 collective-permute-start.2
  101.4 0.9 collective-permute-done.2
  102.2 2.4 %fusion.10 = bf16[4,32,512]{2,1,0:T(8,128)(2,1)S(1)} fusion(s32[4,512]{1,0:T(4,128)S(1)} %copy-done.4, f32[3,32,512]{2,1,0:T(8,128)S(1)} %slice.55, f32[1,32,512]{2,1,0:T(8,128)S(1)} %collective-permute-done.2), kind=kOutput, calls=%fused_computation.12 | convolution fusion | flops 403898368 | bytes 401408 | tf_op jit(solution)/shard_map/sck,sjk->scj/dot_general | solution.py:20
  104.6 0.0 copy-start.2
  104.6 9.8 %fusion.11 = f32[4,32,1024]{2,1,0:T(8,128)S(1)} fusion(bf16[4,1024,1024]{2,1,0:T(8,128)(2,1)} %param.13, bf16[4,32,512]{2,1,0:T(8,128)(2,1)S(1)} %get-tuple-element.3, bf16[4,32,512]{2,1,0:T(8,128)(2,1)S(1)} %fusion.10), kind=kOutput, calls=%fused_computation.15 | convolution fusion | flops 537526272 | bytes 9175040 | tf_op jit(solution)/shard_map/sci,sij->scj/dot_general | solution.py:77
  114.5 1.8 %fusion = f32[4,32,512]{2,1,0:T(8,128)S(1)} fusion(s32[4,512]{1,0:T(4,128)S(1)} %copy-done.4, f32[4,32,1024]{2,1,0:T(8,128)S(1)} %fusion.11), kind=kOutput, calls=%fused_computation.1 | convolution fusion | flops 403701760 | bytes 532480 | tf_op jit(solution)/shard_map/sci,sik->sck/dot_general | solution.py:27
  116.3 1.3 collective-permute-start.3
  117.6 4.8 %collective-permute-done.3 = f32[1,32,512]{2,1,0:T(8,128)S(1)} collective-permute-done((f32[1,32,512]{2,1,0:T(8,128)S(1)}, f32[1,32,512]{2,1,0:T(8,128)S(1)}, u32[]{:S(2)}, u32[]{:S(2)}) %collective-permute-start.3) | collective-permute-done | bytes 65568 | tf_op jit(solution)/shard_map/ppermute | solution.py:10
  122.4 0.2 multiply_reduce_fusion
  122.6 44.5 %psum.15 = f32[32]{0:T(128)S(1)} all-reduce(f32[32]{0:T(128)S(1)} %multiply_reduce_fusion), channel_id=1, replica_groups=mesh['sub'=8,'grp'=4] {'sub','grp'}, use_global_device_ids=true, to_apply=%region_3.0 | all-reduce | flops 32 | bytes 256 | tf_op jit(solution)/shard_map/psum | solution.py:34
  167.1 0.0 copy-done.1
  167.1 0.0 copy-done.2
  167.1 1.0 multiply_subtract_fusion
  (13 shorter events, 0.1 us)
Async XLA Ops:
  0.6 7.3 %copy-start = (f32[4,6,1024]{2,0,1:T(4,128)S(1)}, f32[4,6,1024]{2,0,1:T(4,128)}, u32[]{:S(2)}) copy-start(f32[4,6,1024]{2,0,1:T(4,128)} %param.14) | copy-start | bytes 294916
  0.6 56.4 %copy-start.4 = (s32[4,512]{1,0:T(4,128)S(1)}, s32[4,512]{1,0:T(4,128)}, u32[]{:S(2)}) copy-start(s32[4,512]{1,0:T(4,128)} %param.12) | copy-start | bytes 24580
  0.7 99.2 %copy-start.5 = (f32[32]{0:T(128)S(1)}, f32[32]{0:T(128)}, u32[]{:S(2)}) copy-start(f32[32]{0:T(128)} %param.11) | copy-start | bytes 388
  0.7 99.2 %copy-start.3 = (f32[4,32,512]{2,1,0:T(8,128)S(1)}, f32[4,32,512]{2,1,0:T(8,128)}, u32[]{:S(2)}) copy-start(f32[4,32,512]{2,1,0:T(8,128)} %param.10) | copy-start | bytes 786436
  1.8 3.2 %collective-permute-start = (f32[1,32,512]{2,1,0:T(8,128)S(1)}, f32[1,32,512]{2,1,0:T(8,128)S(1)}, u32[]{:S(2)}, u32[]{:S(2)}) collective-permute-start(f32[1,32,512]{2,1,0:T(8,128)S(1)} %slice.48), channel_id=1, source_target_pairs={{0,1},{1,2},{2,3},{3,4},{4,5},{5,6},{6,7},{7,8},{8,9},{9,10},{10,1... | collective-permute-start | bytes 196616 | tf_op jit(solution)/shard_map/ppermute | solution.py:10
  58.9 3.1 %collective-permute-start.1 = (f32[1,32,512]{2,1,0:T(8,128)S(1)}, f32[1,32,512]{2,1,0:T(8,128)S(1)}, u32[]{:S(2)}, u32[]{:S(2)}) collective-permute-start(f32[1,32,512]{2,1,0:T(8,128)S(1)} %slice.53), channel_id=1, source_target_pairs={{1,0},{2,1},{3,2},{4,3},{5,4},{6,5},{7,6},{8,7},{9,8},{10,9},{11,1... | collective-permute-start | bytes 196616 | tf_op jit(solution)/shard_map/ppermute | solution.py:10
  100.0 67.0 %copy-start.1 = (f32[4,32,512]{2,1,0:T(8,128)}, f32[4,32,512]{2,1,0:T(8,128)S(1)}, u32[]{:S(2)}) copy-start(f32[4,32,512]{2,1,0:T(8,128)S(1)} %get-tuple-element.4) | copy-start | bytes 786436
  100.1 2.2 %collective-permute-start.2 = (f32[1,32,512]{2,1,0:T(8,128)S(1)}, f32[1,32,512]{2,1,0:T(8,128)S(1)}, u32[]{:S(2)}, u32[]{:S(2)}) collective-permute-start(f32[1,32,512]{2,1,0:T(8,128)S(1)} %slice.54), channel_id=1, source_target_pairs={{0,1},{1,2},{2,3},{3,4},{4,5},{5,6},{6,7},{7,8},{8,9},{9,10},{10,1... | collective-permute-start | bytes 196616 | tf_op jit(solution)/shard_map/ppermute | solution.py:10
  104.6 62.4 %copy-start.2 = (f32[4,32,512]{2,1,0:T(8,128)S(1)}, f32[4,32,512]{2,1,0:T(8,128)}, u32[]{:S(2)}) copy-start(f32[4,32,512]{2,1,0:T(8,128)} %param.8) | copy-start | bytes 786436
  116.3 6.1 %collective-permute-start.3 = (f32[1,32,512]{2,1,0:T(8,128)S(1)}, f32[1,32,512]{2,1,0:T(8,128)S(1)}, u32[]{:S(2)}, u32[]{:S(2)}) collective-permute-start(f32[1,32,512]{2,1,0:T(8,128)S(1)} %slice.59), channel_id=1, source_target_pairs={{1,0},{2,1},{3,2},{4,3},{5,4},{6,5},{7,6},{8,7},{9,8},{10,9},{11,1... | collective-permute-start | bytes 196616 | tf_op jit(solution)/shard_map/ppermute | solution.py:10
where the time goes:
time: 169 us; the launch traced here: 168 us
  blocking collectives  129 us (76%)
  matrix products  21.1 us (12%)
  waiting for transfers between devices  8.3 us (5%)
  starting transfers between devices  6.24 us (4%)
  other arithmetic  2.64 us (2%)
    psum x2, blocking collectives, inner_sums(): lax.psum(jnp.sum(first_field * second_field, axis=(0, 2)), ('sub', 'grp'))  82.1 us
    all_gather x1, blocking collectives, on_device(): lax.all_gather(modes, ('sub', 'grp'), axis=0, tiled=True)  46.6 us
    dot_general x1, matrix products, on_device(): jnp.einsum('sci,sij->scj', inner, factor_inverse, preferred_element_type=...  9.82 us
    ppermute x4, waiting for transfers between devices, shifted(): return lax.ppermute(block, axis, route)  8.3 us
    ppermute x4, starting transfers between devices, shifted(): return lax.ppermute(block, axis, route)  6.24 us
    dot_general x2, matrix products, interface(): jnp.einsum('sck,sjk->scj', before, match_table, precision=lax.Precision.H...  5.22 us
    dot_general x2, matrix products, assemble(): jnp.einsum('sci,sik->sck', leftpart, match_table, precision=lax.Precision...  3.61 us
  transfers between devices with their start and end apart: 4, of which 4 were waited for; matrix products, arithmetic and copies ran while one was open for 0% of the time, Pallas kernels for 0%

commit v1 on v0

v1 whole, which is shorter than its diff:
```python
import functools

import jax
import jax.numpy as jnp
from jax import lax
from jax.experimental import pallas as pl
from jax.experimental.pallas import tpu as pltpu
from jax.sharding import PartitionSpec as P

AXES = ("sub", "grp")
HIGHEST = lax.Precision.HIGHEST
VMEM = pl.BlockSpec(memory_space=pltpu.VMEM)


def shifted(block, distance):
    devices = range(lax.axis_size(AXES))
    route = [(i - distance, i) for i in devices if i - distance in devices]
    return lax.ppermute(block, AXES, route)


def swapped(block, distance):
    route = [(i, i ^ distance) for i in range(lax.axis_size(AXES))]
    return lax.ppermute(block, AXES, route)


def rows_dot(first, second, precision=None):
    return lax.dot_general(
        first,
        second,
        (((1,), (1,)), ((), ())),
        precision=precision,
        preferred_element_type=jnp.float32,
    )


def plain_dot(first, second, precision=None):
    return lax.dot_general(
        first,
        second,
        (((1,), (0,)), ((), ())),
        precision=precision,
        preferred_element_type=jnp.float32,
    )


def halves(values):
    high = values.astype(jnp.bfloat16)
    low = (values - high.astype(jnp.float32)).astype(jnp.bfloat16)
    return high, low


def thirds(values):
    high = values.astype(jnp.bfloat16)
    rest = values - high.astype(jnp.float32)
    middle = rest.astype(jnp.bfloat16)
    low = (rest - middle.astype(jnp.float32)).astype(jnp.bfloat16)
    return high, middle, low


def match_table(row):
    width = row.shape[1]
    positions = lax.broadcasted_iota(jnp.int32, (width, width), 0)
    return (positions == row).astype(jnp.float32).astype(jnp.bfloat16)


def in_lane_block(values, lane_block, copies):
    cases = values.shape[1]
    wide = jnp.concatenate([values] * copies, axis=1)
    lanes = lax.broadcasted_iota(jnp.int32, wide.shape, 1)
    first = lane_block * cases
    inside = (lanes >= first) & (lanes < first + cases)
    return jnp.where(inside, wide, 0.0)


def prepare_kernel(
    copies,
    share,
    matching,
    modes_ref,
    residual,
    coarse,
    face_modes,
    own_sums,
    pack_next,
    pack_before,
    padded,
):
    count, ranks, _ = modes_ref.shape
    half = matching.shape[2]
    cases = residual.shape[1]
    me = lax.axis_index(AXES)
    is_last = me == lax.axis_size(AXES) - 1
    lane_block = me // share
    padded[...] = jnp.zeros_like(padded)
    for g in range(count):
        padded[g, 0:ranks, :] = modes_ref[g]
    for g in range(count):
        table = match_table(matching[g])
        left = padded[g, :, :half]
        high, middle, low = thirds(left)
        stacked = jnp.concatenate(
            [high.astype(jnp.float32), middle.astype(jnp.float32), low.astype(jnp.float32), left * 0.0],
            axis=0,
        ).astype(jnp.bfloat16)
        moved = rows_dot(stacked, table)
        face_modes[g] = moved[0:8] + moved[8:16] + moved[16:24]
    sums = [None] * count
    for g in range(count):
        field = residual[g]
        if g == count - 1:
            field = jnp.where(is_last, 0.0, field)
            sums[g] = (sums[g] if g else 0.0) + rows_dot(padded[g, :, half:], field, HIGHEST)
        else:
            both = jnp.concatenate([padded[g, :, half:], face_modes[g + 1]], axis=0)
            found = rows_dot(both, field, HIGHEST)
            sums[g] = found[0:8] + (sums[g] if g else 0.0)
            sums[g + 1] = -found[8:16]
    for g in range(count):
        own_sums[g * ranks : (g + 1) * ranks, :] = in_lane_block(sums[g], lane_block, copies)[0:ranks]
    pack_next[...] = jnp.zeros_like(pack_next)
    pack_before[...] = jnp.zeros_like(pack_before)
    pack_next[:, :half] = padded[count - 1, :, half:]
    pack_next[0:ranks, half:] = coarse[(count - 1) * ranks : count * ranks, :]
    pack_before[:, :half] = face_modes[0]
    pack_before[0:ranks, half:] = coarse[0:ranks, :]


def cross_kernel(copies, share, ranks, own_sums, face_modes, before_face, out):
    lane_block = lax.axis_index(AXES) // share
    cross = rows_dot(face_modes[0], before_face[0], HIGHEST)
    out[...] = own_sums[...]
    out[0:ranks, :] = own_sums[0:ranks, :] - in_lane_block(cross, lane_block, copies)[0:ranks]


def inner_kernel(
    matching,
    modes_ref,
    residual,
    old_direction,
    coarse,
    face_modes,
    before_residual,
    before_direction,
    from_before,
    from_next,
    factor,
    inner_res,
    inner_old,
    basis,
    coarse_ext,
    operand,
):
    g = pl.program_id(0)
    count, ranks, _ = modes_ref.shape
    half = matching.shape[2]
    full = 2 * half
    cases = residual.shape[1]
    rows = operand.shape[0] // 2
    me = lax.axis_index(AXES)
    is_last = (me == lax.axis_size(AXES) - 1) & (g == count - 1)
    is_first = (me == 0) & (g == 0)
    keep = jnp.where(is_last, 0.0, 1.0)
    keep_left = jnp.where(is_first, 0.0, 1.0)
    q = 2 * cases
    zeros8 = jnp.zeros((8, half), jnp.float32)
    zero2 = jnp.zeros((8 - ranks, half), jnp.float32)

    @pl.when(g == 0)
    def _():
        coarse_ext[...] = jnp.zeros_like(coarse_ext)
        coarse_ext[0:8, :] = from_before[:, half:]
        for s in range(count):
            coarse_ext[8 * (s + 1) : 8 * (s + 1) + ranks, :] = coarse[s * ranks : (s + 1) * ranks, :]
        coarse_ext[8 * (count + 1) : 8 * (count + 2), :] = from_next[:, half:]

    here = g
    prior = jnp.maximum(g - 1, 0)
    later = jnp.minimum(g + 1, count - 1)
    at_start = g == 0
    at_end = g == count - 1
    own = modes_ref[here]
    left_modes = jnp.concatenate([own[:, :half], zero2], axis=0)
    right_modes = jnp.concatenate([own[:, half:], zero2], axis=0)
    prior_modes = jnp.concatenate([modes_ref[prior][:, half:], zero2], axis=0)
    prior_modes = jnp.where(at_start, from_before[:, :half], prior_modes)
    next_faces = jnp.where(at_end, from_next[:, :half], face_modes[later])
    prior_res = jnp.where(at_start, before_residual[0], residual[prior])
    prior_old = jnp.where(at_start, before_direction[0], old_direction[prior])

    right = (
        jnp.concatenate(
            [residual[here], old_direction[here], zeros8, right_modes, -next_faces, zeros8], axis=0
        )
        * keep
    )
    right_high, right_low = halves(right)
    operand[0:rows, half:] = right_high
    operand[rows:, half:] = right_low

    moving = jnp.concatenate([prior_res, prior_old, prior_modes, zeros8], axis=0)
    high, low = halves(-moving)
    table = match_table(matching[here])
    moved = plain_dot(jnp.concatenate([high, low], axis=0), table)
    part = moving.shape[0]
    own_high, own_low = halves(left_modes * keep_left)
    own_high = own_high.astype(jnp.float32)
    own_low = own_low.astype(jnp.float32)
    operand[0:rows, :half] = jnp.concatenate(
        [moved[0 : q + 8], own_high, zeros8, zeros8], axis=0
    ).astype(jnp.bfloat16)
    operand[rows:, :half] = jnp.concatenate(
        [moved[part : part + q + 8], own_low, zeros8, zeros8], axis=0
    ).astype(jnp.bfloat16)

    block = min(256, full)
    for a in range(full // block):
        lanes = slice(a * block, (a + 1) * block)
        found = rows_dot(operand[:, : (a + 1) * block], factor[0, lanes, : (a + 1) * block])
        found = found[0:rows] + found[rows:]
        inner_res[0, :, lanes] = found[0:cases]
        inner_old[0, :, lanes] = found[cases:q]
        basis[0, :, half + a * block : half + (a + 1) * block] = found[q : q + 24]
    basis[0, :, :half] = right[q : q + 24]


def combine_kernel(
    copies,
    gathered,
    coarse_ext,
    basis,
    residual,
    inner_res,
    inner_old,
    projected,
    inner_proj,
    sums,
):
    count, cases, half = residual.shape
    me = lax.axis_index(AXES)
    is_last = me == lax.axis_size(AXES) - 1
    found = gathered[...]
    stacked = jnp.concatenate([found[:, b * cases : (b + 1) * cases] for b in range(copies)], axis=0)
    coeffs = plain_dot(coarse_ext[...], stacked, HIGHEST)
    width = 128
    totals = [jnp.zeros((cases, width), jnp.float32) for _ in range(4)]

    def folded(values):
        out = values[:, :width]
        for k in range(1, values.shape[1] // width):
            out = out + values[:, k * width : (k + 1) * width]
        return out

    for g in range(count):
        near = coeffs[8 * g : 8 * g + 24]
        spread = lax.dot_general(
            near,
            basis[g],
            (((0,), (0,)), ((), ())),
            precision=HIGHEST,
            preferred_element_type=jnp.float32,
        )
        field = residual[g]
        if g == count - 1:
            field = jnp.where(is_last, 0.0, field)
        proj = field - spread[:, :half]
        mine = inner_res[g] - spread[:, half:]
        other = inner_old[g]
        projected[g] = proj
        inner_proj[g] = mine
        totals[0] += folded(proj * proj)
        totals[1] += folded(mine * mine)
        totals[2] += folded(mine * other)
        totals[3] += folded(other * other)
    sums[...] = rows_dot(jnp.ones((8, width), jnp.float32), jnp.concatenate(totals, axis=0), HIGHEST)


def outer_kernel(matching, inner_proj, inner_old, factor, image_proj, image_old, returned, held):
    step = pl.program_id(0)
    half = matching.shape[2]
    cases = inner_proj.shape[1]
    full = 2 * half
    both = jnp.concatenate([inner_proj[0], inner_old[0]], axis=0)
    high, low = halves(both)
    operand = jnp.concatenate([high, low], axis=0)
    rows = 2 * cases
    block = min(256, full)
    pieces = []
    for b in range(full // block):
        found = plain_dot(operand[:, b * block :], factor[0, b * block :, b * block : (b + 1) * block])
        pieces.append(found[0:rows] + found[rows:])
    per_half = half // block
    left = jnp.concatenate(pieces[:per_half], axis=1)
    right = jnp.concatenate(pieces[per_half:], axis=1)
    following = jnp.where(step == 0, 0.0, held[...])
    result = right - following
    image_proj[0] = result[0:cases]
    image_old[0] = result[cases:]
    high, low = halves(left)
    moved = rows_dot(jnp.concatenate([high, low], axis=0), match_table(matching[0]))
    moved = moved[0:rows] + moved[rows:]
    held[...] = moved
    returned[...] = moved


def finish_kernel(
    sums,
    old_norms,
    multipliers,
    residual,
    old_direction,
    projected,
    image_proj,
    image_old,
    returned,
    new_multipliers,
    new_residual,
    direction,
):
    count, cases, half = residual.shape
    me = lax.axis_index(AXES)
    is_last = me == lax.axis_size(AXES) - 1
    diagonal = lax.broadcasted_iota(jnp.int32, (cases, cases), 0) == lax.broadcasted_iota(
        jnp.int32, (cases, cases), 1
    )

    def column(row):
        return jnp.sum(jnp.where(diagonal, row, 0.0), axis=1, keepdims=True)

    norms = sums[0:1, 0:cases]
    ratio = norms / old_norms[...]
    curvature = (
        sums[0:1, cases : 2 * cases]
        + 2.0 * ratio * sums[0:1, 2 * cases : 3 * cases]
        + ratio * ratio * sums[0:1, 3 * cases : 4 * cases]
    )
    step_len = column(norms / curvature)
    ratio = column(ratio)
    for g in range(count):
        field, old = residual[g], old_direction[g]
        proj_part, old_part = image_proj[g], image_old[g]
        if g == count - 1:
            keep = jnp.where(is_last, 0.0, 1.0)
            field, old = field * keep, old * keep
            proj_part = (proj_part - returned[0:cases]) * keep
            old_part = (old_part - returned[cases:]) * keep
        towards = projected[g] + ratio * old
        direction[g] = towards
        new_multipliers[g] = multipliers[g] + step_len * towards
        new_residual[g] = field - step_len * (proj_part + ratio * old_part)


def on_device(
    multipliers,
    residual,
    old_direction,
    old_norms,
    matching,
    factor_inverse,
    rigid_modes,
    coarse_inverse,
):
    count, cases, half = residual.shape
    ranks = rigid_modes.shape[1]
    full = factor_inverse.shape[1]
    coarse_rows, coarse_width = coarse_inverse.shape
    devices = lax.axis_size(AXES)
    copies = min(128 // cases, devices)
    share = devices // copies
    f32 = jnp.float32
    shape = jax.ShapeDtypeStruct
    matching = matching.reshape(count, 1, half)

    before_residual = shifted(residual[count - 1 :], 1)
    before_direction = shifted(old_direction[count - 1 :], 1)

    face_modes, own_sums, pack_next, pack_before = pl.pallas_call(
        functools.partial(prepare_kernel, copies, share),
        out_shape=(
            shape((count, 8, half), f32),
            shape((coarse_rows, copies * cases), f32),
            shape((8, half + coarse_width), f32),
            shape((8, half + coarse_width), f32),
        ),
        in_specs=[VMEM] * 4,
        out_specs=(VMEM,) * 4,
        scratch_shapes=[pltpu.VMEM((count, 8, full), f32)],
        name="prepare",
    )(matching, rigid_modes, residual, coarse_inverse)

    from_before = shifted(pack_next, 1)
    from_next = shifted(pack_before, -1)

    block = pl.pallas_call(
        functools.partial(cross_kernel, copies, share, ranks),
        out_shape=shape((coarse_rows, copies * cases), f32),
        in_specs=[VMEM] * 3,
        out_specs=VMEM,
        name="cross",
    )(own_sums, face_modes, before_residual)

    me = lax.axis_index(AXES)
    distance = devices // 2
    while distance >= share:
        block = block + swapped(block, distance)
        distance //= 2
    block = block[None]
    while distance >= 1:
        partner = swapped(block, distance)
        upper = (me & distance) != 0
        pair = jnp.where(
            upper, jnp.stack([partner, block], axis=1), jnp.stack([block, partner], axis=1)
        )
        block = pair.reshape(2 * block.shape[0], coarse_rows, copies * cases)
        distance //= 2
    gathered = block.reshape(share * coarse_rows, copies * cases)

    whole = lambda *dims: pl.BlockSpec(dims, lambda g: (0,) * len(dims))
    each = lambda *dims: pl.BlockSpec((1,) + dims, lambda g: (g,) + (0,) * len(dims))
    inner_res, inner_old, basis, coarse_ext = pl.pallas_call(
        inner_kernel,
        grid=(count,),
        out_shape=(
            shape((count, cases, full), f32),
            shape((count, cases, full), f32),
            shape((count, 24, half + full), f32),
            shape((8 * (count + 2), coarse_width), f32),
        ),
        in_specs=[
            whole(count, 1, half),
            whole(count, ranks, full),
            whole(count, cases, half),
            whole(count, cases, half),
            whole(coarse_rows, coarse_width),
            whole(count, 8, half),
            whole(1, cases, half),
            whole(1, cases, half),
            whole(8, half + coarse_width),
            whole(8, half + coarse_width),
            each(full, full),
        ],
        out_specs=(
            each(cases, full),
            each(cases, full),
            each(24, half + full),
            whole(8 * (count + 2), coarse_width),
        ),
        scratch_shapes=[pltpu.VMEM((2 * (2 * cases + 32), full), jnp.bfloat16)],
        compiler_params=pltpu.CompilerParams(vmem_limit_bytes=32 << 20),
        name="inner",
    )(
        matching,
        rigid_modes,
        residual,
        old_direction,
        coarse_inverse,
        face_modes,
        before_residual,
        before_direction,
        from_before,
        from_next,
        factor_inverse,
    )

    projected, inner_proj, sums = pl.pallas_call(
        functools.partial(combine_kernel, copies),
        out_shape=(
            shape((count, cases, half), f32),
            shape((count, cases, full), f32),
            shape((8, 4 * cases), f32),
        ),
        in_specs=[VMEM] * 6,
        out_specs=(VMEM,) * 3,
        compiler_params=pltpu.CompilerParams(vmem_limit_bytes=16 << 20),
        name="combine",
    )(gathered, coarse_ext, basis, residual, inner_res, inner_old)

    distance = devices // 2
    while distance >= 1:
        sums = sums + swapped(sums, distance)
        distance //= 2

    backward = lambda *dims: pl.BlockSpec(
        (1,) + dims, lambda s: (count - 1 - s,) + (0,) * len(dims)
    )
    image_proj, image_old, returned = pl.pallas_call(
        outer_kernel,
        grid=(count,),
        out_shape=(
            shape((count, cases, half), f32),
            shape((count, cases, half), f32),
            shape((2 * cases, half), f32),
        ),
        in_specs=[
            backward(1, half),
            backward(cases, full),
            backward(cases, full),
            backward(full, full),
        ],
        out_specs=(backward(cases, half), backward(cases, half), whole(2 * cases, half)),
        scratch_shapes=[pltpu.VMEM((2 * cases, half), f32)],
        compiler_params=pltpu.CompilerParams(vmem_limit_bytes=32 << 20),
        name="outer",
    )(matching, inner_proj, inner_old, factor_inverse)

    returned = shifted(returned, -1)

    return pl.pallas_call(
        finish_kernel,
        out_shape=(shape((count, cases, half), f32),) * 3,
        in_specs=[VMEM] * 9,
        out_specs=(VMEM,) * 3,
        compiler_params=pltpu.CompilerParams(vmem_limit_bytes=16 << 20),
        name="finish",
    )(
        sums,
        old_norms.reshape(1, cases),
        multipliers,
        residual,
        old_direction,
        projected,
        image_proj,
        image_old,
        returned,
    )


def solution(mesh):
    placed = (
        P(AXES, None, None),
        P(AXES, None, None),
        P(AXES, None, None),
        P(),
        P(AXES, None),
        P(AXES, None, None),
        P(AXES, None, None),
        P(AXES, None),
    )
    return jax.shard_map(
        on_device,
        mesh=mesh,
        in_specs=placed,
        out_specs=(P(AXES, None, None),) * 3,
        check_vma=False,
    )
```

time: 169 us -> 81.2 us (0.48)
  blocking collectives: 129 us -> 0 us
  starting transfers between devices: 6.24 us -> 30 us
  matrix products: 21.1 us -> 0 us
  local copies, waits for them, and re-layouts: 0.13 us -> 14.7 us
  waiting for transfers between devices: 8.3 us -> 21.9 us
  Pallas kernels: 0 us -> 12.3 us
  other arithmetic: 2.64 us -> 0.76 us
    psum x2 -> x0, blocking collectives: 82.1 us -> none  [inner_sums(): lax.psum(jnp.sum(first_field * second_field, axis=(0, 2)), ('sub', 'grp'))]
    all_gather x1 -> x0, blocking collectives: 46.6 us -> none  [on_device(): lax.all_gather(modes, ('sub', 'grp'), axis=0, tiled=True)]
    ppermute x4 -> x15, starting transfers between devices: 6.24 us -> 30 us  [the longest x10 21.8 us: swapped(): return lax.ppermute(block, AXES, route)]
    dot_general x8 -> x0, matrix products: 21.1 us -> none  [the longest x1 9.82 us: on_device(): jnp.einsum('sci,sij->scj', inner, factor_inverse, preferred_element_type=...]
    ppermute x4 -> x15, waiting for transfers between devices: 8.3 us -> 21.9 us  [the longest x10 18.9 us: swapped(): return lax.ppermute(block, AXES, route)]
    pallas_call x0 -> x6, Pallas kernels: none -> 12.3 us  [the longest x1 3.05 us: on_device(): pl.pallas_call(inner_kernel, grid=(count,), out_shape=(shape((count, case...]
    unnamed x12 -> x25, local copies, waits for them, and re-layouts: 0.04 us -> 11.7 us
  transfers between devices with their start and end apart: 4 -> 15, of which waited for: 4 -> 9; matrix products, arithmetic and copies ran while one was open for 0% -> 5% of each run, Pallas kernels for 0% -> 7%
where the time goes in v1:
time: 81.2 us; the launch traced here: 80.4 us
  starting transfers between devices  30 us (37%)
  waiting for transfers between devices  21.9 us (27%)
  local copies, waits for them, and re-layouts  14.7 us (18%)
  Pallas kernels  12.3 us (15%)
    ppermute x10, starting transfers between devices, swapped(): return lax.ppermute(block, AXES, route)  21.8 us
    ppermute x10, waiting for transfers between devices, swapped(): return lax.ppermute(block, AXES, route)  18.9 us
    unnamed x25, local copies, waits for them, and re-layouts  11.7 us
    ppermute x5, starting transfers between devices, shifted(): return lax.ppermute(block, AXES, route)  8.13 us
    pallas_call x1, Pallas kernels, on_device(): pl.pallas_call(inner_kernel, grid=(count,), out_shape=(shape((count, case...  3.05 us
    ppermute x5, waiting for transfers between devices, shifted(): return lax.ppermute(block, AXES, route)  2.99 us
    pallas_call x1, Pallas kernels, on_device(): pl.pallas_call(functools.partial(prepare_kernel, copies, share), out_shap...  2.71 us
    pallas_call x1, Pallas kernels, on_device(): pl.pallas_call(outer_kernel, grid=(count,), out_shape=(shape((count, case...  2.26 us
  transfers between devices with their start and end apart: 15, of which 9 were waited for; matrix products, arithmetic and copies ran while one was open for 5% of the time, Pallas kernels for 7%

profile of v1, /device:TPU:0, one launch (start us, length us, event | category | flops | bytes accessed | tf_op | source)
XLA Modules:
  0.0 80.4 jit_solution(15720485880037075334)
XLA Ops:
  0.6 0.8 %slice.6 = f32[1,32,512]{2,1,0:T(8,128)S(1)} slice(f32[4,32,512]{2,1,0:T(8,128)} %residual.7), slice={[3:4], [0:32], [0:512]} | slice | bytes 131072 | tf_op jit(solution)/shard_map/slice | solution.py:373
  1.5 2.3 %collective-permute-start = (f32[1,32,512]{2,1,0:T(8,128)S(1)}, f32[1,32,512]{2,1,0:T(8,128)S(1)}, u32[]{:S(2)}, u32[]{:S(2)}) collective-permute-start(f32[1,32,512]{2,1,0:T(8,128)S(1)} %slice.6), channel_id=1, source_target_pairs={{0,1},{1,2},{2,3},{3,4},{4,5},{5,6},{6,7},{7,8},{8,9},{9,10},{10,1... | collective-permute-start | bytes 196616 | tf_op jit(solution)/shard_map/ppermute | solution.py:18
  3.8 1.3 %reshape.121.matching = s32[4,1,512]{2,1,0:T(1,128)} reshape(s32[4,512]{1,0:T(4,128)} %param.12) | data formatting | bytes 16384 | tf_op jit(solution)/shard_map/reshape | solution.py:371
  5.1 1.6 %copy.11.modes_ref = f32[4,6,1024]{2,1,0:T(8,128)} copy(f32[4,6,1024]{2,0,1:T(4,128)} %param.14) | data formatting | bytes 196608 | tf_op args[6]
  6.7 2.7 %prepare.1 = (f32[4,8,512]{2,1,0:T(8,128)}, f32[24,128]{1,0:T(8,128)}, f32[8,1280]{1,0:T(8,128)}, f32[8,1280]{1,0:T(8,128)}) custom-call(s32[4,1,512]{2,1,0:T(1,128)} %reshape.121.matching, f32[4,6,1024]{2,1,0:T(8,128)} %copy.11.modes_ref, f32[4,32,512]{2,1,0:T(8,128)} %residual.7, f32[24,768]{1,0:T(8,128)} %coarse.3), custom_call_target="tpu_custom_call" | custom-call | tf_op jit(solution)/shard_map/prepare/pallas_call | solution.py:376
  9.4 0.0 collective-permute-done.before_face.before_residual
  9.4 0.6 copy-done.6
  10.1 1.7 %cross.1 = f32[24,128]{1,0:T(8,128)} custom-call(f32[24,128]{1,0:T(8,128)} %get-tuple-element.17.own_sums, f32[4,8,512]{2,1,0:T(8,128)} %get-tuple-element.18.face_modes, f32[1,32,512]{2,1,0:T(8,128)} %copy-done.6), custom_call_target="tpu_custom_call" | custom-call | tf_op jit(solution)/shard_map/cross/pallas_call | solution.py:393
  11.8 3.6 %collective-permute-start.1 = (f32[24,128]{1,0:T(8,128)}, f32[24,128]{1,0:T(8,128)S(1)}, u32[]{:S(2)}, u32[]{:S(2)}) collective-permute-start(f32[24,128]{1,0:T(8,128)} %cross.1), channel_id=1, source_target_pairs={{0,16},{1,17},{2,18},{3,19},{4,20},{5,21},{6,22},{7,23},{8,24},{9,... | collective-permute-start | bytes 36872 | tf_op jit(solution)/shard_map/ppermute | solution.py:23
  15.4 1.9 %collective-permute-done.1 = f32[24,128]{1,0:T(8,128)S(1)} collective-permute-done((f32[24,128]{1,0:T(8,128)}, f32[24,128]{1,0:T(8,128)S(1)}, u32[]{:S(2)}, u32[]{:S(2)}) %collective-permute-start.1) | collective-permute-done | bytes 12320 | tf_op jit(solution)/shard_map/ppermute | solution.py:23
  17.3 0.7 add.25
  18.0 1.9 %collective-permute-start.2 = (f32[24,128]{1,0:T(8,128)S(1)}, f32[24,128]{1,0:T(8,128)S(1)}, u32[]{:S(2)}, u32[]{:S(2)}) collective-permute-start(f32[24,128]{1,0:T(8,128)S(1)} %add.25), channel_id=1, source_target_pairs={{0,8},{1,9},{2,10},{3,11},{4,12},{5,13},{6,14},{7,15},{8,0},{9,1},... | collective-permute-start | bytes 36872 | tf_op jit(solution)/shard_map/ppermute | solution.py:23
  19.9 1.8 %collective-permute-done.2 = f32[24,128]{1,0:T(8,128)S(1)} collective-permute-done((f32[24,128]{1,0:T(8,128)S(1)}, f32[24,128]{1,0:T(8,128)S(1)}, u32[]{:S(2)}, u32[]{:S(2)}) %collective-permute-start.2) | collective-permute-done | bytes 12320 | tf_op jit(solution)/shard_map/ppermute | solution.py:23
  21.7 1.9 %collective-permute-start.3 = (f32[1,24,128]{2,1,0:T(8,128)S(1)}, f32[1,24,128]{2,1,0:T(8,128)S(1)}, u32[]{:S(2)}, u32[]{:S(2)}) collective-permute-start(f32[1,24,128]{2,1,0:T(8,128)S(1)} %get-tuple-element.31), channel_id=1, source_target_pairs={{0,4},{1,5},{2,6},{3,7},{4,0},{5,1},{6,2},{7,3},{8,12},{9,13},{10,... | collective-permute-start | bytes 36872 | tf_op jit(solution)/shard_map/ppermute | solution.py:23
  23.5 0.8 %slice.7 = f32[1,32,512]{2,1,0:T(8,128)S(1)} slice(f32[4,32,512]{2,1,0:T(8,128)} %old_direction.3), slice={[3:4], [0:32], [0:512]} | slice | bytes 131072 | tf_op jit(solution)/shard_map/slice | solution.py:374
  24.4 1.3 %collective-permute-start.6 = (f32[1,32,512]{2,1,0:T(8,128)S(1)}, f32[1,32,512]{2,1,0:T(8,128)S(1)}, u32[]{:S(2)}, u32[]{:S(2)}) collective-permute-start(f32[1,32,512]{2,1,0:T(8,128)S(1)} %slice.7), channel_id=1, source_target_pairs={{0,1},{1,2},{2,3},{3,4},{4,5},{5,6},{6,7},{7,8},{8,9},{9,10},{10,1... | collective-permute-start | bytes 196616 | tf_op jit(solution)/shard_map/ppermute | solution.py:18
  25.7 2.2 %collective-permute-start.4 = (f32[2,24,128]{2,1,0:T(8,128)S(1)}, f32[2,24,128]{2,1,0:T(8,128)S(1)}, u32[]{:S(2)}, u32[]{:S(2)}) collective-permute-start(f32[2,24,128]{2,1,0:T(8,128)S(1)} %maximum_select_fusion.2), channel_id=1, source_target_pairs={{0,2},{1,3},{2,0},{3,1},{4,6},{5,7},{6,4},{7,5},{8,10},{9,11},{10,... | collective-permute-start | bytes 73736 | tf_op jit(solution)/shard_map/ppermute | solution.py:23
  27.9 1.9 %collective-permute-done.4 = f32[2,24,128]{2,1,0:T(8,128)S(1)} collective-permute-done((f32[2,24,128]{2,1,0:T(8,128)S(1)}, f32[2,24,128]{2,1,0:T(8,128)S(1)}, u32[]{:S(2)}, u32[]{:S(2)}) %collective-permute-start.4) | collective-permute-done | bytes 24608 | tf_op jit(solution)/shard_map/ppermute | solution.py:23
  29.8 0.8 %collective-permute-start.5 = (f32[4,24,128]{2,1,0:T(8,128)S(1)}, f32[4,24,128]{2,1,0:T(8,128)S(1)}, u32[]{:S(2)}, u32[]{:S(2)}) collective-permute-start(f32[4,24,128]{2,1,0:T(8,128)S(1)} %bitcast.15), channel_id=1, source_target_pairs={{0,1},{1,0},{2,3},{3,2},{4,5},{5,4},{6,7},{7,6},{8,9},{9,8},{10,11... | collective-permute-start | bytes 147464 | tf_op jit(solution)/shard_map/ppermute | solution.py:23
  30.7 1.9 %collective-permute-start.7 = (f32[8,1280]{1,0:T(8,128)}, f32[8,1280]{1,0:T(8,128)S(1)}, u32[]{:S(2)}, u32[]{:S(2)}) collective-permute-start(f32[8,1280]{1,0:T(8,128)} %get-tuple-element.19), channel_id=1, source_target_pairs={{0,1},{1,2},{2,3},{3,4},{4,5},{5,6},{6,7},{7,8},{8,9},{9,10},{10,1... | collective-permute-start | bytes 122888 | tf_op jit(solution)/shard_map/ppermute | solution.py:18
  32.6 1.3 %collective-permute-start.8 = (f32[8,1280]{1,0:T(8,128)}, f32[8,1280]{1,0:T(8,128)S(1)}, u32[]{:S(2)}, u32[]{:S(2)}) collective-permute-start(f32[8,1280]{1,0:T(8,128)} %get-tuple-element.20), channel_id=1, source_target_pairs={{1,0},{2,1},{3,2},{4,3},{5,4},{6,5},{7,6},{8,7},{9,8},{10,9},{11,1... | collective-permute-start | bytes 122888 | tf_op jit(solution)/shard_map/ppermute | solution.py:18
  33.9 0.0 copy-start.11
  33.9 3.0 %collective-permute-done.8.from_next = f32[8,1280]{1,0:T(8,128)S(1)} collective-permute-done((f32[8,1280]{1,0:T(8,128)}, f32[8,1280]{1,0:T(8,128)S(1)}, u32[]{:S(2)}, u32[]{:S(2)}) %collective-permute-start.8) | collective-permute-done | bytes 40992 | tf_op jit(solution)/shard_map/ppermute | solution.py:18
  36.9 0.0 collective-permute-done.6.before_direction
  36.9 3.4 %copy-done = bf16[4,1024,1024]{2,1,0:T(8,128)(2,1)S(1)} copy-done((bf16[4,1024,1024]{2,1,0:T(8,128)(2,1)S(1)}, bf16[4,1024,1024]{2,1,0:T(8,128)(2,1)}, u32[]{:S(2)}) %copy-start) | copy-done | bytes 8388632
  40.3 0.9 %copy-done.2 = f32[4,32,512]{2,1,0:T(8,128)S(1)} copy-done((f32[4,32,512]{2,1,0:T(8,128)S(1)}, f32[4,32,512]{2,1,0:T(8,128)}, u32[]{:S(2)}) %copy-start.2) | copy-done | bytes 262168
  41.2 0.9 %copy-done.3 = f32[4,32,512]{2,1,0:T(8,128)S(1)} copy-done((f32[4,32,512]{2,1,0:T(8,128)S(1)}, f32[4,32,512]{2,1,0:T(8,128)}, u32[]{:S(2)}) %copy-start.3) | copy-done | bytes 262168
  42.2 0.9 %copy-done.4 = f32[4,6,1024]{2,1,0:T(8,128)S(1)} copy-done((f32[4,6,1024]{2,1,0:T(8,128)S(1)}, f32[4,6,1024]{2,1,0:T(8,128)}, u32[]{:S(2)}) %copy-start.4) | copy-done | bytes 98328
  43.1 0.9 %copy-done.5 = f32[24,768]{1,0:T(8,128)S(1)} copy-done((f32[24,768]{1,0:T(8,128)S(1)}, f32[24,768]{1,0:T(8,128)}, u32[]{:S(2)}) %copy-start.5) | copy-done | bytes 73752
  44.0 0.8 %copy-done.7 = f32[1,32,512]{2,1,0:T(8,128)S(1)} copy-done((f32[1,32,512]{2,1,0:T(8,128)S(1)}, f32[1,32,512]{2,1,0:T(8,128)}, u32[]{:S(2)}) %copy-start.7) | copy-done | bytes 65560
  44.8 0.8 %copy-done.8 = f32[4,8,512]{2,1,0:T(8,128)S(1)} copy-done((f32[4,8,512]{2,1,0:T(8,128)S(1)}, f32[4,8,512]{2,1,0:T(8,128)}, u32[]{:S(2)}) %copy-start.8) | copy-done | bytes 65560
  45.7 0.7 copy-done.10
  46.4 3.1 %inner.1 = (f32[4,32,1024]{2,1,0:T(8,128)S(1)}, f32[4,32,1024]{2,1,0:T(8,128)S(1)}, f32[4,24,1536]{2,1,0:T(8,128)S(1)}, f32[48,768]{1,0:T(8,128)S(1)}) custom-call(s32[4,1,512]{2,1,0:T(1,128)S(1)} %copy-done.10, f32[4,6,1024]{2,1,0:T(8,128)S(1)} %copy-done.4, f32[4,32,512]{2,1,0:T(8,128)S(1)} %copy-done.2, f32[4,32,512]{2,1,0:T(8,128)S(1)} %copy-done.3, ...), custom_call_target="tpu_custom_call" | custom-call | tf_op jit(solution)/shard_map/inner/pallas_call | solution.py:419
  49.4 0.0 collective-permute-done.5
  49.5 1.4 %combine.1 = (f32[4,32,512]{2,1,0:T(8,128)S(1)}, f32[4,32,1024]{2,1,0:T(8,128)S(1)}, f32[8,128]{1,0:T(8,128)S(1)}) custom-call(f32[192,128]{1,0:T(8,128)S(1)} %bitcast.13, f32[48,768]{1,0:T(8,128)S(1)} %get-tuple-element.21.coarse_ext, f32[4,24,1536]{2,1,0:T(8,128)S(1)} %get-tuple-element.22.basis, f32[4,32,512]{2,1,0:T(8,128)S(1)} %copy-done.2, ...), custom_call_target="tpu_custom_call" | custom-call | tf_op jit(solution)/shard_map/combine/pallas_call | solution.py:464
  50.8 2.3 %outer.1 = (f32[4,32,512]{2,1,0:T(8,128)S(1)}, f32[4,32,512]{2,1,0:T(8,128)S(1)}, f32[64,512]{1,0:T(8,128)S(1)}) custom-call(s32[4,1,512]{2,1,0:T(1,128)S(1)} %copy-done.10, f32[4,32,1024]{2,1,0:T(8,128)S(1)} %get-tuple-element.27.inner_proj, f32[4,32,1024]{2,1,0:T(8,128)S(1)} %get-tuple-element.24.inner_old, bf16[4,1024,1024]{2,1,0:T(8,128)(2,1)S(1)} %copy-done.1), custom_call_target="tpu_custom_call" | custom-call | tf_op jit(solution)/shard_map/outer/pallas_call | solution.py:485
  53.1 1.3 %collective-permute-start.14 = (f32[64,512]{1,0:T(8,128)S(1)}, f32[64,512]{1,0:T(8,128)S(1)}, u32[]{:S(2)}, u32[]{:S(2)}) collective-permute-start(f32[64,512]{1,0:T(8,128)S(1)} %get-tuple-element.30), channel_id=1, source_target_pairs={{1,0},{2,1},{3,2},{4,3},{5,4},{6,5},{7,6},{8,7},{9,8},{10,9},{11,1... | collective-permute-start | bytes 393224 | tf_op jit(solution)/shard_map/ppermute | solution.py:18
  54.4 9.8 %collective-permute-start.9 = (f32[8,128]{1,0:T(8,128)S(1)}, f32[8,128]{1,0:T(8,128)S(1)}, u32[]{:S(2)}, u32[]{:S(2)}) collective-permute-start(f32[8,128]{1,0:T(8,128)S(1)} %get-tuple-element.25), channel_id=1, source_target_pairs={{0,16},{1,17},{2,18},{3,19},{4,20},{5,21},{6,22},{7,23},{8,24},{9,... | collective-permute-start | bytes 12296 | tf_op jit(solution)/shard_map/ppermute | solution.py:23
  64.2 2.9 %collective-permute-done.9 = f32[8,128]{1,0:T(8,128)S(1)} collective-permute-done((f32[8,128]{1,0:T(8,128)S(1)}, f32[8,128]{1,0:T(8,128)S(1)}, u32[]{:S(2)}, u32[]{:S(2)}) %collective-permute-start.9) | collective-permute-done | bytes 4128 | tf_op jit(solution)/shard_map/ppermute | solution.py:23
  67.1 1.6 %collective-permute-start.10 = (f32[8,128]{1,0:T(8,128)S(1)}, f32[8,128]{1,0:T(8,128)S(1)}, u32[]{:S(2)}, u32[]{:S(2)}) collective-permute-start(f32[8,128]{1,0:T(8,128)S(1)} %add.27), channel_id=1, source_target_pairs={{0,8},{1,9},{2,10},{3,11},{4,12},{5,13},{6,14},{7,15},{8,0},{9,1},... | collective-permute-start | bytes 12296 | tf_op jit(solution)/shard_map/ppermute | solution.py:23
  68.8 2.0 %collective-permute-done.10 = f32[8,128]{1,0:T(8,128)S(1)} collective-permute-done((f32[8,128]{1,0:T(8,128)S(1)}, f32[8,128]{1,0:T(8,128)S(1)}, u32[]{:S(2)}, u32[]{:S(2)}) %collective-permute-start.10) | collective-permute-done | bytes 4128 | tf_op jit(solution)/shard_map/ppermute | solution.py:23
  70.7 0.0 collective-permute-start.11
  70.8 3.6 %collective-permute-done.11 = f32[8,128]{1,0:T(8,128)S(1)} collective-permute-done((f32[8,128]{1,0:T(8,128)S(1)}, f32[8,128]{1,0:T(8,128)S(1)}, u32[]{:S(2)}, u32[]{:S(2)}) %collective-permute-start.11) | collective-permute-done | bytes 4128 | tf_op jit(solution)/shard_map/ppermute | solution.py:23
  74.4 0.0 collective-permute-start.12
  74.4 3.6 %collective-permute-done.12 = f32[8,128]{1,0:T(8,128)S(1)} collective-permute-done((f32[8,128]{1,0:T(8,128)S(1)}, f32[8,128]{1,0:T(8,128)S(1)}, u32[]{:S(2)}, u32[]{:S(2)}) %collective-permute-start.12) | collective-permute-done | bytes 4128 | tf_op jit(solution)/shard_map/ppermute | solution.py:23
  78.0 0.0 collective-permute-start.13
  78.0 1.2 %collective-permute-done.13 = f32[8,128]{1,0:T(8,128)S(1)} collective-permute-done((f32[8,128]{1,0:T(8,128)S(1)}, f32[8,128]{1,0:T(8,128)S(1)}, u32[]{:S(2)}, u32[]{:S(2)}) %collective-permute-start.13) | collective-permute-done | bytes 4128 | tf_op jit(solution)/shard_map/ppermute | solution.py:23
  79.2 1.2 %finish.1 = (f32[4,32,512]{2,1,0:T(8,128)}, f32[4,32,512]{2,1,0:T(8,128)}, f32[4,32,512]{2,1,0:T(8,128)}) custom-call(f32[8,128]{1,0:T(8,128)S(1)} %add.31.sums, f32[1,32]{1,0:T(1,128)S(1)} %bitcast.14, f32[4,32,512]{2,1,0:T(8,128)S(1)} %copy-done.9, f32[4,32,512]{2,1,0:T(8,128)S(1)} %copy-done.2, f32[4,32,512]{2,1,0:T(8,128)S(1)} %copy-done.3, ...), custom_call_target="tpu_custom_call" | custom-call | tf_op jit(solution)/shard_map/finish/pallas_call | solution.py:507
  (27 shorter events, 0.1 us)
Async XLA Ops:
  1.5 8.0 %collective-permute-start = (f32[1,32,512]{2,1,0:T(8,128)S(1)}, f32[1,32,512]{2,1,0:T(8,128)S(1)}, u32[]{:S(2)}, u32[]{:S(2)}) collective-permute-start(f32[1,32,512]{2,1,0:T(8,128)S(1)} %slice.6), channel_id=1, source_target_pairs={{0,1},{1,2},{2,3},{3,4},{4,5},{5,6},{6,7},{7,8},{8,9},{9,10},{10,1... | collective-permute-start | bytes 196616 | tf_op jit(solution)/shard_map/ppermute | solution.py:18
  9.4 0.6 copy-start.6
  11.8 5.5 %collective-permute-start.1 = (f32[24,128]{1,0:T(8,128)}, f32[24,128]{1,0:T(8,128)S(1)}, u32[]{:S(2)}, u32[]{:S(2)}) collective-permute-start(f32[24,128]{1,0:T(8,128)} %cross.1), channel_id=1, source_target_pairs={{0,16},{1,17},{2,18},{3,19},{4,20},{5,21},{6,22},{7,23},{8,24},{9,... | collective-permute-start | bytes 36872 | tf_op jit(solution)/shard_map/ppermute | solution.py:23
  18.0 3.7 %collective-permute-start.2 = (f32[24,128]{1,0:T(8,128)S(1)}, f32[24,128]{1,0:T(8,128)S(1)}, u32[]{:S(2)}, u32[]{:S(2)}) collective-permute-start(f32[24,128]{1,0:T(8,128)S(1)} %add.25), channel_id=1, source_target_pairs={{0,8},{1,9},{2,10},{3,11},{4,12},{5,13},{6,14},{7,15},{8,0},{9,1},... | collective-permute-start | bytes 36872 | tf_op jit(solution)/shard_map/ppermute | solution.py:23
  21.7 4.0 %collective-permute-start.3 = (f32[1,24,128]{2,1,0:T(8,128)S(1)}, f32[1,24,128]{2,1,0:T(8,128)S(1)}, u32[]{:S(2)}, u32[]{:S(2)}) collective-permute-start(f32[1,24,128]{2,1,0:T(8,128)S(1)} %get-tuple-element.31), channel_id=1, source_target_pairs={{0,4},{1,5},{2,6},{3,7},{4,0},{5,1},{6,2},{7,3},{8,12},{9,13},{10,... | collective-permute-start | bytes 36872 | tf_op jit(solution)/shard_map/ppermute | solution.py:23
  24.4 12.5 %collective-permute-start.6 = (f32[1,32,512]{2,1,0:T(8,128)S(1)}, f32[1,32,512]{2,1,0:T(8,128)S(1)}, u32[]{:S(2)}, u32[]{:S(2)}) collective-permute-start(f32[1,32,512]{2,1,0:T(8,128)S(1)} %slice.7), channel_id=1, source_target_pairs={{0,1},{1,2},{2,3},{3,4},{4,5},{5,6},{6,7},{7,8},{8,9},{9,10},{10,1... | collective-permute-start | bytes 196616 | tf_op jit(solution)/shard_map/ppermute | solution.py:18
  25.7 4.1 %collective-permute-start.4 = (f32[2,24,128]{2,1,0:T(8,128)S(1)}, f32[2,24,128]{2,1,0:T(8,128)S(1)}, u32[]{:S(2)}, u32[]{:S(2)}) collective-permute-start(f32[2,24,128]{2,1,0:T(8,128)S(1)} %maximum_select_fusion.2), channel_id=1, source_target_pairs={{0,2},{1,3},{2,0},{3,1},{4,6},{5,7},{6,4},{7,5},{8,10},{9,11},{10,... | collective-permute-start | bytes 73736 | tf_op jit(solution)/shard_map/ppermute | solution.py:23
  29.8 19.6 %collective-permute-start.5 = (f32[4,24,128]{2,1,0:T(8,128)S(1)}, f32[4,24,128]{2,1,0:T(8,128)S(1)}, u32[]{:S(2)}, u32[]{:S(2)}) collective-permute-start(f32[4,24,128]{2,1,0:T(8,128)S(1)} %bitcast.15), channel_id=1, source_target_pairs={{0,1},{1,0},{2,3},{3,2},{4,5},{5,4},{6,7},{7,6},{8,9},{9,8},{10,11... | collective-permute-start | bytes 147464 | tf_op jit(solution)/shard_map/ppermute | solution.py:23
  30.7 3.2 %collective-permute-start.7 = (f32[8,1280]{1,0:T(8,128)}, f32[8,1280]{1,0:T(8,128)S(1)}, u32[]{:S(2)}, u32[]{:S(2)}) collective-permute-start(f32[8,1280]{1,0:T(8,128)} %get-tuple-element.19), channel_id=1, source_target_pairs={{0,1},{1,2},{2,3},{3,4},{4,5},{5,6},{6,7},{7,8},{8,9},{9,10},{10,1... | collective-permute-start | bytes 122888 | tf_op jit(solution)/shard_map/ppermute | solution.py:18
  32.6 4.3 %collective-permute-start.8 = (f32[8,1280]{1,0:T(8,128)}, f32[8,1280]{1,0:T(8,128)S(1)}, u32[]{:S(2)}, u32[]{:S(2)}) collective-permute-start(f32[8,1280]{1,0:T(8,128)} %get-tuple-element.20), channel_id=1, source_target_pairs={{1,0},{2,1},{3,2},{4,3},{5,4},{6,5},{7,6},{8,7},{9,8},{10,9},{11,1... | collective-permute-start | bytes 122888 | tf_op jit(solution)/shard_map/ppermute | solution.py:18
  33.9 45.2 %copy-start.11 = (f32[32]{0:T(128)S(1)}, f32[32]{0:T(128)}, u32[]{:S(2)}) copy-start(f32[32]{0:T(128)} %param.11) | copy-start | bytes 388
  36.9 3.4 %copy-start = (bf16[4,1024,1024]{2,1,0:T(8,128)(2,1)S(1)}, bf16[4,1024,1024]{2,1,0:T(8,128)(2,1)}, u32[]{:S(2)}) copy-start(bf16[4,1024,1024]{2,1,0:T(8,128)(2,1)} %factor.3) | copy-start | bytes 25165828
  40.3 0.9 %copy-start.2 = (f32[4,32,512]{2,1,0:T(8,128)S(1)}, f32[4,32,512]{2,1,0:T(8,128)}, u32[]{:S(2)}) copy-start(f32[4,32,512]{2,1,0:T(8,128)} %residual.7) | copy-start | bytes 786436
  41.2 0.9 %copy-start.3 = (f32[4,32,512]{2,1,0:T(8,128)S(1)}, f32[4,32,512]{2,1,0:T(8,128)}, u32[]{:S(2)}) copy-start(f32[4,32,512]{2,1,0:T(8,128)} %old_direction.3) | copy-start | bytes 786436
  42.2 0.9 %copy-start.4 = (f32[4,6,1024]{2,1,0:T(8,128)S(1)}, f32[4,6,1024]{2,1,0:T(8,128)}, u32[]{:S(2)}) copy-start(f32[4,6,1024]{2,1,0:T(8,128)} %copy.11.modes_ref) | copy-start | bytes 294916
  43.1 0.9 %copy-start.5 = (f32[24,768]{1,0:T(8,128)S(1)}, f32[24,768]{1,0:T(8,128)}, u32[]{:S(2)}) copy-start(f32[24,768]{1,0:T(8,128)} %coarse.3) | copy-start | bytes 221188
  44.0 0.8 %copy-start.7 = (f32[1,32,512]{2,1,0:T(8,128)S(1)}, f32[1,32,512]{2,1,0:T(8,128)}, u32[]{:S(2)}) copy-start(f32[1,32,512]{2,1,0:T(8,128)} %copy-done.6) | copy-start | bytes 196612
  44.8 0.8 %copy-start.8 = (f32[4,8,512]{2,1,0:T(8,128)S(1)}, f32[4,8,512]{2,1,0:T(8,128)}, u32[]{:S(2)}) copy-start(f32[4,8,512]{2,1,0:T(8,128)} %get-tuple-element.18.face_modes) | copy-start | bytes 196612
  45.7 0.7 copy-start.10
  46.4 4.5 %copy-start.1 = (bf16[4,1024,1024]{2,1,0:T(8,128)(2,1)S(1)}, bf16[4,1024,1024]{2,1,0:T(8,128)(2,1)}, u32[]{:S(2)}) copy-start(bf16[4,1024,1024]{2,1,0:T(8,128)(2,1)} %factor.3) | copy-start | bytes 25165828
  46.4 32.8 %copy-start.9 = (f32[4,32,512]{2,1,0:T(8,128)S(1)}, f32[4,32,512]{2,1,0:T(8,128)}, u32[]{:S(2)}) copy-start(f32[4,32,512]{2,1,0:T(8,128)} %multipliers.1) | copy-start | bytes 786436
  53.1 26.0 %collective-permute-start.14 = (f32[64,512]{1,0:T(8,128)S(1)}, f32[64,512]{1,0:T(8,128)S(1)}, u32[]{:S(2)}, u32[]{:S(2)}) collective-permute-start(f32[64,512]{1,0:T(8,128)S(1)} %get-tuple-element.30), channel_id=1, source_target_pairs={{1,0},{2,1},{3,2},{4,3},{5,4},{6,5},{7,6},{8,7},{9,8},{10,9},{11,1... | collective-permute-start | bytes 393224 | tf_op jit(solution)/shard_map/ppermute | solution.py:18
  54.4 12.7 %collective-permute-start.9 = (f32[8,128]{1,0:T(8,128)S(1)}, f32[8,128]{1,0:T(8,128)S(1)}, u32[]{:S(2)}, u32[]{:S(2)}) collective-permute-start(f32[8,128]{1,0:T(8,128)S(1)} %get-tuple-element.25), channel_id=1, source_target_pairs={{0,16},{1,17},{2,18},{3,19},{4,20},{5,21},{6,22},{7,23},{8,24},{9,... | collective-permute-start | bytes 12296 | tf_op jit(solution)/shard_map/ppermute | solution.py:23
  67.1 3.6 %collective-permute-start.10 = (f32[8,128]{1,0:T(8,128)S(1)}, f32[8,128]{1,0:T(8,128)S(1)}, u32[]{:S(2)}, u32[]{:S(2)}) collective-permute-start(f32[8,128]{1,0:T(8,128)S(1)} %add.27), channel_id=1, source_target_pairs={{0,8},{1,9},{2,10},{3,11},{4,12},{5,13},{6,14},{7,15},{8,0},{9,1},... | collective-permute-start | bytes 12296 | tf_op jit(solution)/shard_map/ppermute | solution.py:23
  70.7 3.6 %collective-permute-start.11 = (f32[8,128]{1,0:T(8,128)S(1)}, f32[8,128]{1,0:T(8,128)S(1)}, u32[]{:S(2)}, u32[]{:S(2)}) collective-permute-start(f32[8,128]{1,0:T(8,128)S(1)} %add.28), channel_id=1, source_target_pairs={{0,4},{1,5},{2,6},{3,7},{4,0},{5,1},{6,2},{7,3},{8,12},{9,13},{10,... | collective-permute-start | bytes 12296 | tf_op jit(solution)/shard_map/ppermute | solution.py:23
  74.4 3.6 %collective-permute-start.12 = (f32[8,128]{1,0:T(8,128)S(1)}, f32[8,128]{1,0:T(8,128)S(1)}, u32[]{:S(2)}, u32[]{:S(2)}) collective-permute-start(f32[8,128]{1,0:T(8,128)S(1)} %add.29), channel_id=1, source_target_pairs={{0,2},{1,3},{2,0},{3,1},{4,6},{5,7},{6,4},{7,5},{8,10},{9,11},{10,... | collective-permute-start | bytes 12296 | tf_op jit(solution)/shard_map/ppermute | solution.py:23
  78.0 1.2 %collective-permute-start.13 = (f32[8,128]{1,0:T(8,128)S(1)}, f32[8,128]{1,0:T(8,128)S(1)}, u32[]{:S(2)}, u32[]{:S(2)}) collective-permute-start(f32[8,128]{1,0:T(8,128)S(1)} %add.30), channel_id=1, source_target_pairs={{0,1},{1,0},{2,3},{3,2},{4,5},{5,4},{6,7},{7,6},{8,9},{9,8},{10,11... | collective-permute-start | bytes 12296 | tf_op jit(solution)/shard_map/ppermute | solution.py:23

commit v2 on v1

v2 whole, which is shorter than its diff:
```python
import functools

import jax
import jax.numpy as jnp
from jax import lax
from jax.experimental import pallas as pl
from jax.experimental.pallas import tpu as pltpu
from jax.sharding import PartitionSpec as P

AXES = ("sub", "grp")
HIGHEST = lax.Precision.HIGHEST
VMEM = pl.BlockSpec(memory_space=pltpu.VMEM)
HBM = pl.BlockSpec(memory_space=pltpu.HBM)
BLOCK = 256
ANY = pl.BlockSpec(memory_space=pl.ANY)
PARAMS = pltpu.CompilerParams(vmem_limit_bytes=12 << 20)


def shifted(block, distance):
    devices = range(lax.axis_size(AXES))
    route = [(i - distance, i) for i in devices if i - distance in devices]
    return lax.ppermute(block, AXES, route)


def swapped(block, distance):
    route = [(i, i ^ distance) for i in range(lax.axis_size(AXES))]
    return lax.ppermute(block, AXES, route)


def rows_dot(first, second, precision=None):
    return lax.dot_general(
        first,
        second,
        (((1,), (1,)), ((), ())),
        precision=precision,
        preferred_element_type=jnp.float32,
    )


def plain_dot(first, second, precision=None):
    return lax.dot_general(
        first,
        second,
        (((1,), (0,)), ((), ())),
        precision=precision,
        preferred_element_type=jnp.float32,
    )


def halves(values):
    high = values.astype(jnp.bfloat16)
    low = (values - high.astype(jnp.float32)).astype(jnp.bfloat16)
    return high, low


def thirds(values):
    high = values.astype(jnp.bfloat16)
    rest = values - high.astype(jnp.float32)
    middle = rest.astype(jnp.bfloat16)
    low = (rest - middle.astype(jnp.float32)).astype(jnp.bfloat16)
    return high, middle, low


def match_table(row):
    width = row.shape[1]
    positions = lax.broadcasted_iota(jnp.int32, (width, width), 0)
    return (positions == row).astype(jnp.float32).astype(jnp.bfloat16)


def in_lane_block(values, lane_block, copies):
    cases = values.shape[1]
    wide = jnp.concatenate([values] * copies, axis=1)
    lanes = lax.broadcasted_iota(jnp.int32, wide.shape, 1)
    first = lane_block * cases
    inside = (lanes >= first) & (lanes < first + cases)
    return jnp.where(inside, wide, 0.0)


def prepare_kernel(
    copies,
    share,
    matching_in,
    modes_in,
    residual_in,
    old_in,
    coarse_in,
    factor_in,
    face_modes,
    own_sums,
    pack_next,
    pack_before,
    masked,
    old_masked,
    padded,
    matching,
    coarse_rows,
    *others,
):
    held, (modes, coarse, arrived, factor_arrived) = others[:-4], others[-4:]
    ranks, count, _ = modes_in.shape
    half = matching_in.shape[1]
    pairs = [
        (matching_in, matching),
        (modes_in, modes),
        (residual_in, masked),
        (coarse_in, coarse),
        (old_in, old_masked),
    ]
    fetches = [pltpu.make_async_copy(a, b, arrived.at[i]) for i, (a, b) in enumerate(pairs)]
    for fetch in fetches:
        fetch.start()
    for a, rows in enumerate(held):
        _, depth, width = rows.shape
        fetch = pltpu.make_async_copy(
            factor_in.at[:, pl.ds(a * depth, depth), pl.ds(0, width)], rows, factor_arrived.at[a]
        )
        fetch.start()
        fetches.append(fetch)
    me = lax.axis_index(AXES)
    keep = jnp.where(me == lax.axis_size(AXES) - 1, 0.0, 1.0)
    lane_block = me // share
    padded[...] = jnp.zeros_like(padded)
    pack_next[...] = jnp.zeros_like(pack_next)
    pack_before[...] = jnp.zeros_like(pack_before)
    coarse_rows[...] = jnp.zeros_like(coarse_rows)
    fetches[0].wait()
    fetches[1].wait()
    for g in range(count):
        padded[g, 0:ranks, :] = modes[:, g, :]
    for g in range(count):
        table = match_table(matching[g : g + 1, :])
        left = padded[g, :, :half]
        high, middle, low = thirds(left)
        stacked = jnp.concatenate(
            [high.astype(jnp.float32), middle.astype(jnp.float32), low.astype(jnp.float32), left * 0.0],
            axis=0,
        ).astype(jnp.bfloat16)
        moved = rows_dot(stacked, table)
        face_modes[g] = moved[0:8] + moved[8:16] + moved[16:24]
    fetches[2].wait()
    masked[count - 1] = masked[count - 1] * keep
    sums = [None] * count
    for g in range(count):
        if g == count - 1:
            sums[g] = (sums[g] if g else 0.0) + rows_dot(padded[g, :, half:], masked[g], HIGHEST)
        else:
            both = jnp.concatenate([padded[g, :, half:], face_modes[g + 1]], axis=0)
            found = rows_dot(both, masked[g], HIGHEST)
            sums[g] = found[0:8] + (sums[g] if g else 0.0)
            sums[g + 1] = -found[8:16]
    for g in range(count):
        own_sums[g * ranks : (g + 1) * ranks, :] = in_lane_block(sums[g], lane_block, copies)[0:ranks]
    pack_next[:, :half] = padded[count - 1, :, half:]
    pack_before[:, :half] = face_modes[0]
    width = half + coarse_in.shape[1]
    fetches[3].wait()
    for g in range(count):
        coarse_rows[8 * g : 8 * g + ranks, :] = coarse[g * ranks : (g + 1) * ranks, :]
    pack_next[0:ranks, half:width] = coarse[(count - 1) * ranks : count * ranks, :]
    pack_before[0:ranks, half:] = coarse[0:ranks, :]
    fetches[4].wait()
    for k in range(old_masked.shape[1] // 8):
        lanes = slice(width + k * half, width + (k + 1) * half)
        pack_next[:, lanes] = old_masked[count - 1, 8 * k : 8 * k + 8, :]
    old_masked[count - 1] = old_masked[count - 1] * keep
    for fetch in fetches[5:]:
        fetch.wait()


def cross_kernel(copies, share, ranks, own_sums, face_modes, before_face, out):
    lane_block = lax.axis_index(AXES) // share
    cross = rows_dot(face_modes[0], before_face[0], HIGHEST)
    out[...] = own_sums[...]
    out[0:ranks, :] = own_sums[0:ranks, :] - in_lane_block(cross, lane_block, copies)[0:ranks]


def inner_kernel(
    subs,
    order,
    matching,
    padded,
    masked,
    old_masked,
    face_modes,
    *others,
):
    count, cases, half = masked.shape
    full = 2 * half
    block = min(BLOCK, full)
    held, halos = others[: full // block], others[full // block : -4]
    inner_res, inner_old, basis, operand = others[-4:]
    rows = operand.shape[0] // 2
    me = lax.axis_index(AXES)
    q = 2 * cases
    zeros8 = jnp.zeros((8, half), jnp.float32)

    for slot, g in enumerate(subs):
        left_modes = padded[g, :, :half]
        right_modes = padded[g, :, half:]
        if g == 0:
            before_residual, from_before, _ = halos
            width = from_before.shape[1] - half * (cases // 8)
            prior_modes = from_before[:, :half]
            prior_res = before_residual[0]
            prior_old = jnp.concatenate(
                [
                    from_before[:, width + k * half : width + (k + 1) * half]
                    for k in range(cases // 8)
                ],
                axis=0,
            )
            left_modes = left_modes * jnp.where(me == 0, 0.0, 1.0)
        else:
            prior_modes = padded[g - 1, :, half:]
            prior_res, prior_old = masked[g - 1], old_masked[g - 1]
        if g == count - 1:
            keep = jnp.where(me == lax.axis_size(AXES) - 1, 0.0, 1.0)
            next_faces = halos[2][:, :half] * keep
            right_modes = right_modes * keep
        else:
            next_faces = face_modes[g + 1]

        right = jnp.concatenate(
            [masked[g], old_masked[g], zeros8, right_modes, -next_faces, zeros8], axis=0
        )
        right_high, right_low = halves(right)
        operand[0:rows, half:] = right_high
        operand[rows:, half:] = right_low

        moving = jnp.concatenate([prior_res, prior_old, prior_modes, zeros8], axis=0)
        high, low = halves(-moving)
        table = match_table(matching[g : g + 1, :])
        moved = plain_dot(jnp.concatenate([high, low], axis=0), table)
        part = moving.shape[0]
        own_high, own_low = halves(left_modes)
        own_high = own_high.astype(jnp.float32)
        own_low = own_low.astype(jnp.float32)
        operand[0:rows, :half] = jnp.concatenate(
            [moved[0 : q + 8], own_high, zeros8, zeros8], axis=0
        ).astype(jnp.bfloat16)
        operand[rows:, :half] = jnp.concatenate(
            [moved[part : part + q + 8], own_low, zeros8, zeros8], axis=0
        ).astype(jnp.bfloat16)

        for a in range(full // block):
            lanes = slice(a * block, (a + 1) * block)
            found = rows_dot(operand[:, : (a + 1) * block], held[a][g])
            found = found[0:rows] + found[rows:]
            inner_res[slot, :, lanes] = found[0:cases]
            inner_old[slot, :, lanes] = found[cases:q]
            basis[slot, :, half + a * block : half + (a + 1) * block] = found[q : q + 24]
        basis[slot, :, :half] = right[q : q + 24]


def add_kernel(first, second, *others):
    others[-1][...] = first[...] + second[...]


def pair_kernel(distance, first, second, *others):
    out = others[-1]
    upper = (lax.axis_index(AXES) // distance) % 2
    out[:, pl.ds(upper, 1)] = first[...][:, None]
    out[:, pl.ds(1 - upper, 1)] = second[...][:, None]


def located(parts, g, count):
    if g == 0 or g == count - 1:
        return parts[3], parts[4], parts[5], min(g, 1)
    return parts[0], parts[1], parts[2], g - 1


def combine_kernel(
    copies,
    gathered,
    from_before,
    coarse_rows,
    from_next,
    masked,
    *others,
):
    parts, (projected, inner_proj, sums) = others[:-3], others[-3:]
    count, cases, half = masked.shape
    coarse_width = coarse_rows.shape[1]
    found = gathered[...]
    stacked = jnp.concatenate([found[:, b * cases : (b + 1) * cases] for b in range(copies)], axis=0)
    rows = jnp.concatenate([from_before[:, half : half + coarse_width], coarse_rows[...], from_next[:, half:]], axis=0)
    coeffs = plain_dot(rows, stacked, HIGHEST)
    width = 128
    totals = [jnp.zeros((cases, width), jnp.float32) for _ in range(4)]

    def folded(values):
        out = values[:, :width]
        for k in range(1, values.shape[1] // width):
            out = out + values[:, k * width : (k + 1) * width]
        return out

    for g in range(count):
        inner_res, inner_old, basis, slot = located(parts, g, count)
        near = coeffs[8 * g : 8 * g + 24]
        spread = lax.dot_general(
            near,
            basis[slot],
            (((0,), (0,)), ((), ())),
            precision=HIGHEST,
            preferred_element_type=jnp.float32,
        )
        proj = masked[g] - spread[:, :half]
        mine = inner_res[slot] - spread[:, half:]
        other = inner_old[slot]
        projected[g] = proj
        inner_proj[g] = mine
        totals[0] += folded(proj * proj)
        totals[1] += folded(mine * mine)
        totals[2] += folded(mine * other)
        totals[3] += folded(other * other)
    sums[...] = rows_dot(jnp.ones((8, width), jnp.float32), jnp.concatenate(totals, axis=0), HIGHEST)


def outer_kernel(matching, inner_proj, mid_old, end_old, *others):
    held, (image_proj, image_old, returned) = others[:-3], others[-3:]
    count, cases, full = inner_proj.shape
    half = full // 2
    rows = 2 * cases
    block = full // len(held)
    following = None
    for g in reversed(range(count)):
        _, other, _, slot = located((None, mid_old, None, None, end_old, None), g, count)
        high, low = halves(jnp.concatenate([inner_proj[g], other[slot]], axis=0))
        operand = jnp.concatenate([high, low], axis=0)
        pieces = [0.0] * len(held)
        for a in range(len(held)):
            found = plain_dot(operand[:, a * block : (a + 1) * block], held[a][g])
            found = found[0:rows] + found[rows:]
            for b in range(a + 1):
                pieces[b] = pieces[b] + found[:, b * block : (b + 1) * block]
        per_half = half // block
        left = jnp.concatenate(pieces[:per_half], axis=1)
        result = jnp.concatenate(pieces[per_half:], axis=1)
        if following is not None:
            result = result - following
        image_proj[g] = result[0:cases]
        image_old[g] = result[cases:]
        high, low = halves(left)
        table = match_table(matching[g : g + 1, :])
        moved = rows_dot(jnp.concatenate([high, low], axis=0), table)
        following = moved[0:rows] + moved[rows:]
    returned[...] = following


def finish_kernel(
    sums,
    old_norms,
    multipliers,
    masked,
    old_masked,
    projected,
    image_proj,
    image_old,
    returned,
    new_multipliers,
    new_residual,
    direction,
):
    count, cases, half = masked.shape
    me = lax.axis_index(AXES)
    is_last = me == lax.axis_size(AXES) - 1
    diagonal = lax.broadcasted_iota(jnp.int32, (cases, cases), 0) == lax.broadcasted_iota(
        jnp.int32, (cases, cases), 1
    )

    def column(row):
        return jnp.sum(jnp.where(diagonal, row, 0.0), axis=1, keepdims=True)

    norms = sums[0:1, 0:cases]
    ratio = norms / old_norms[...]
    curvature = (
        sums[0:1, cases : 2 * cases]
        + 2.0 * ratio * sums[0:1, 2 * cases : 3 * cases]
        + ratio * ratio * sums[0:1, 3 * cases : 4 * cases]
    )
    step_len = column(norms / curvature)
    ratio = column(ratio)
    for g in range(count):
        proj_part, old_part = image_proj[g], image_old[g]
        if g == count - 1:
            keep = jnp.where(is_last, 0.0, 1.0)
            proj_part = (proj_part - returned[0:cases]) * keep
            old_part = (old_part - returned[cases:]) * keep
        towards = projected[g] + ratio * old_masked[g]
        direction[g] = towards
        new_multipliers[g] = multipliers[g] + step_len * towards
        new_residual[g] = masked[g] - step_len * (proj_part + ratio * old_part)


def on_device(
    multipliers,
    residual,
    old_direction,
    old_norms,
    matching,
    factor_inverse,
    rigid_modes,
    coarse_inverse,
):
    count, cases, half = residual.shape
    ranks = rigid_modes.shape[1]
    full = factor_inverse.shape[1]
    own_rows, coarse_width = coarse_inverse.shape
    devices = lax.axis_size(AXES)
    copies = min(128 // cases, devices)
    share = devices // copies
    f32 = jnp.float32
    shape = jax.ShapeDtypeStruct
    modes_by_rank = rigid_modes.transpose(1, 0, 2)

    before_residual = shifted(residual[count - 1 :], 1)

    row_block = min(BLOCK, full)
    row_blocks = full // row_block
    next_width = half + coarse_width + half * (cases // 8)
    (
        face_modes,
        own_sums,
        pack_next,
        pack_before,
        masked,
        old_masked,
        padded,
        match_copy,
        coarse_rows,
        *factor,
    ) = pl.pallas_call(
        functools.partial(prepare_kernel, copies, share),
        out_shape=(
            shape((count, 8, half), f32),
            shape((own_rows, copies * cases), f32),
            shape((8, next_width), f32),
            shape((8, half + coarse_width), f32),
            shape((count, cases, half), f32),
            shape((count, cases, half), f32),
            shape((count, 8, full), f32),
            shape((count, half), jnp.int32),
            shape((8 * count, coarse_width), f32),
        )
        + tuple(
            shape((count, row_block, (a + 1) * row_block), jnp.bfloat16) for a in range(row_blocks)
        ),
        in_specs=[HBM] * 6,
        out_specs=(VMEM,) * (9 + row_blocks),
        scratch_shapes=[
            pltpu.VMEM((ranks, count, full), f32),
            pltpu.VMEM((own_rows, coarse_width), f32),
            pltpu.SemaphoreType.DMA((5,)),
            pltpu.SemaphoreType.DMA((row_blocks,)),
        ],
        compiler_params=pltpu.CompilerParams(vmem_limit_bytes=12 << 20),
        name="prepare",
    )(
        *(
            pltpu.with_memory_space_constraint(x, pltpu.HBM)
            for x in (
                matching,
                modes_by_rank,
                residual,
                old_direction,
                coarse_inverse,
                factor_inverse,
            )
        )
    )

    from_before = shifted(pack_next, 1)
    from_next = shifted(pack_before, -1)

    block = pl.pallas_call(
        functools.partial(cross_kernel, copies, share, ranks),
        out_shape=shape((own_rows, copies * cases), f32),
        in_specs=[VMEM] * 3,
        out_specs=VMEM,
        compiler_params=PARAMS,
        name="cross",
    )(own_sums, face_modes, before_residual)

    def inner(subs, order, *halos):
        return pl.pallas_call(
            functools.partial(inner_kernel, subs),
            out_shape=(
                shape((len(subs), cases, full), f32),
                shape((len(subs), cases, full), f32),
                shape((len(subs), 24, half + full), f32),
            ),
            in_specs=[ANY] + [VMEM] * (5 + row_blocks + len(halos)),
            out_specs=(VMEM,) * 3,
            scratch_shapes=[pltpu.VMEM((2 * (2 * cases + 32), full), jnp.bfloat16)],
            compiler_params=PARAMS,
            name="inner_ends" if halos else "inner_middle",
        )(order, match_copy, padded, masked, old_masked, face_modes, *factor, *halos)

    def merged(kernel, out_shape, first, second, *after):
        return pl.pallas_call(
            kernel,
            out_shape=shape(out_shape, f32),
            in_specs=[VMEM] * 2 + [ANY] * len(after),
            out_specs=VMEM,
            compiler_params=PARAMS,
            name="merge",
        )(first, second, *after)

    turn = 0
    distance = devices // 2
    while distance >= 1:
        after = ()
        turn += 1
        if turn == 1:
            middle = inner(tuple(range(1, count - 1)), block)
            after = (middle[0],)
        elif turn == 4:
            ends = inner((0, count - 1), block, before_residual, from_before, from_next)
            after = (ends[0],)
        partner = swapped(block, distance)
        if distance >= share:
            block = merged(add_kernel, block.shape, block, partner, *after)
        else:
            if block.ndim == 2:
                block, partner = block[None], partner[None]
            pair = functools.partial(pair_kernel, distance)
            size = block.shape[0]
            block = merged(pair, (size, 2) + block.shape[1:], block, partner, *after)
            block = block.reshape((2 * size,) + block.shape[2:])
        distance //= 2
    gathered = block.reshape(share * own_rows, copies * cases)

    projected, inner_proj, sums = pl.pallas_call(
        functools.partial(combine_kernel, copies),
        out_shape=(
            shape((count, cases, half), f32),
            shape((count, cases, full), f32),
            shape((8, 4 * cases), f32),
        ),
        in_specs=[VMEM] * 11,
        out_specs=(VMEM,) * 3,
        compiler_params=PARAMS,
        name="combine",
    )(gathered, from_before, coarse_rows, from_next, masked, *middle, *ends)

    image_proj, image_old, returned = pl.pallas_call(
        outer_kernel,
        out_shape=(
            shape((count, cases, half), f32),
            shape((count, cases, half), f32),
            shape((2 * cases, half), f32),
        ),
        in_specs=[VMEM] * (4 + row_blocks),
        out_specs=(VMEM,) * 3,
        compiler_params=PARAMS,
        name="outer",
    )(match_copy, inner_proj, middle[1], ends[1], *factor)

    distance = devices // 2
    sums = merged(add_kernel, sums.shape, sums, swapped(sums, distance), returned)
    returned, sums = lax.optimization_barrier((returned, sums))
    returned = shifted(returned, -1)
    while distance > 1:
        distance //= 2
        sums = sums + swapped(sums, distance)


    return pl.pallas_call(
        finish_kernel,
        out_shape=(shape((count, cases, half), f32),) * 3,
        in_specs=[VMEM] * 9,
        out_specs=(VMEM,) * 3,
        compiler_params=PARAMS,
        name="finish",
    )(
        sums,
        old_norms.reshape(1, cases),
        multipliers,
        masked,
        old_masked,
        projected,
        image_proj,
        image_old,
        returned,
    )


def solution(mesh):
    placed = (
        P(AXES, None, None),
        P(AXES, None, None),
        P(AXES, None, None),
        P(),
        P(AXES, None),
        P(AXES, None, None),
        P(AXES, None, None),
        P(AXES, None),
    )
    return jax.shard_map(
        on_device,
        mesh=mesh,
        in_specs=placed,
        out_specs=(P(AXES, None, None),) * 3,
        check_vma=False,
    )
```

time: 81.2 us -> 52.6 us (0.65)
  local copies, waits for them, and re-layouts: 14.7 us -> 0.86 us
  starting transfers between devices: 30 us -> 23.1 us
  waiting for transfers between devices: 21.9 us -> 17.7 us
  Pallas kernels: 12.3 us -> 9.91 us
    unnamed x25 -> x4, local copies, waits for them, and re-layouts: 11.7 us -> 0.01 us
    ppermute x10, starting transfers between devices: 21.8 us -> 13.7 us  [swapped(): return lax.ppermute(block, AXES, route)]
    ppermute x5 -> x4, waiting for transfers between devices: 2.99 us -> 0.01 us  [shifted(): return lax.ppermute(block, AXES, route)]
    pallas_call x1, Pallas kernels: 1.72 us -> 0.23 us  [on_device(): pl.pallas_call(functools.partial(cross_kernel, copies, share, ranks), out...]
    ppermute x5 -> x4, starting transfers between devices: 8.13 us -> 9.42 us  [shifted(): return lax.ppermute(block, AXES, route)]
    reshape x1 -> x0, local copies, waits for them, and re-layouts: 1.28 us -> none  [on_device(): matching = matching.reshape(count, 1, half)]
    pallas_call x2 -> x9, Pallas kernels: 5.31 us -> 4.12 us  [the longest x2 2.34 us: inner(): pl.pallas_call(functools.partial(inner_kernel, subs), out_shape=(shape((l...]
    ppermute x10, waiting for transfers between devices: 18.9 us -> 17.7 us  [swapped(): return lax.ppermute(block, AXES, route)]
  transfers between devices with their start and end apart: 15 -> 14, of which waited for: 9 -> 10; matrix products, arithmetic and copies ran while one was open for 5% -> 0% of each run, Pallas kernels for 7% -> 14%
where the time goes in v2:
time: 52.6 us; the launch traced here: 52.3 us
  starting transfers between devices  23.1 us (44%)
  waiting for transfers between devices  17.7 us (34%)
  Pallas kernels  9.91 us (19%)
  local copies, waits for them, and re-layouts  0.86 us (2%)
  between operations  0.74 us (1%)
    ppermute x10, waiting for transfers between devices, swapped(): return lax.ppermute(block, AXES, route)  17.7 us
    ppermute x10, starting transfers between devices, swapped(): return lax.ppermute(block, AXES, route)  13.7 us
    ppermute x4, starting transfers between devices, shifted(): return lax.ppermute(block, AXES, route)  9.42 us
    pallas_call x1, Pallas kernels, on_device(): pl.pallas_call(functools.partial(prepare_kernel, copies, share), out_shap...  2.95 us
    pallas_call x2, Pallas kernels, inner(): pl.pallas_call(functools.partial(inner_kernel, subs), out_shape=(shape((l...  2.34 us
    pallas_call x1, Pallas kernels, on_device(): pl.pallas_call(outer_kernel, out_shape=(shape((count, cases, half), f32),...  1.74 us
    pallas_call x1, Pallas kernels, on_device(): pl.pallas_call(functools.partial(combine_kernel, copies), out_shape=(shap...  1.38 us
    pallas_call x1, Pallas kernels, on_device(): pl.pallas_call(finish_kernel, out_shape=(shape((count, cases, half), f32)...  1.23 us
  transfers between devices with their start and end apart: 14, of which 10 were waited for; matrix products, arithmetic and copies ran while one was open for 0% of the time, Pallas kernels for 14%

profile of v2, /device:TPU:0, one launch (start us, length us, event | category | flops | bytes accessed | tf_op | source)
XLA Modules:
  0.0 52.3 jit_solution(16860010245973239033)
XLA Ops:
  0.6 0.8 %slice.3 = f32[1,32,512]{2,1,0:T(8,128)S(1)} slice(f32[4,32,512]{2,1,0:T(8,128)} %residual_in.1), slice={[3:4], [0:32], [0:512]} | slice | bytes 131072 | tf_op jit(solution)/shard_map/slice | solution.py:416
  1.5 2.3 %collective-permute-start = (f32[1,32,512]{2,1,0:T(8,128)S(1)}, f32[1,32,512]{2,1,0:T(8,128)S(1)}, u32[]{:S(2)}, u32[]{:S(2)}) collective-permute-start(f32[1,32,512]{2,1,0:T(8,128)S(1)} %slice.3), channel_id=1, source_target_pairs={{0,1},{1,2},{2,3},{3,4},{4,5},{5,6},{6,7},{7,8},{8,9},{9,10},{10,1... | collective-permute-start | bytes 196616 | tf_op jit(solution)/shard_map/ppermute | solution.py:22
  3.8 3.0 %prepare.1 = (f32[4,8,512]{2,1,0:T(8,128)S(1)}, f32[24,128]{1,0:T(8,128)S(1)}, f32[8,3328]{1,0:T(8,128)S(1)}, f32[8,1280]{1,0:T(8,128)S(1)}, f32[4,32,512]{2,1,0...) custom-call(s32[4,512]{1,0:T(4,128)} %matching_in.1, ...), custom_call_target="tpu_custom_call" | custom-call | tf_op jit(solution)/shard_map/prepare/pallas_call | solution.py:432
  6.8 4.5 %collective-permute-start.5 = (f32[8,3328]{1,0:T(8,128)S(1)}, f32[8,3328]{1,0:T(8,128)S(1)}, u32[]{:S(2)}, u32[]{:S(2)}) collective-permute-start(f32[8,3328]{1,0:T(8,128)S(1)} %get-tuple-element.41), channel_id=1, source_target_pairs={{0,1},{1,2},{2,3},{3,4},{4,5},{5,6},{6,7},{7,8},{8,9},{9,10},{10,1... | collective-permute-start | bytes 319496 | tf_op jit(solution)/shard_map/ppermute | solution.py:22
  11.3 0.0 collective-permute-done.before_face.others_4_
  11.3 0.2 cross.1.order.first
  11.6 2.6 %collective-permute-start.1 = (f32[24,128]{1,0:T(8,128)S(1)}, f32[24,128]{1,0:T(8,128)S(1)}, u32[]{:S(2)}, u32[]{:S(2)}) collective-permute-start(f32[24,128]{1,0:T(8,128)S(1)} %cross.1.order.first), channel_id=1, source_target_pairs={{0,16},{1,17},{2,18},{3,19},{4,20},{5,21},{6,22},{7,23},{8,24},{9,... | collective-permute-start | bytes 36872 | tf_op jit(solution)/shard_map/ppermute | solution.py:27
  14.2 1.2 %inner_middle.1 = (f32[2,32,1024]{2,1,0:T(8,128)S(1)}, f32[2,32,1024]{2,1,0:T(8,128)S(1)}, f32[2,24,1536]{2,1,0:T(8,128)S(1)}) custom-call(f32[24,128]{1,0:T(8,128)S(1)} %cross.1.order.first, s32[4,512]{1,0:T(4,128)S(1)} %get-tuple-element.30.matching, f32[4,8,1024]{2,1,0:T(8,128)S(1)} %get-tuple-element.33.padded, ...), custom_call_target="tpu_custom_call" | custom-call | tf_op jit(solution)/shard_map/inner_middle/pallas_call | solution.py:485
  15.3 0.8 %collective-permute-done.1.second = f32[24,128]{1,0:T(8,128)S(1)} collective-permute-done((f32[24,128]{1,0:T(8,128)S(1)}, f32[24,128]{1,0:T(8,128)S(1)}, u32[]{:S(2)}, u32[]{:S(2)}) %collective-permute-start.1) | collective-permute-done | bytes 12320 | tf_op jit(solution)/shard_map/ppermute | solution.py:27
  16.2 1.6 %collective-permute-start.2 = (f32[24,128]{1,0:T(8,128)S(1)}, f32[24,128]{1,0:T(8,128)S(1)}, u32[]{:S(2)}, u32[]{:S(2)}) collective-permute-start(f32[24,128]{1,0:T(8,128)S(1)} %merge.6.first), channel_id=1, source_target_pairs={{0,8},{1,9},{2,10},{3,11},{4,12},{5,13},{6,14},{7,15},{8,0},{9,1},... | collective-permute-start | bytes 36872 | tf_op jit(solution)/shard_map/ppermute | solution.py:27
  17.7 1.3 %collective-permute-start.6 = (f32[8,1280]{1,0:T(8,128)S(1)}, f32[8,1280]{1,0:T(8,128)S(1)}, u32[]{:S(2)}, u32[]{:S(2)}) collective-permute-start(f32[8,1280]{1,0:T(8,128)S(1)} %get-tuple-element.42), channel_id=1, source_target_pairs={{1,0},{2,1},{3,2},{4,3},{5,4},{6,5},{7,6},{8,7},{9,8},{10,9},{11,1... | collective-permute-start | bytes 122888 | tf_op jit(solution)/shard_map/ppermute | solution.py:22
  19.0 0.8 %collective-permute-done.2.second = f32[24,128]{1,0:T(8,128)S(1)} collective-permute-done((f32[24,128]{1,0:T(8,128)S(1)}, f32[24,128]{1,0:T(8,128)S(1)}, u32[]{:S(2)}, u32[]{:S(2)}) %collective-permute-start.2) | collective-permute-done | bytes 12320 | tf_op jit(solution)/shard_map/ppermute | solution.py:27
  19.9 1.5 %collective-permute-start.3 = (f32[24,128]{1,0:T(8,128)S(1)}, f32[24,128]{1,0:T(8,128)S(1)}, u32[]{:S(2)}, u32[]{:S(2)}) collective-permute-start(f32[24,128]{1,0:T(8,128)S(1)} %merge.7), channel_id=1, source_target_pairs={{0,4},{1,5},{2,6},{3,7},{4,0},{5,1},{6,2},{7,3},{8,12},{9,13},{10,... | collective-permute-start | bytes 36872 | tf_op jit(solution)/shard_map/ppermute | solution.py:27
  21.4 2.2 %collective-permute-done.3 = f32[24,128]{1,0:T(8,128)S(1)} collective-permute-done((f32[24,128]{1,0:T(8,128)S(1)}, f32[24,128]{1,0:T(8,128)S(1)}, u32[]{:S(2)}, u32[]{:S(2)}) %collective-permute-start.3) | collective-permute-done | bytes 12320 | tf_op jit(solution)/shard_map/ppermute | solution.py:27
  23.6 1.5 %collective-permute-start.4 = (f32[2,24,128]{2,1,0:T(8,128)S(1)}, f32[2,24,128]{2,1,0:T(8,128)S(1)}, u32[]{:S(2)}, u32[]{:S(2)}) collective-permute-start(f32[2,24,128]{2,1,0:T(8,128)S(1)} %bitcast.8), channel_id=1, source_target_pairs={{0,2},{1,3},{2,0},{3,1},{4,6},{5,7},{6,4},{7,5},{8,10},{9,11},{10,... | collective-permute-start | bytes 73736 | tf_op jit(solution)/shard_map/ppermute | solution.py:27
  25.1 0.0 collective-permute-done.6.others_6_.from_next
  25.1 0.0 collective-permute-done.5.others_5_.from_before
  25.1 1.2 %inner_ends.1 = (f32[2,32,1024]{2,1,0:T(8,128)S(1)}, f32[2,32,1024]{2,1,0:T(8,128)S(1)}, f32[2,24,1536]{2,1,0:T(8,128)S(1)}) custom-call(f32[2,24,128]{2,1,0:T(8,128)S(1)} %bitcast.9, s32[4,512]{1,0:T(4,128)S(1)} %get-tuple-element.30.matching, f32[4,8,1024]{2,1,0:T(8,128)S(1)} %get-tuple-element.33.padded, f32[4,32,512]{2,1,0:T(8,128)S(1)} %get-tuple-element.34.masked, ...), custom_call_target="tpu_custom_call" | custom-call | tf_op jit(solution)/shard_map/inner_ends/pallas_call | solution.py:485
  26.3 1.1 %collective-permute-done.4.second = f32[2,24,128]{2,1,0:T(8,128)S(1)} collective-permute-done((f32[2,24,128]{2,1,0:T(8,128)S(1)}, f32[2,24,128]{2,1,0:T(8,128)S(1)}, u32[]{:S(2)}, u32[]{:S(2)}) %collective-permute-start.4) | collective-permute-done | bytes 24608 | tf_op jit(solution)/shard_map/ppermute | solution.py:27
  27.4 0.0 collective-permute-start.7
  27.4 1.2 %collective-permute-done.7.second = f32[4,24,128]{2,1,0:T(8,128)S(1)} collective-permute-done((f32[4,24,128]{2,1,0:T(8,128)S(1)}, f32[4,24,128]{2,1,0:T(8,128)S(1)}, u32[]{:S(2)}, u32[]{:S(2)}) %collective-permute-start.7) | collective-permute-done | bytes 49184 | tf_op jit(solution)/shard_map/ppermute | solution.py:27
  28.7 1.4 %combine.1 = (f32[4,32,512]{2,1,0:T(8,128)S(1)}, f32[4,32,1024]{2,1,0:T(8,128)S(1)}, f32[8,128]{1,0:T(8,128)S(1)}) custom-call(f32[192,128]{1,0:T(8,128)S(1)} %bitcast.7, f32[8,3328]{1,0:T(8,128)S(1)} %collective-permute-done.5.others_5_.from_before, f32[32,768]{1,0:T(8,128)S(1)} %get-tuple-element.44.coarse_rows, ...), custom_call_target="tpu_custom_call" | custom-call | tf_op jit(solution)/shard_map/combine/pallas_call | solution.py:533
  30.1 2.6 %collective-permute-start.8 = (f32[8,128]{1,0:T(8,128)S(1)}, f32[8,128]{1,0:T(8,128)S(1)}, u32[]{:S(2)}, u32[]{:S(2)}) collective-permute-start(f32[8,128]{1,0:T(8,128)S(1)} %get-tuple-element.51.first), channel_id=1, source_target_pairs={{0,16},{1,17},{2,18},{3,19},{4,20},{5,21},{6,22},{7,23},{8,24},{9,... | collective-permute-start | bytes 12296 | tf_op jit(solution)/shard_map/ppermute | solution.py:27
  32.7 0.0 copy-start
  32.7 0.0 copy-start.1
  32.7 1.7 %outer.1 = (f32[4,32,512]{2,1,0:T(8,128)S(1)}, f32[4,32,512]{2,1,0:T(8,128)S(1)}, f32[64,512]{1,0:T(8,128)S(1)}) custom-call(s32[4,512]{1,0:T(4,128)S(1)} %get-tuple-element.30.matching, f32[4,32,1024]{2,1,0:T(8,128)S(1)} %get-tuple-element.49.inner_proj, f32[2,32,1024]{2,1,0:T(8,128)S(1)} %get-tuple-element.45.others_1_.mid_old, ...), custom_call_target="tpu_custom_call" | custom-call | tf_op jit(solution)/shard_map/outer/pallas_call | solution.py:546
  34.4 0.2 collective-permute-done.8.second
  34.6 1.3 %collective-permute-start.13 = (f32[64,512]{1,0:T(8,128)S(1)}, f32[64,512]{1,0:T(8,128)S(1)}, u32[]{:S(2)}, u32[]{:S(2)}) collective-permute-start(f32[64,512]{1,0:T(8,128)S(1)} %get-tuple-element.56.others_0_), channel_id=1, source_target_pairs={{1,0},{2,1},{3,2},{4,3},{5,4},{6,5},{7,6},{8,7},{9,8},{10,9},{11,1... | collective-permute-start | bytes 393224 | tf_op jit(solution)/shard_map/ppermute | solution.py:22
  35.9 3.9 %collective-permute-start.9 = (f32[8,128]{1,0:T(8,128)S(1)}, f32[8,128]{1,0:T(8,128)S(1)}, u32[]{:S(2)}, u32[]{:S(2)}) collective-permute-start(f32[8,128]{1,0:T(8,128)S(1)} %merge.11), channel_id=1, source_target_pairs={{0,8},{1,9},{2,10},{3,11},{4,12},{5,13},{6,14},{7,15},{8,0},{9,1},... | collective-permute-start | bytes 12296 | tf_op jit(solution)/shard_map/ppermute | solution.py:27
  39.8 2.9 %collective-permute-done.9 = f32[8,128]{1,0:T(8,128)S(1)} collective-permute-done((f32[8,128]{1,0:T(8,128)S(1)}, f32[8,128]{1,0:T(8,128)S(1)}, u32[]{:S(2)}, u32[]{:S(2)}) %collective-permute-start.9) | collective-permute-done | bytes 4128 | tf_op jit(solution)/shard_map/ppermute | solution.py:27
  42.7 0.0 collective-permute-start.10
  42.7 3.6 %collective-permute-done.10 = f32[8,128]{1,0:T(8,128)S(1)} collective-permute-done((f32[8,128]{1,0:T(8,128)S(1)}, f32[8,128]{1,0:T(8,128)S(1)}, u32[]{:S(2)}, u32[]{:S(2)}) %collective-permute-start.10) | collective-permute-done | bytes 4128 | tf_op jit(solution)/shard_map/ppermute | solution.py:27
  46.3 0.0 collective-permute-start.11
  46.3 3.6 %collective-permute-done.11 = f32[8,128]{1,0:T(8,128)S(1)} collective-permute-done((f32[8,128]{1,0:T(8,128)S(1)}, f32[8,128]{1,0:T(8,128)S(1)}, u32[]{:S(2)}, u32[]{:S(2)}) %collective-permute-start.11) | collective-permute-done | bytes 4128 | tf_op jit(solution)/shard_map/ppermute | solution.py:27
  49.9 0.0 collective-permute-start.12
  49.9 1.2 %collective-permute-done.12 = f32[8,128]{1,0:T(8,128)S(1)} collective-permute-done((f32[8,128]{1,0:T(8,128)S(1)}, f32[8,128]{1,0:T(8,128)S(1)}, u32[]{:S(2)}, u32[]{:S(2)}) %collective-permute-start.12) | collective-permute-done | bytes 4128 | tf_op jit(solution)/shard_map/ppermute | solution.py:27
  51.1 0.0 collective-permute-done.13.returned
  51.1 0.0 copy-done
  51.1 0.0 copy-done.1
  51.1 1.2 %finish.1 = (f32[4,32,512]{2,1,0:T(8,128)}, f32[4,32,512]{2,1,0:T(8,128)}, f32[4,32,512]{2,1,0:T(8,128)}) custom-call(f32[8,128]{1,0:T(8,128)S(1)} %add.15.sums, f32[1,32]{1,0:T(1,128)S(1)} %bitcast.15, f32[4,32,512]{2,1,0:T(8,128)S(1)} %copy-done, f32[4,32,512]{2,1,0:T(8,128)S(1)} %get-tuple-element.34.masked, ...), custom_call_target="tpu_custom_call" | custom-call | tf_op jit(solution)/shard_map/finish/pallas_call | solution.py:568
  (10 shorter events, 0.0 us)
Async XLA Ops:
  1.5 9.8 %collective-permute-start = (f32[1,32,512]{2,1,0:T(8,128)S(1)}, f32[1,32,512]{2,1,0:T(8,128)S(1)}, u32[]{:S(2)}, u32[]{:S(2)}) collective-permute-start(f32[1,32,512]{2,1,0:T(8,128)S(1)} %slice.3), channel_id=1, source_target_pairs={{0,1},{1,2},{2,3},{3,4},{4,5},{5,6},{6,7},{7,8},{8,9},{9,10},{10,1... | collective-permute-start | bytes 196616 | tf_op jit(solution)/shard_map/ppermute | solution.py:22
  6.8 18.3 %collective-permute-start.5 = (f32[8,3328]{1,0:T(8,128)S(1)}, f32[8,3328]{1,0:T(8,128)S(1)}, u32[]{:S(2)}, u32[]{:S(2)}) collective-permute-start(f32[8,3328]{1,0:T(8,128)S(1)} %get-tuple-element.41), channel_id=1, source_target_pairs={{0,1},{1,2},{2,3},{3,4},{4,5},{5,6},{6,7},{7,8},{8,9},{9,10},{10,1... | collective-permute-start | bytes 319496 | tf_op jit(solution)/shard_map/ppermute | solution.py:22
  11.6 4.6 %collective-permute-start.1 = (f32[24,128]{1,0:T(8,128)S(1)}, f32[24,128]{1,0:T(8,128)S(1)}, u32[]{:S(2)}, u32[]{:S(2)}) collective-permute-start(f32[24,128]{1,0:T(8,128)S(1)} %cross.1.order.first), channel_id=1, source_target_pairs={{0,16},{1,17},{2,18},{3,19},{4,20},{5,21},{6,22},{7,23},{8,24},{9,... | collective-permute-start | bytes 36872 | tf_op jit(solution)/shard_map/ppermute | solution.py:27
  16.2 3.7 %collective-permute-start.2 = (f32[24,128]{1,0:T(8,128)S(1)}, f32[24,128]{1,0:T(8,128)S(1)}, u32[]{:S(2)}, u32[]{:S(2)}) collective-permute-start(f32[24,128]{1,0:T(8,128)S(1)} %merge.6.first), channel_id=1, source_target_pairs={{0,8},{1,9},{2,10},{3,11},{4,12},{5,13},{6,14},{7,15},{8,0},{9,1},... | collective-permute-start | bytes 36872 | tf_op jit(solution)/shard_map/ppermute | solution.py:27
  17.7 7.3 %collective-permute-start.6 = (f32[8,1280]{1,0:T(8,128)S(1)}, f32[8,1280]{1,0:T(8,128)S(1)}, u32[]{:S(2)}, u32[]{:S(2)}) collective-permute-start(f32[8,1280]{1,0:T(8,128)S(1)} %get-tuple-element.42), channel_id=1, source_target_pairs={{1,0},{2,1},{3,2},{4,3},{5,4},{6,5},{7,6},{8,7},{9,8},{10,9},{11,1... | collective-permute-start | bytes 122888 | tf_op jit(solution)/shard_map/ppermute | solution.py:22
  19.9 3.7 %collective-permute-start.3 = (f32[24,128]{1,0:T(8,128)S(1)}, f32[24,128]{1,0:T(8,128)S(1)}, u32[]{:S(2)}, u32[]{:S(2)}) collective-permute-start(f32[24,128]{1,0:T(8,128)S(1)} %merge.7), channel_id=1, source_target_pairs={{0,4},{1,5},{2,6},{3,7},{4,0},{5,1},{6,2},{7,3},{8,12},{9,13},{10,... | collective-permute-start | bytes 36872 | tf_op jit(solution)/shard_map/ppermute | solution.py:27
  23.6 3.8 %collective-permute-start.4 = (f32[2,24,128]{2,1,0:T(8,128)S(1)}, f32[2,24,128]{2,1,0:T(8,128)S(1)}, u32[]{:S(2)}, u32[]{:S(2)}) collective-permute-start(f32[2,24,128]{2,1,0:T(8,128)S(1)} %bitcast.8), channel_id=1, source_target_pairs={{0,2},{1,3},{2,0},{3,1},{4,6},{5,7},{6,4},{7,5},{8,10},{9,11},{10,... | collective-permute-start | bytes 73736 | tf_op jit(solution)/shard_map/ppermute | solution.py:27
  27.4 1.2 %collective-permute-start.7 = (f32[4,24,128]{2,1,0:T(8,128)S(1)}, f32[4,24,128]{2,1,0:T(8,128)S(1)}, u32[]{:S(2)}, u32[]{:S(2)}) collective-permute-start(f32[4,24,128]{2,1,0:T(8,128)S(1)} %bitcast.11), channel_id=1, source_target_pairs={{0,1},{1,0},{2,3},{3,2},{4,5},{5,4},{6,7},{7,6},{8,9},{9,8},{10,11... | collective-permute-start | bytes 147464 | tf_op jit(solution)/shard_map/ppermute | solution.py:27
  30.1 4.5 %collective-permute-start.8 = (f32[8,128]{1,0:T(8,128)S(1)}, f32[8,128]{1,0:T(8,128)S(1)}, u32[]{:S(2)}, u32[]{:S(2)}) collective-permute-start(f32[8,128]{1,0:T(8,128)S(1)} %get-tuple-element.51.first), channel_id=1, source_target_pairs={{0,16},{1,17},{2,18},{3,19},{4,20},{5,21},{6,22},{7,23},{8,24},{9,... | collective-permute-start | bytes 12296 | tf_op jit(solution)/shard_map/ppermute | solution.py:27
  32.7 18.4 %copy-start = (f32[4,32,512]{2,1,0:T(8,128)S(1)}, f32[4,32,512]{2,1,0:T(8,128)}, u32[]{:S(2)}) copy-start(f32[4,32,512]{2,1,0:T(8,128)} %multipliers.1) | copy-start | bytes 786436
  32.7 18.4 %copy-start.1 = (f32[32]{0:T(128)S(1)}, f32[32]{0:T(128)}, u32[]{:S(2)}) copy-start(f32[32]{0:T(128)} %param.11) | copy-start | bytes 388
  34.6 16.5 %collective-permute-start.13 = (f32[64,512]{1,0:T(8,128)S(1)}, f32[64,512]{1,0:T(8,128)S(1)}, u32[]{:S(2)}, u32[]{:S(2)}) collective-permute-start(f32[64,512]{1,0:T(8,128)S(1)} %get-tuple-element.56.others_0_), channel_id=1, source_target_pairs={{1,0},{2,1},{3,2},{4,3},{5,4},{6,5},{7,6},{8,7},{9,8},{10,9},{11,1... | collective-permute-start | bytes 393224 | tf_op jit(solution)/shard_map/ppermute | solution.py:22
  35.9 6.8 %collective-permute-start.9 = (f32[8,128]{1,0:T(8,128)S(1)}, f32[8,128]{1,0:T(8,128)S(1)}, u32[]{:S(2)}, u32[]{:S(2)}) collective-permute-start(f32[8,128]{1,0:T(8,128)S(1)} %merge.11), channel_id=1, source_target_pairs={{0,8},{1,9},{2,10},{3,11},{4,12},{5,13},{6,14},{7,15},{8,0},{9,1},... | collective-permute-start | bytes 12296 | tf_op jit(solution)/shard_map/ppermute | solution.py:27
  42.7 3.6 %collective-permute-start.10 = (f32[8,128]{1,0:T(8,128)S(1)}, f32[8,128]{1,0:T(8,128)S(1)}, u32[]{:S(2)}, u32[]{:S(2)}) collective-permute-start(f32[8,128]{1,0:T(8,128)S(1)} %add.12), channel_id=1, source_target_pairs={{0,4},{1,5},{2,6},{3,7},{4,0},{5,1},{6,2},{7,3},{8,12},{9,13},{10,... | collective-permute-start | bytes 12296 | tf_op jit(solution)/shard_map/ppermute | solution.py:27
  46.3 3.6 %collective-permute-start.11 = (f32[8,128]{1,0:T(8,128)S(1)}, f32[8,128]{1,0:T(8,128)S(1)}, u32[]{:S(2)}, u32[]{:S(2)}) collective-permute-start(f32[8,128]{1,0:T(8,128)S(1)} %add.13), channel_id=1, source_target_pairs={{0,2},{1,3},{2,0},{3,1},{4,6},{5,7},{6,4},{7,5},{8,10},{9,11},{10,... | collective-permute-start | bytes 12296 | tf_op jit(solution)/shard_map/ppermute | solution.py:27
  49.9 1.2 %collective-permute-start.12 = (f32[8,128]{1,0:T(8,128)S(1)}, f32[8,128]{1,0:T(8,128)S(1)}, u32[]{:S(2)}, u32[]{:S(2)}) collective-permute-start(f32[8,128]{1,0:T(8,128)S(1)} %add.14), channel_id=1, source_target_pairs={{0,1},{1,0},{2,3},{3,2},{4,5},{5,4},{6,7},{7,6},{8,9},{9,8},{10,11... | collective-permute-start | bytes 12296 | tf_op jit(solution)/shard_map/ppermute | solution.py:27

commit v3 on v2

v3 whole, which is shorter than its diff:
```python
import functools

import jax
import jax.numpy as jnp
from jax import lax
from jax.experimental import pallas as pl
from jax.experimental.pallas import tpu as pltpu
from jax.sharding import PartitionSpec as P

AXES = ("sub", "grp")
HIGHEST = lax.Precision.HIGHEST
VMEM = pl.BlockSpec(memory_space=pltpu.VMEM)
HBM = pl.BlockSpec(memory_space=pltpu.HBM)
BLOCK = 256
ANY = pl.BlockSpec(memory_space=pl.ANY)
PARAMS = pltpu.CompilerParams(vmem_limit_bytes=8 << 20)


def shifted(block, distance):
    devices = range(lax.axis_size(AXES))
    route = [(i - distance, i) for i in devices if i - distance in devices]
    return lax.ppermute(block, AXES, route)


def swapped(block, distance):
    route = [(i, i ^ distance) for i in range(lax.axis_size(AXES))]
    return lax.ppermute(block, AXES, route)


def rows_dot(first, second, precision=None):
    return lax.dot_general(
        first,
        second,
        (((1,), (1,)), ((), ())),
        precision=precision,
        preferred_element_type=jnp.float32,
    )


def plain_dot(first, second, precision=None):
    return lax.dot_general(
        first,
        second,
        (((1,), (0,)), ((), ())),
        precision=precision,
        preferred_element_type=jnp.float32,
    )


def halves(values):
    high = values.astype(jnp.bfloat16)
    low = (values - high.astype(jnp.float32)).astype(jnp.bfloat16)
    return high, low


def thirds(values):
    high = values.astype(jnp.bfloat16)
    rest = values - high.astype(jnp.float32)
    middle = rest.astype(jnp.bfloat16)
    low = (rest - middle.astype(jnp.float32)).astype(jnp.bfloat16)
    return high, middle, low


def match_table(row):
    width = row.shape[1]
    positions = lax.broadcasted_iota(jnp.int32, (width, width), 0)
    return (positions == row).astype(jnp.float32).astype(jnp.bfloat16)


def in_lane_block(values, lane_block, copies):
    cases = values.shape[1]
    wide = jnp.concatenate([values] * copies, axis=1)
    lanes = lax.broadcasted_iota(jnp.int32, wide.shape, 1)
    first = lane_block * cases
    inside = (lanes >= first) & (lanes < first + cases)
    return jnp.where(inside, wide, 0.0)


def first_kernel(modes_in, coarse_in, residual_in, old_in, pack_next, modes, coarse, arrived):
    ranks, count, full = modes_in.shape
    half = full // 2
    width = coarse_in.shape[1]
    pairs = [(modes_in, modes), (coarse_in, coarse)]
    lane = half + width
    for field in (residual_in, old_in):
        for k in range(field.shape[1] // 8):
            pairs.append(
                (field.at[count - 1, pl.ds(8 * k, 8)], pack_next.at[:, pl.ds(lane, half)])
            )
            lane += half
    fetches = [pltpu.make_async_copy(a, b, arrived.at[i]) for i, (a, b) in enumerate(pairs)]
    for fetch in fetches:
        fetch.start()
    pack_next[:, : half + width] = jnp.zeros((8, half + width), jnp.float32)
    fetches[0].wait()
    pack_next[0:ranks, :half] = modes[:, count - 1, half:]
    fetches[1].wait()
    pack_next[0:ranks, half : half + width] = coarse[(count - 1) * ranks : count * ranks, :]
    for fetch in fetches[2:]:
        fetch.wait()


def at_face_before(left, table):
    high, middle, low = thirds(left)
    stacked = jnp.concatenate(
        [high.astype(jnp.float32), middle.astype(jnp.float32), low.astype(jnp.float32), left * 0.0],
        axis=0,
    ).astype(jnp.bfloat16)
    moved = rows_dot(stacked, table)
    return moved[0:8] + moved[8:16] + moved[16:24]


def prepare_kernel(
    copies,
    share,
    matching_in,
    modes_in,
    coarse_in,
    residual_in,
    old_in,
    factor_in,
    face_modes,
    own_sums,
    pack_before,
    masked,
    old_masked,
    padded,
    matching,
    coarse_rows,
    *others,
):
    held, (modes, coarse, arrived) = others[:-3], others[-3:]
    count, cases, half = residual_in.shape
    ranks = modes_in.shape[0]
    fetches = []

    def fetch(source, target):
        copy = pltpu.make_async_copy(source, target, arrived.at[len(fetches)])
        copy.start()
        fetches.append(copy)

    fetch(matching_in, matching)
    fetch(modes_in, modes)
    fetch(residual_in, masked)
    fetch(old_in, old_masked)
    fetch(coarse_in, coarse)
    for a, rows in enumerate(held):
        _, depth, width = rows.shape
        fetch(factor_in.at[:, pl.ds(a * depth, depth), pl.ds(0, width)], rows)
    me = lax.axis_index(AXES)
    keep = jnp.where(me == lax.axis_size(AXES) - 1, 0.0, 1.0)
    lane_block = me // share
    padded[...] = jnp.zeros_like(padded)
    coarse_rows[...] = jnp.zeros_like(coarse_rows)
    fetches[0].wait()
    fetches[1].wait()
    for g in range(count):
        padded[g, 0:ranks, :] = modes[:, g, :]
    for g in range(count):
        face_modes[g] = at_face_before(padded[g, :, :half], match_table(matching[g : g + 1, :]))
    fetches[2].wait()
    masked[count - 1] = masked[count - 1] * keep
    sums = [0.0] * count
    for g in range(count):
        if g == count - 1:
            sums[g] = sums[g] + rows_dot(padded[g, :, half:], masked[g], HIGHEST)
        else:
            both = jnp.concatenate([padded[g, :, half:], face_modes[g + 1]], axis=0)
            found = rows_dot(both, masked[g], HIGHEST)
            sums[g] = sums[g] + found[0:8]
            sums[g + 1] = -found[8:16]
    own_sums[...] = jnp.zeros_like(own_sums)
    for g in range(count):
        own_sums[g * ranks : (g + 1) * ranks, :] = in_lane_block(sums[g], lane_block, copies)[0:ranks]
    fetches[4].wait()
    for g in range(count):
        coarse_rows[8 * g : 8 * g + ranks, :] = coarse[g * ranks : (g + 1) * ranks, :]
    width = half + coarse_rows.shape[1]
    pack_before[:, :half] = face_modes[0]
    pack_before[:, half:width] = coarse_rows[0:8, :]
    pack_before[:, width:] = coarse_rows[8:16, :]
    fetches[3].wait()
    old_masked[count - 1] = old_masked[count - 1] * keep
    for copy in fetches[5:]:
        copy.wait()


def cross_kernel(copies, share, ranks, own_sums, face_modes, from_before, order, out):
    lane_block = lax.axis_index(AXES) // share
    half = face_modes.shape[2]
    fields = from_before.shape[1] - 2 * half * (out.shape[1] // copies // 8)
    field = unpacked(from_before, fields, out.shape[1] // copies, half)
    cross = rows_dot(face_modes[0], field, HIGHEST)
    out[...] = own_sums[...]
    out[0:ranks, :] = own_sums[0:ranks, :] - in_lane_block(cross, lane_block, copies)[0:ranks]


def unpacked(pack, start, cases, half):
    return jnp.concatenate(
        [pack[:, start + k * half : start + (k + 1) * half] for k in range(cases // 8)], axis=0
    )


def inner_part(g, matching, padded, masked, old_masked, face_modes, held, from_before, from_next, operand):
    count, cases, half = masked.shape
    full = 2 * half
    block = full // len(held)
    rows = operand.shape[0] // 2
    me = lax.axis_index(AXES)
    q = 2 * cases
    zeros8 = jnp.zeros((8, half), jnp.float32)
    left_modes = padded[g, :, :half]
    right_modes = padded[g, :, half:]
    if g == 0:
        fields = from_before.shape[1] - 2 * half * (cases // 8)
        prior_modes = from_before[:, :half]
        prior_res = unpacked(from_before, fields, cases, half)
        prior_old = unpacked(from_before, fields + half * (cases // 8), cases, half)
        left_modes = left_modes * jnp.where(me == 0, 0.0, 1.0)
    else:
        prior_modes = padded[g - 1, :, half:]
        prior_res, prior_old = masked[g - 1], old_masked[g - 1]
    if g == count - 1:
        keep = jnp.where(me == lax.axis_size(AXES) - 1, 0.0, 1.0)
        next_faces = from_next[:, :half] * keep
        right_modes = right_modes * keep
    else:
        next_faces = face_modes[g + 1]

    right = jnp.concatenate(
        [masked[g], old_masked[g], zeros8, right_modes, -next_faces, zeros8], axis=0
    )
    right_high, right_low = halves(right)
    operand[0:rows, half:] = right_high
    operand[rows:, half:] = right_low

    moving = jnp.concatenate([prior_res, prior_old, prior_modes, zeros8], axis=0)
    high, low = halves(-moving)
    moved = plain_dot(jnp.concatenate([high, low], axis=0), match_table(matching[g : g + 1, :]))
    part = moving.shape[0]
    own_high, own_low = halves(left_modes)
    own_high = own_high.astype(jnp.float32)
    own_low = own_low.astype(jnp.float32)
    operand[0:rows, :half] = jnp.concatenate(
        [moved[0 : q + 8], own_high, zeros8, zeros8], axis=0
    ).astype(jnp.bfloat16)
    operand[rows:, :half] = jnp.concatenate(
        [moved[part : part + q + 8], own_low, zeros8, zeros8], axis=0
    ).astype(jnp.bfloat16)

    pieces = []
    for a in range(len(held)):
        found = rows_dot(operand[:, : (a + 1) * block], held[a][g])
        pieces.append(found[0:rows] + found[rows:])
    return right, jnp.concatenate(pieces, axis=1)


def store_inner(slot, right, found, inner, basis):
    cases, half = inner.shape[1] // 2, right.shape[1]
    q = 2 * cases
    inner[slot] = found[0:q]
    wide = jnp.concatenate([right[q : q + 24], found[q : q + 24]], axis=1)
    basis[slot] = three_terms(wide)


def three_terms(wide):
    high, low = halves(wide)
    high = high.astype(jnp.float32)
    return jnp.concatenate(
        [high, low.astype(jnp.float32), high, jnp.zeros_like(wide[0:8])], axis=0
    ).astype(jnp.bfloat16)


def across(coeffs, terms):
    high, low = halves(coeffs)
    high = high.astype(jnp.float32)
    stacked = jnp.concatenate(
        [high, high, low.astype(jnp.float32), jnp.zeros_like(coeffs[0:8])], axis=0
    ).astype(jnp.bfloat16)
    return lax.dot_general(
        stacked, terms, (((0,), (0,)), ((), ())), preferred_element_type=jnp.float32
    )


def outer_part(g, found, matching, held):
    rows, full = found.shape
    half = full // 2
    block = full // len(held)
    high, low = halves(found)
    operand = jnp.concatenate([high, low], axis=0)
    pieces = [0.0] * len(held)
    for a in range(len(held)):
        part = plain_dot(operand[:, a * block : (a + 1) * block], held[a][g])
        part = part[0:rows] + part[rows:]
        for b in range(a + 1):
            pieces[b] = pieces[b] + part[:, b * block : (b + 1) * block]
    per_half = half // block
    left = jnp.concatenate(pieces[:per_half], axis=1)
    right = jnp.concatenate(pieces[per_half:], axis=1)
    high, low = halves(left)
    moved = rows_dot(jnp.concatenate([high, low], axis=0), match_table(matching[g : g + 1, :]))
    return moved[0:rows] + moved[rows:], right


def later_kernel(subs, order, matching, padded, masked, old_masked, face_modes, *others):
    halos = len(subs) == 1
    from_next = others[0] if halos else None
    held, (inner, basis, whole, operand) = others[halos:-4], others[-4:]
    operand[...] = jnp.zeros_like(operand)
    for slot, g in enumerate(subs):
        right, found = inner_part(
            g, matching, padded, masked, old_masked, face_modes, held, None, from_next, operand
        )
        store_inner(slot, right, found, inner, basis)
        whole[slot] = found


def start_kernel(order, matching, padded, masked, old_masked, face_modes, from_before, *others):
    held, (inner, basis, right_first, returned, returned_rest, operand) = others[:-6], others[-6:]
    operand[...] = jnp.zeros_like(operand)
    right, found = inner_part(
        0, matching, padded, masked, old_masked, face_modes, held, from_before, None, operand
    )
    store_inner(0, right, found, inner, basis)
    moved, solved = outer_part(0, found, matching, held)
    right_first[...] = solved
    cut = returned.shape[0]
    returned[...] = moved[0:cut]
    returned_rest[...] = jnp.zeros_like(returned_rest)
    returned_rest[0 : returned_rest.shape[0] - 16] = moved[cut : cut + returned_rest.shape[0] - 16]


def outer_kernel(order, matching, whole_middle, whole_last, right_first, coeffs, *others):
    held, (image_proj, image_old) = others[:-2], others[-2:]
    count, cases, half = image_proj.shape
    q = 2 * cases
    keep = jnp.where(lax.axis_index(AXES) == lax.axis_size(AXES) - 1, 0.0, 1.0)
    following = jnp.zeros((q + 24, half), jnp.float32)
    zeros8 = jnp.zeros((8, half), jnp.float32)
    for g in reversed(range(count)):
        if g:
            found = whole_last[0] if g == count - 1 else whole_middle[g - 1]
            moved, solved = outer_part(g, found, matching, held)
        else:
            solved = right_first[...]
        both = solved[0:q] - following[0:q]
        basis = jnp.concatenate([solved[q : q + 24], zeros8], axis=0) - jnp.concatenate(
            [zeros8, following[q : q + 24]], axis=0
        )
        if g == count - 1:
            both, basis = both * keep, basis * keep
        image_proj[g] = both[0:cases] - across(coeffs[8 * g : 8 * g + 32], three_terms(basis))
        image_old[g] = both[cases:]
        if g:
            following = moved


def add_kernel(first, second, *others):
    others[-1][...] = first[...] + second[...]


def pair_kernel(distance, first, second, *others):
    out = others[-1]
    upper = (lax.axis_index(AXES) // distance) % 2
    out[:, pl.ds(upper, 1)] = first[...][:, None]
    out[:, pl.ds(1 - upper, 1)] = second[...][:, None]


def combine_kernel(
    copies,
    gathered,
    from_before,
    coarse_rows,
    from_next,
    masked,
    *others,
):
    parts, (projected, coeffs, sums) = others[:-3], others[-3:]
    count, cases, half = masked.shape
    width = coarse_rows.shape[1]
    own = gathered[...].reshape(gathered.shape[0] * gathered.shape[1], copies * cases)
    stacked = jnp.concatenate([own[:, b * cases : (b + 1) * cases] for b in range(copies)], axis=0)
    rows = jnp.concatenate(
        [
            from_before[:, half : half + width],
            coarse_rows[...],
            from_next[:, half : half + width],
            from_next[:, half + width :],
        ],
        axis=0,
    )
    near = plain_dot(rows, stacked, HIGHEST)
    coeffs[...] = near
    lanes = 128
    totals = [jnp.zeros((cases, lanes), jnp.float32) for _ in range(4)]

    def folded(values):
        out = values[:, :lanes]
        for k in range(1, values.shape[1] // lanes):
            out = out + values[:, k * lanes : (k + 1) * lanes]
        return out

    for g in range(count):
        place = 0 if g == 0 else 4 if g == count - 1 else 2
        slot = g - 1 if place == 2 else 0
        inner = parts[place][slot]
        spread = across(near[8 * g : 8 * g + 24], parts[place + 1][slot])
        proj = masked[g] - spread[:, :half]
        mine = inner[0:cases] - spread[:, half:]
        other = inner[cases:]
        projected[g] = proj
        totals[0] += folded(proj * proj)
        totals[1] += folded(mine * mine)
        totals[2] += folded(mine * other)
        totals[3] += folded(other * other)
    sums[...] = rows_dot(jnp.ones((8, lanes), jnp.float32), jnp.concatenate(totals, axis=0), HIGHEST)


def finish_kernel(
    sums,
    old_norms,
    multipliers,
    masked,
    old_masked,
    projected,
    image_proj,
    image_old,
    coeffs,
    received_first,
    received_rest,
    new_multipliers,
    new_residual,
    direction,
):
    count, cases, half = masked.shape
    diagonal = lax.broadcasted_iota(jnp.int32, (cases, cases), 0) == lax.broadcasted_iota(
        jnp.int32, (cases, cases), 1
    )

    def column(row):
        return jnp.sum(jnp.where(diagonal, row, 0.0), axis=1, keepdims=True)

    norms = sums[0:1, 0:cases]
    ratio = norms / old_norms[...]
    curvature = (
        sums[0:1, cases : 2 * cases]
        + 2.0 * ratio * sums[0:1, 2 * cases : 3 * cases]
        + ratio * ratio * sums[0:1, 3 * cases : 4 * cases]
    )
    step_len = column(norms / curvature)
    ratio = column(ratio)
    for g in range(count):
        image_p, image_o = image_proj[g], image_old[g]
        if g == count - 1:
            received = jnp.concatenate([received_first[...], received_rest[...]], axis=0)
            basis = three_terms(received[2 * cases : 2 * cases + 24])
            near = coeffs[8 * count : 8 * count + 24]
            image_p = image_p - received[0:cases] + across(near, basis)
            image_o = image_o - received[cases : 2 * cases]
        towards = projected[g] + ratio * old_masked[g]
        direction[g] = towards
        new_multipliers[g] = multipliers[g] + step_len * towards
        new_residual[g] = masked[g] - step_len * (image_p + ratio * image_o)


def on_device(
    multipliers,
    residual,
    old_direction,
    old_norms,
    matching,
    factor_inverse,
    rigid_modes,
    coarse_inverse,
):
    count, cases, half = residual.shape
    ranks = rigid_modes.shape[1]
    full = factor_inverse.shape[1]
    own_rows, coarse_width = coarse_inverse.shape
    devices = lax.axis_size(AXES)
    copies = min(128 // cases, devices)
    share = devices // copies
    f32 = jnp.float32
    shape = jax.ShapeDtypeStruct
    row_block = min(BLOCK, full)
    row_blocks = full // row_block
    q = 2 * cases
    cut = q - 8
    in_hbm = lambda *arrays: (pltpu.with_memory_space_constraint(x, pltpu.HBM) for x in arrays)

    modes_by_rank = rigid_modes.transpose(1, 0, 2)
    next_width = half + coarse_width + 2 * half * (cases // 8)
    pack_next = pl.pallas_call(
        first_kernel,
        out_shape=shape((8, next_width), f32),
        in_specs=[HBM] * 4,
        out_specs=VMEM,
        scratch_shapes=[
            pltpu.VMEM((ranks, count, full), f32),
            pltpu.VMEM((own_rows, coarse_width), f32),
            pltpu.SemaphoreType.DMA((2 + 2 * (cases // 8),)),
        ],
        compiler_params=PARAMS,
        name="first",
    )(*in_hbm(modes_by_rank, coarse_inverse, residual, old_direction))

    from_before = shifted(pack_next, 1)

    (
        face_modes,
        own_sums,
        pack_before,
        masked,
        old_masked,
        padded,
        match_copy,
        coarse_rows,
        *factor,
    ) = pl.pallas_call(
        functools.partial(prepare_kernel, copies, share),
        out_shape=(
            shape((count, 8, half), f32),
            shape((own_rows, copies * cases), f32),
            shape((8, half + 2 * coarse_width), f32),
            shape((count, cases, half), f32),
            shape((count, cases, half), f32),
            shape((count, 8, full), f32),
            shape((count, half), jnp.int32),
            shape((8 * count, coarse_width), f32),
        )
        + tuple(
            shape((count, row_block, (a + 1) * row_block), jnp.bfloat16) for a in range(row_blocks)
        ),
        in_specs=[HBM] * 6,
        out_specs=(VMEM,) * (8 + row_blocks),
        scratch_shapes=[
            pltpu.VMEM((ranks, count, full), f32),
            pltpu.VMEM((own_rows, coarse_width), f32),
            pltpu.SemaphoreType.DMA((5 + row_blocks,)),
        ],
        compiler_params=PARAMS,
        name="prepare",
    )(
        *in_hbm(
            matching, modes_by_rank, coarse_inverse, residual, old_direction, factor_inverse
        )
    )

    from_next = shifted(pack_before, -1)

    operand = pltpu.VMEM((2 * (q + 32), full), jnp.bfloat16)
    fields = (match_copy, padded, masked, old_masked, face_modes)

    def merged(kernel, out_shape, first, second, *after):
        return pl.pallas_call(
            kernel,
            out_shape=shape(out_shape, f32),
            in_specs=[VMEM] * 2 + [ANY] * len(after),
            out_specs=VMEM,
            compiler_params=PARAMS,
            name="merge",
        )(first, second, *after)

    def inner(subs, order, *halos):
        return pl.pallas_call(
            functools.partial(later_kernel, subs),
            out_shape=(
                shape((len(subs), q, full), f32),
                shape((len(subs), 80, half + full), jnp.bfloat16),
                shape((len(subs), q + 32, full), f32),
            ),
            in_specs=[ANY] + [VMEM] * (5 + len(halos) + row_blocks),
            out_specs=(VMEM,) * 3,
            scratch_shapes=[operand],
            compiler_params=PARAMS,
            name="inner_last" if halos else "inner_middle",
        )(order, *fields, *halos, *factor)

    inner_middle, basis_middle, whole_middle = inner(tuple(range(1, count - 1)), own_sums)
    block = pl.pallas_call(
        functools.partial(cross_kernel, copies, share, ranks),
        out_shape=shape((own_rows, copies * cases), f32),
        in_specs=[VMEM] * 3 + [ANY],
        out_specs=VMEM,
        compiler_params=PARAMS,
        name="cross",
    )(own_sums, face_modes, from_before, whole_middle)

    turn = 0
    distance = devices // 2
    while distance >= 1:
        turn += 1
        after = ()
        if turn == 1:
            inner_first, basis_first, right_first, *returned = pl.pallas_call(
                start_kernel,
                out_shape=(
                    shape((1, q, full), f32),
                    shape((1, 80, half + full), jnp.bfloat16),
                    shape((q + 32, half), f32),
                    shape((cut, half), f32),
                    shape((q + 40 - cut, half), f32),
                ),
                in_specs=[ANY] + [VMEM] * (6 + row_blocks),
                out_specs=(VMEM,) * 5,
                scratch_shapes=[operand],
                compiler_params=PARAMS,
                name="inner_first",
            )(block, *fields, from_before, *factor)
            after = (returned[0],)
            received = [shifted(part, -1) for part in returned]
        elif turn == 5:
            inner_last, basis_last, whole_last = inner((count - 1,), block, from_next)
            after = (whole_last,)
        partner = swapped(block, distance)
        if distance >= share:
            block = merged(add_kernel, block.shape, block, partner, *after)
        else:
            if block.ndim == 2:
                block, partner = block[None], partner[None]
            pair = functools.partial(pair_kernel, distance)
            size = block.shape[0]
            block = merged(pair, (size, 2) + block.shape[1:], block, partner, *after)
            block = block.reshape((2 * size,) + block.shape[2:])
        distance //= 2

    projected, coeffs, sums = pl.pallas_call(
        functools.partial(combine_kernel, copies),
        out_shape=(
            shape((count, cases, half), f32),
            shape((8 * (count + 3), cases), f32),
            shape((8, 4 * cases), f32),
        ),
        in_specs=[VMEM] * 11,
        out_specs=(VMEM,) * 3,
        compiler_params=PARAMS,
        name="combine",
    )(
        block,
        from_before,
        coarse_rows,
        from_next,
        masked,
        inner_first,
        basis_first,
        inner_middle,
        basis_middle,
        inner_last,
        basis_last,
    )

    image_proj, image_old = pl.pallas_call(
        outer_kernel,
        out_shape=(shape((count, cases, half), f32),) * 2,
        in_specs=[ANY] + [VMEM] * (5 + row_blocks),
        out_specs=(VMEM,) * 2,
        compiler_params=PARAMS,
        name="outer",
    )(sums, match_copy, whole_middle, whole_last, right_first, coeffs, *factor)
    after = (image_proj,)
    distance = devices // 2
    while distance >= 1:
        sums = merged(add_kernel, sums.shape, sums, swapped(sums, distance), *after)
        after = ()
        distance //= 2

    return pl.pallas_call(
        finish_kernel,
        out_shape=(shape((count, cases, half), f32),) * 3,
        in_specs=[VMEM] * 11,
        out_specs=(VMEM,) * 3,
        compiler_params=PARAMS,
        name="finish",
    )(
        sums,
        old_norms.reshape(1, cases),
        multipliers,
        masked,
        old_masked,
        projected,
        image_proj,
        image_old,
        coeffs,
        *received,
    )


def solution(mesh):
    placed = (
        P(AXES, None, None),
        P(AXES, None, None),
        P(AXES, None, None),
        P(),
        P(AXES, None),
        P(AXES, None, None),
        P(AXES, None, None),
        P(AXES, None),
    )
    return jax.shard_map(
        on_device,
        mesh=mesh,
        in_specs=placed,
        out_specs=(P(AXES, None, None),) * 3,
        check_vma=False,
    )
```

time: 52.6 us -> 49 us (0.932)
  waiting for transfers between devices: 17.7 us -> 13.6 us
  Pallas kernels: 9.91 us -> 11.2 us
  local copies, waits for them, and re-layouts: 0.86 us -> 0.01 us
    ppermute x10, waiting for transfers between devices: 17.7 us -> 13.4 us  [swapped(): return lax.ppermute(block, AXES, route)]
    ppermute x4, starting transfers between devices: 9.42 us -> 6.21 us  [shifted(): return lax.ppermute(block, AXES, route)]
    ppermute x10, starting transfers between devices: 13.7 us -> 16.9 us  [swapped(): return lax.ppermute(block, AXES, route)]
    pallas_call x2 -> x4, Pallas kernels: 2.34 us -> 4.11 us  [the longest x2 1.93 us: inner(): pl.pallas_call(functools.partial(later_kernel, subs), out_shape=(shape((l...]
    slice x1 -> x0, local copies, waits for them, and re-layouts: 0.85 us -> none  [on_device(): before_residual = shifted(residual[count - 1:], 1)]
  transfers between devices with their start and end apart: 14 -> 14, of which waited for: 10 -> 10; matrix products, arithmetic and copies ran while one was open for 0% -> 0% of each run, Pallas kernels for 14% -> 18%
where the time goes in v3:
time: 49 us; the launch traced here: 48.7 us
  starting transfers between devices  23.1 us (47%)
  waiting for transfers between devices  13.6 us (28%)
  Pallas kernels  11.2 us (23%)
  between operations  0.77 us (2%)
    ppermute x10, starting transfers between devices, swapped(): return lax.ppermute(block, AXES, route)  16.9 us
    ppermute x10, waiting for transfers between devices, swapped(): return lax.ppermute(block, AXES, route)  13.4 us
    ppermute x4, starting transfers between devices, shifted(): return lax.ppermute(block, AXES, route)  6.21 us
    pallas_call x1, Pallas kernels, on_device(): pl.pallas_call(functools.partial(prepare_kernel, copies, share), out_shap...  2.93 us
    pallas_call x2, Pallas kernels, inner(): pl.pallas_call(functools.partial(later_kernel, subs), out_shape=(shape((l...  1.93 us
    pallas_call x1, Pallas kernels, on_device(): pl.pallas_call(outer_kernel, out_shape=(shape((count, cases, half), f32),...  1.82 us
    pallas_call x1, Pallas kernels, on_device(): pl.pallas_call(finish_kernel, out_shape=(shape((count, cases, half), f32)...  1.23 us
    pallas_call x1, Pallas kernels, on_device(): pl.pallas_call(start_kernel, out_shape=(shape((1, q, full), f32), shape((...  1.14 us
  transfers between devices with their start and end apart: 14, of which 10 were waited for; matrix products, arithmetic and copies ran while one was open for 0% of the time, Pallas kernels for 18%

profile of v3, /device:TPU:0, one launch (start us, length us, event | category | flops | bytes accessed | tf_op | source)
XLA Modules:
  0.0 48.7 jit_solution(13061733703262736764)
XLA Ops:
  0.6 1.0 %first.1 = f32[8,5376]{1,0:T(8,128)S(1)} custom-call(f32[6,4,1024]{2,1,0:T(4,128)} %bitcast.16, f32[24,768]{1,0:T(8,128)} %coarse_in.3, f32[4,32,512]{2,1,0:T(8,128)} %residual_in.3, f32[4,32,512]{2,1,0:T(8,128)} %old_in.3), custom_call_target="tpu_custom_call" | custom-call | tf_op jit(solution)/shard_map/first/pallas_call | solution.py:493
  1.7 2.4 %collective-permute-start = (f32[8,5376]{1,0:T(8,128)S(1)}, f32[8,5376]{1,0:T(8,128)S(1)}, u32[]{:S(2)}, u32[]{:S(2)}) collective-permute-start(f32[8,5376]{1,0:T(8,128)S(1)} %first.1), channel_id=1, source_target_pairs={{0,1},{1,2},{2,3},{3,4},{4,5},{5,6},{6,7},{7,8},{8,9},{9,10},{10,1... | collective-permute-start | bytes 516104 | tf_op jit(solution)/shard_map/ppermute | solution.py:22
  4.1 2.9 %prepare.1 = (f32[4,8,512]{2,1,0:T(8,128)S(1)}, f32[24,128]{1,0:T(8,128)S(1)}, f32[8,2048]{1,0:T(8,128)S(1)}, f32[4,32,512]{2,1,0:T(8,128)S(1)}, f32[4,32,512]{2...) custom-call(s32[4,512]{1,0:T(4,128)} %matching_in.1, ...), custom_call_target="tpu_custom_call" | custom-call | tf_op jit(solution)/shard_map/prepare/pallas_call | solution.py:519
  7.0 1.2 %inner_middle.1 = (f32[2,64,1024]{2,1,0:T(8,128)S(1)}, bf16[2,80,1536]{2,1,0:T(8,128)(2,1)S(1)}, f32[2,96,1024]{2,1,0:T(8,128)S(1)}) custom-call(f32[24,128]{1,0:T(8,128)S(1)} %get-tuple-element.31.order.own_sums, s32[4,512]{1,0:T(4,128)S(1)} %get-tuple-element.33.matching, f32[4,8,1024]{2,1,0:T(8,128)S(1)} %get-tuple-element.34.padded, ...), custom_call_target="tpu_custom_call" | custom-call | tf_op jit(solution)/shard_map/inner_middle/pallas_call | solution.py:565
  8.2 0.0 collective-permute-done.from_before
  8.2 0.2 cross.1.order.first
  8.4 6.1 %collective-permute-start.1 = (f32[24,128]{1,0:T(8,128)S(1)}, f32[24,128]{1,0:T(8,128)S(1)}, u32[]{:S(2)}, u32[]{:S(2)}) collective-permute-start(f32[24,128]{1,0:T(8,128)S(1)} %cross.1.order.first), channel_id=1, source_target_pairs={{0,16},{1,17},{2,18},{3,19},{4,20},{5,21},{6,22},{7,23},{8,24},{9,... | collective-permute-start | bytes 36872 | tf_op jit(solution)/shard_map/ppermute | solution.py:27
  14.5 1.1 %inner_first.1 = (f32[1,64,1024]{2,1,0:T(8,128)S(1)}, bf16[1,80,1536]{2,1,0:T(8,128)(2,1)S(1)}, f32[96,512]{1,0:T(8,128)S(1)}, f32[56,512]{1,0:T(8,128)S(1)}, f32[48,512]{1,0:T(8,128)S(1)}) custom-call(f32[24,128]{1,0:T(8,128)S(1)} %cross.1.order.first, s32[4,512]{1,0:T(4,128)S(1)} %get-tuple-element.33.matching, ...), custom_call_target="tpu_custom_call" | custom-call | tf_op jit(solution)/shard_map/inner_first/pallas_call | solution.py:595
  15.6 0.5 %collective-permute-done.1.second = f32[24,128]{1,0:T(8,128)S(1)} collective-permute-done((f32[24,128]{1,0:T(8,128)S(1)}, f32[24,128]{1,0:T(8,128)S(1)}, u32[]{:S(2)}, u32[]{:S(2)}) %collective-permute-start.1) | collective-permute-done | bytes 12320 | tf_op jit(solution)/shard_map/ppermute | solution.py:27
  16.2 1.9 %collective-permute-start.2 = (f32[24,128]{1,0:T(8,128)S(1)}, f32[24,128]{1,0:T(8,128)S(1)}, u32[]{:S(2)}, u32[]{:S(2)}) collective-permute-start(f32[24,128]{1,0:T(8,128)S(1)} %merge.10.first), channel_id=1, source_target_pairs={{0,8},{1,9},{2,10},{3,11},{4,12},{5,13},{6,14},{7,15},{8,0},{9,1},... | collective-permute-start | bytes 36872 | tf_op jit(solution)/shard_map/ppermute | solution.py:27
  18.1 1.3 %collective-permute-start.12 = (f32[56,512]{1,0:T(8,128)S(1)}, f32[56,512]{1,0:T(8,128)S(1)}, u32[]{:S(2)}, u32[]{:S(2)}) collective-permute-start(f32[56,512]{1,0:T(8,128)S(1)} %get-tuple-element.42.others_0_), channel_id=1, source_target_pairs={{1,0},{2,1},{3,2},{4,3},{5,4},{6,5},{7,6},{8,7},{9,8},{10,9},{11,1... | collective-permute-start | bytes 344072 | tf_op jit(solution)/shard_map/ppermute | solution.py:22
  19.4 0.5 %collective-permute-done.2.second = f32[24,128]{1,0:T(8,128)S(1)} collective-permute-done((f32[24,128]{1,0:T(8,128)S(1)}, f32[24,128]{1,0:T(8,128)S(1)}, u32[]{:S(2)}, u32[]{:S(2)}) %collective-permute-start.2) | collective-permute-done | bytes 12320 | tf_op jit(solution)/shard_map/ppermute | solution.py:27
  19.9 1.0 %collective-permute-start.3 = (f32[24,128]{1,0:T(8,128)S(1)}, f32[24,128]{1,0:T(8,128)S(1)}, u32[]{:S(2)}, u32[]{:S(2)}) collective-permute-start(f32[24,128]{1,0:T(8,128)S(1)} %merge.11), channel_id=1, source_target_pairs={{0,4},{1,5},{2,6},{3,7},{4,0},{5,1},{6,2},{7,3},{8,12},{9,13},{10,... | collective-permute-start | bytes 36872 | tf_op jit(solution)/shard_map/ppermute | solution.py:27
  20.8 1.3 %collective-permute-start.13 = (f32[48,512]{1,0:T(8,128)S(1)}, f32[48,512]{1,0:T(8,128)S(1)}, u32[]{:S(2)}, u32[]{:S(2)}) collective-permute-start(f32[48,512]{1,0:T(8,128)S(1)} %get-tuple-element.58), channel_id=1, source_target_pairs={{1,0},{2,1},{3,2},{4,3},{5,4},{6,5},{7,6},{8,7},{9,8},{10,9},{11,1... | collective-permute-start | bytes 294920 | tf_op jit(solution)/shard_map/ppermute | solution.py:22
  22.1 1.4 %collective-permute-done.3 = f32[24,128]{1,0:T(8,128)S(1)} collective-permute-done((f32[24,128]{1,0:T(8,128)S(1)}, f32[24,128]{1,0:T(8,128)S(1)}, u32[]{:S(2)}, u32[]{:S(2)}) %collective-permute-start.3) | collective-permute-done | bytes 12320 | tf_op jit(solution)/shard_map/ppermute | solution.py:27
  23.6 1.0 %collective-permute-start.4 = (f32[2,24,128]{2,1,0:T(8,128)S(1)}, f32[2,24,128]{2,1,0:T(8,128)S(1)}, u32[]{:S(2)}, u32[]{:S(2)}) collective-permute-start(f32[2,24,128]{2,1,0:T(8,128)S(1)} %bitcast.11), channel_id=1, source_target_pairs={{0,2},{1,3},{2,0},{3,1},{4,6},{5,7},{6,4},{7,5},{8,10},{9,11},{10,... | collective-permute-start | bytes 73736 | tf_op jit(solution)/shard_map/ppermute | solution.py:27
  24.6 1.3 %collective-permute-start.6 = (f32[8,2048]{1,0:T(8,128)S(1)}, f32[8,2048]{1,0:T(8,128)S(1)}, u32[]{:S(2)}, u32[]{:S(2)}) collective-permute-start(f32[8,2048]{1,0:T(8,128)S(1)} %get-tuple-element.43), channel_id=1, source_target_pairs={{1,0},{2,1},{3,2},{4,3},{5,4},{6,5},{7,6},{8,7},{9,8},{10,9},{11,1... | collective-permute-start | bytes 196616 | tf_op jit(solution)/shard_map/ppermute | solution.py:22
  25.8 1.7 %collective-permute-done.4.second = f32[2,24,128]{2,1,0:T(8,128)S(1)} collective-permute-done((f32[2,24,128]{2,1,0:T(8,128)S(1)}, f32[2,24,128]{2,1,0:T(8,128)S(1)}, u32[]{:S(2)}, u32[]{:S(2)}) %collective-permute-start.4) | collective-permute-done | bytes 24608 | tf_op jit(solution)/shard_map/ppermute | solution.py:27
  27.5 0.0 collective-permute-start.5
  27.6 0.1 collective-permute-done.6.others_0_.from_next
  27.7 0.7 %inner_last.1 = (f32[1,64,1024]{2,1,0:T(8,128)S(1)}, bf16[1,80,1536]{2,1,0:T(8,128)(2,1)S(1)}, f32[1,96,1024]{2,1,0:T(8,128)S(1)}) custom-call(f32[4,24,128]{2,1,0:T(8,128)S(1)} %bitcast.8, s32[4,512]{1,0:T(4,128)S(1)} %get-tuple-element.33.matching, f32[4,8,1024]{2,1,0:T(8,128)S(1)} %get-tuple-element.34.padded, ...), custom_call_target="tpu_custom_call" | custom-call | tf_op jit(solution)/shard_map/inner_last/pallas_call | solution.py:565
  28.4 0.3 collective-permute-done.5.second
  28.8 0.9 %combine.1 = (f32[4,32,512]{2,1,0:T(8,128)S(1)}, f32[56,32]{1,0:T(8,128)S(1)}, f32[8,128]{1,0:T(8,128)S(1)}) custom-call(f32[8,24,128]{2,1,0:T(8,128)S(1)} %bitcast.10, f32[8,5376]{1,0:T(8,128)S(1)} %collective-permute-done.from_before, f32[32,768]{1,0:T(8,128)S(1)} %get-tuple-element.45.coarse_rows, ...), custom_call_target="tpu_custom_call" | custom-call | tf_op jit(solution)/shard_map/combine/pallas_call | solution.py:627
  29.7 3.8 %collective-permute-start.7 = (f32[8,128]{1,0:T(8,128)S(1)}, f32[8,128]{1,0:T(8,128)S(1)}, u32[]{:S(2)}, u32[]{:S(2)}) collective-permute-start(f32[8,128]{1,0:T(8,128)S(1)} %get-tuple-element.52.order.first), channel_id=1, source_target_pairs={{0,16},{1,17},{2,18},{3,19},{4,20},{5,21},{6,22},{7,23},{8,24},{9,... | collective-permute-start | bytes 12296 | tf_op jit(solution)/shard_map/ppermute | solution.py:27
  33.5 0.0 copy-start
  33.5 0.0 copy-start.1
  33.5 1.8 %outer.1 = (f32[4,32,512]{2,1,0:T(8,128)S(1)}, f32[4,32,512]{2,1,0:T(8,128)S(1)}) custom-call(f32[8,128]{1,0:T(8,128)S(1)} %get-tuple-element.52.order.first, s32[4,512]{1,0:T(4,128)S(1)} %get-tuple-element.33.matching, f32[2,96,1024]{2,1,0:T(8,128)S(1)} %get-tuple-element.41.order.whole_middle, f32[1,96,1024]{2,1,0:T(8,128)S(1)} %get-tuple-element.44.others_0_.whole_last, ...), custom_call_target="tpu_custom_call" | custom-call | tf_op jit(solution)/shard_map/outer/pallas_call | solution.py:652
  35.3 0.0 collective-permute-done.7.second
  35.3 1.7 %collective-permute-start.8 = (f32[8,128]{1,0:T(8,128)S(1)}, f32[8,128]{1,0:T(8,128)S(1)}, u32[]{:S(2)}, u32[]{:S(2)}) collective-permute-start(f32[8,128]{1,0:T(8,128)S(1)} %merge.15.first), channel_id=1, source_target_pairs={{0,8},{1,9},{2,10},{3,11},{4,12},{5,13},{6,14},{7,15},{8,0},{9,1},... | collective-permute-start | bytes 12296 | tf_op jit(solution)/shard_map/ppermute | solution.py:27
  37.0 2.0 %collective-permute-done.8.second = f32[8,128]{1,0:T(8,128)S(1)} collective-permute-done((f32[8,128]{1,0:T(8,128)S(1)}, f32[8,128]{1,0:T(8,128)S(1)}, u32[]{:S(2)}, u32[]{:S(2)}) %collective-permute-start.8) | collective-permute-done | bytes 4128 | tf_op jit(solution)/shard_map/ppermute | solution.py:27
  39.0 0.9 %collective-permute-start.9 = (f32[8,128]{1,0:T(8,128)S(1)}, f32[8,128]{1,0:T(8,128)S(1)}, u32[]{:S(2)}, u32[]{:S(2)}) collective-permute-start(f32[8,128]{1,0:T(8,128)S(1)} %merge.16.first), channel_id=1, source_target_pairs={{0,4},{1,5},{2,6},{3,7},{4,0},{5,1},{6,2},{7,3},{8,12},{9,13},{10,... | collective-permute-start | bytes 12296 | tf_op jit(solution)/shard_map/ppermute | solution.py:27
  39.9 2.7 %collective-permute-done.9.second = f32[8,128]{1,0:T(8,128)S(1)} collective-permute-done((f32[8,128]{1,0:T(8,128)S(1)}, f32[8,128]{1,0:T(8,128)S(1)}, u32[]{:S(2)}, u32[]{:S(2)}) %collective-permute-start.9) | collective-permute-done | bytes 4128 | tf_op jit(solution)/shard_map/ppermute | solution.py:27
  42.6 0.6 %collective-permute-start.10 = (f32[8,128]{1,0:T(8,128)S(1)}, f32[8,128]{1,0:T(8,128)S(1)}, u32[]{:S(2)}, u32[]{:S(2)}) collective-permute-start(f32[8,128]{1,0:T(8,128)S(1)} %merge.17.first), channel_id=1, source_target_pairs={{0,2},{1,3},{2,0},{3,1},{4,6},{5,7},{6,4},{7,5},{8,10},{9,11},{10,... | collective-permute-start | bytes 12296 | tf_op jit(solution)/shard_map/ppermute | solution.py:27
  43.2 3.0 %collective-permute-done.10.second = f32[8,128]{1,0:T(8,128)S(1)} collective-permute-done((f32[8,128]{1,0:T(8,128)S(1)}, f32[8,128]{1,0:T(8,128)S(1)}, u32[]{:S(2)}, u32[]{:S(2)}) %collective-permute-start.10) | collective-permute-done | bytes 4128 | tf_op jit(solution)/shard_map/ppermute | solution.py:27
  46.2 0.0 collective-permute-start.11
  46.2 1.2 %collective-permute-done.11.second = f32[8,128]{1,0:T(8,128)S(1)} collective-permute-done((f32[8,128]{1,0:T(8,128)S(1)}, f32[8,128]{1,0:T(8,128)S(1)}, u32[]{:S(2)}, u32[]{:S(2)}) %collective-permute-start.11) | collective-permute-done | bytes 4128 | tf_op jit(solution)/shard_map/ppermute | solution.py:27
  47.4 0.0 collective-permute-done.13.received_rest
  47.4 0.0 collective-permute-done.12.received_first
  47.4 0.0 copy-done
  47.4 0.0 copy-done.1
  47.4 1.2 %finish.1 = (f32[4,32,512]{2,1,0:T(8,128)}, f32[4,32,512]{2,1,0:T(8,128)}, f32[4,32,512]{2,1,0:T(8,128)}) custom-call(f32[8,128]{1,0:T(8,128)S(1)} %merge.19.sums, f32[1,32]{1,0:T(1,128)S(1)} %bitcast.15, f32[4,32,512]{2,1,0:T(8,128)S(1)} %copy-done, f32[4,32,512]{2,1,0:T(8,128)S(1)} %get-tuple-element.35.masked, ...), custom_call_target="tpu_custom_call" | custom-call | tf_op jit(solution)/shard_map/finish/pallas_call | solution.py:667
  (10 shorter events, 0.0 us)
Async XLA Ops:
  1.7 6.5 %collective-permute-start = (f32[8,5376]{1,0:T(8,128)S(1)}, f32[8,5376]{1,0:T(8,128)S(1)}, u32[]{:S(2)}, u32[]{:S(2)}) collective-permute-start(f32[8,5376]{1,0:T(8,128)S(1)} %first.1), channel_id=1, source_target_pairs={{0,1},{1,2},{2,3},{3,4},{4,5},{5,6},{6,7},{7,8},{8,9},{9,10},{10,1... | collective-permute-start | bytes 516104 | tf_op jit(solution)/shard_map/ppermute | solution.py:22
  8.4 7.7 %collective-permute-start.1 = (f32[24,128]{1,0:T(8,128)S(1)}, f32[24,128]{1,0:T(8,128)S(1)}, u32[]{:S(2)}, u32[]{:S(2)}) collective-permute-start(f32[24,128]{1,0:T(8,128)S(1)} %cross.1.order.first), channel_id=1, source_target_pairs={{0,16},{1,17},{2,18},{3,19},{4,20},{5,21},{6,22},{7,23},{8,24},{9,... | collective-permute-start | bytes 36872 | tf_op jit(solution)/shard_map/ppermute | solution.py:27
  16.2 3.7 %collective-permute-start.2 = (f32[24,128]{1,0:T(8,128)S(1)}, f32[24,128]{1,0:T(8,128)S(1)}, u32[]{:S(2)}, u32[]{:S(2)}) collective-permute-start(f32[24,128]{1,0:T(8,128)S(1)} %merge.10.first), channel_id=1, source_target_pairs={{0,8},{1,9},{2,10},{3,11},{4,12},{5,13},{6,14},{7,15},{8,0},{9,1},... | collective-permute-start | bytes 36872 | tf_op jit(solution)/shard_map/ppermute | solution.py:27
  18.1 29.4 %collective-permute-start.12 = (f32[56,512]{1,0:T(8,128)S(1)}, f32[56,512]{1,0:T(8,128)S(1)}, u32[]{:S(2)}, u32[]{:S(2)}) collective-permute-start(f32[56,512]{1,0:T(8,128)S(1)} %get-tuple-element.42.others_0_), channel_id=1, source_target_pairs={{1,0},{2,1},{3,2},{4,3},{5,4},{6,5},{7,6},{8,7},{9,8},{10,9},{11,1... | collective-permute-start | bytes 344072 | tf_op jit(solution)/shard_map/ppermute | solution.py:22
  19.9 3.7 %collective-permute-start.3 = (f32[24,128]{1,0:T(8,128)S(1)}, f32[24,128]{1,0:T(8,128)S(1)}, u32[]{:S(2)}, u32[]{:S(2)}) collective-permute-start(f32[24,128]{1,0:T(8,128)S(1)} %merge.11), channel_id=1, source_target_pairs={{0,4},{1,5},{2,6},{3,7},{4,0},{5,1},{6,2},{7,3},{8,12},{9,13},{10,... | collective-permute-start | bytes 36872 | tf_op jit(solution)/shard_map/ppermute | solution.py:27
  20.8 26.6 %collective-permute-start.13 = (f32[48,512]{1,0:T(8,128)S(1)}, f32[48,512]{1,0:T(8,128)S(1)}, u32[]{:S(2)}, u32[]{:S(2)}) collective-permute-start(f32[48,512]{1,0:T(8,128)S(1)} %get-tuple-element.58), channel_id=1, source_target_pairs={{1,0},{2,1},{3,2},{4,3},{5,4},{6,5},{7,6},{8,7},{9,8},{10,9},{11,1... | collective-permute-start | bytes 294920 | tf_op jit(solution)/shard_map/ppermute | solution.py:22
  23.6 4.0 %collective-permute-start.4 = (f32[2,24,128]{2,1,0:T(8,128)S(1)}, f32[2,24,128]{2,1,0:T(8,128)S(1)}, u32[]{:S(2)}, u32[]{:S(2)}) collective-permute-start(f32[2,24,128]{2,1,0:T(8,128)S(1)} %bitcast.11), channel_id=1, source_target_pairs={{0,2},{1,3},{2,0},{3,1},{4,6},{5,7},{6,4},{7,5},{8,10},{9,11},{10,... | collective-permute-start | bytes 73736 | tf_op jit(solution)/shard_map/ppermute | solution.py:27
  24.6 3.1 %collective-permute-start.6 = (f32[8,2048]{1,0:T(8,128)S(1)}, f32[8,2048]{1,0:T(8,128)S(1)}, u32[]{:S(2)}, u32[]{:S(2)}) collective-permute-start(f32[8,2048]{1,0:T(8,128)S(1)} %get-tuple-element.43), channel_id=1, source_target_pairs={{1,0},{2,1},{3,2},{4,3},{5,4},{6,5},{7,6},{8,7},{9,8},{10,9},{11,1... | collective-permute-start | bytes 196616 | tf_op jit(solution)/shard_map/ppermute | solution.py:22
  27.5 1.2 %collective-permute-start.5 = (f32[4,24,128]{2,1,0:T(8,128)S(1)}, f32[4,24,128]{2,1,0:T(8,128)S(1)}, u32[]{:S(2)}, u32[]{:S(2)}) collective-permute-start(f32[4,24,128]{2,1,0:T(8,128)S(1)} %bitcast.7), channel_id=1, source_target_pairs={{0,1},{1,0},{2,3},{3,2},{4,5},{5,4},{6,7},{7,6},{8,9},{9,8},{10,11... | collective-permute-start | bytes 147464 | tf_op jit(solution)/shard_map/ppermute | solution.py:27
  29.7 5.7 %collective-permute-start.7 = (f32[8,128]{1,0:T(8,128)S(1)}, f32[8,128]{1,0:T(8,128)S(1)}, u32[]{:S(2)}, u32[]{:S(2)}) collective-permute-start(f32[8,128]{1,0:T(8,128)S(1)} %get-tuple-element.52.order.first), channel_id=1, source_target_pairs={{0,16},{1,17},{2,18},{3,19},{4,20},{5,21},{6,22},{7,23},{8,24},{9,... | collective-permute-start | bytes 12296 | tf_op jit(solution)/shard_map/ppermute | solution.py:27
  33.5 13.9 %copy-start = (f32[4,32,512]{2,1,0:T(8,128)S(1)}, f32[4,32,512]{2,1,0:T(8,128)}, u32[]{:S(2)}) copy-start(f32[4,32,512]{2,1,0:T(8,128)} %multipliers.1) | copy-start | bytes 786436
  33.5 13.9 %copy-start.1 = (f32[32]{0:T(128)S(1)}, f32[32]{0:T(128)}, u32[]{:S(2)}) copy-start(f32[32]{0:T(128)} %param.11) | copy-start | bytes 388
  35.3 3.7 %collective-permute-start.8 = (f32[8,128]{1,0:T(8,128)S(1)}, f32[8,128]{1,0:T(8,128)S(1)}, u32[]{:S(2)}, u32[]{:S(2)}) collective-permute-start(f32[8,128]{1,0:T(8,128)S(1)} %merge.15.first), channel_id=1, source_target_pairs={{0,8},{1,9},{2,10},{3,11},{4,12},{5,13},{6,14},{7,15},{8,0},{9,1},... | collective-permute-start | bytes 12296 | tf_op jit(solution)/shard_map/ppermute | solution.py:27
  39.0 3.6 %collective-permute-start.9 = (f32[8,128]{1,0:T(8,128)S(1)}, f32[8,128]{1,0:T(8,128)S(1)}, u32[]{:S(2)}, u32[]{:S(2)}) collective-permute-start(f32[8,128]{1,0:T(8,128)S(1)} %merge.16.first), channel_id=1, source_target_pairs={{0,4},{1,5},{2,6},{3,7},{4,0},{5,1},{6,2},{7,3},{8,12},{9,13},{10,... | collective-permute-start | bytes 12296 | tf_op jit(solution)/shard_map/ppermute | solution.py:27
  42.6 3.6 %collective-permute-start.10 = (f32[8,128]{1,0:T(8,128)S(1)}, f32[8,128]{1,0:T(8,128)S(1)}, u32[]{:S(2)}, u32[]{:S(2)}) collective-permute-start(f32[8,128]{1,0:T(8,128)S(1)} %merge.17.first), channel_id=1, source_target_pairs={{0,2},{1,3},{2,0},{3,1},{4,6},{5,7},{6,4},{7,5},{8,10},{9,11},{10,... | collective-permute-start | bytes 12296 | tf_op jit(solution)/shard_map/ppermute | solution.py:27
  46.2 1.2 %collective-permute-start.11 = (f32[8,128]{1,0:T(8,128)S(1)}, f32[8,128]{1,0:T(8,128)S(1)}, u32[]{:S(2)}, u32[]{:S(2)}) collective-permute-start(f32[8,128]{1,0:T(8,128)S(1)} %merge.18.first), channel_id=1, source_target_pairs={{0,1},{1,0},{2,3},{3,2},{4,5},{5,4},{6,7},{7,6},{8,9},{9,8},{10,11... | collective-permute-start | bytes 12296 | tf_op jit(solution)/shard_map/ppermute | solution.py:27

commit v4 on v3

--- a/solution.py
+++ b/solution.py
@@ -178,7 +178,8 @@
     width = half + coarse_rows.shape[1]
     pack_before[:, :half] = face_modes[0]
     pack_before[:, half:width] = coarse_rows[0:8, :]
-    pack_before[:, width:] = coarse_rows[8:16, :]
+    pack_before[:, width : width + coarse_rows.shape[1]] = coarse_rows[8:16, :]
+    pack_before[:, width + coarse_rows.shape[1] :] = jnp.zeros((8, half), jnp.float32)
     fetches[3].wait()
     old_masked[count - 1] = old_masked[count - 1] * keep
     for copy in fetches[5:]:
@@ -327,7 +328,7 @@
     cut = returned.shape[0]
     returned[...] = moved[0:cut]
     returned_rest[...] = jnp.zeros_like(returned_rest)
-    returned_rest[0 : returned_rest.shape[0] - 16] = moved[cut : cut + returned_rest.shape[0] - 16]
+    returned_rest[0 : returned_rest.shape[0] - 8] = moved[cut : cut + returned_rest.shape[0] - 8]
 
 
 def outer_kernel(order, matching, whole_middle, whole_last, right_first, coeffs, *others):
@@ -355,15 +356,19 @@
             following = moved
 
 
-def add_kernel(first, second, *others):
-    others[-1][...] = first[...] + second[...]
-
-
-def pair_kernel(distance, first, second, *others):
+def add_kernel(offsets, own, *others):
+    total = own[...]
+    for k in range(len(offsets)):
+        total = total + others[k][...]
+    others[-1][...] = total
+
+
+def place_kernel(offsets, distance, own, *others):
     out = others[-1]
-    upper = (lax.axis_index(AXES) // distance) % 2
-    out[:, pl.ds(upper, 1)] = first[...][:, None]
-    out[:, pl.ds(1 - upper, 1)] = second[...][:, None]
+    place = (lax.axis_index(AXES) // distance) % out.shape[1]
+    out[:, pl.ds(place, 1)] = own[...][:, None]
+    for k, offset in enumerate(offsets):
+        out[:, pl.ds(place ^ offset, 1)] = others[k][...][:, None]
 
 
 def combine_kernel(
@@ -385,11 +390,20 @@
             from_before[:, half : half + width],
             coarse_rows[...],
             from_next[:, half : half + width],
-            from_next[:, half + width :],
+            from_next[:, half + width : half + 2 * width],
         ],
         axis=0,
     )
-    near = plain_dot(rows, stacked, HIGHEST)
+    high, low = halves(rows)
+    stacked_high, stacked_low = halves(stacked)
+    depth = rows.shape[0]
+    wide = plain_dot(
+        jnp.concatenate([high.astype(jnp.float32), low.astype(jnp.float32)], axis=0).astype(
+            jnp.bfloat16
+        ),
+        stacked_high,
+    )
+    near = wide[0:depth] + wide[depth:] + plain_dot(high, stacked_low)
     coeffs[...] = near
     lanes = 128
     totals = [jnp.zeros((cases, lanes), jnp.float32) for _ in range(4)]
@@ -413,7 +427,9 @@
         totals[1] += folded(mine * mine)
         totals[2] += folded(mine * other)
         totals[3] += folded(other * other)
-    sums[...] = rows_dot(jnp.ones((8, lanes), jnp.float32), jnp.concatenate(totals, axis=0), HIGHEST)
+    high, low = halves(jnp.concatenate(totals, axis=0))
+    ones = jnp.ones((8, lanes), jnp.bfloat16)
+    sums[...] = rows_dot(ones, high) + rows_dot(ones, low)
 
 
 def finish_kernel(
@@ -521,7 +537,7 @@
         out_shape=(
             shape((count, 8, half), f32),
             shape((own_rows, copies * cases), f32),
-            shape((8, half + 2 * coarse_width), f32),
+            shape((8, 2 * half + 2 * coarse_width), f32),
             shape((count, cases, half), f32),
             shape((count, cases, half), f32),
             shape((count, 8, full), f32),
@@ -551,15 +567,34 @@
     operand = pltpu.VMEM((2 * (q + 32), full), jnp.bfloat16)
     fields = (match_copy, padded, masked, old_masked, face_modes)
 
-    def merged(kernel, out_shape, first, second, *after):
+    def exchanged(block, distance, width, placed, *after):
+        offsets = tuple(range(1, width))
+        partners = [swapped(block, k * distance) for k in offsets]
+        size = block.shape
+        if placed:
+            kernel = functools.partial(place_kernel, offsets, distance)
+            size = (block.shape[0], width) + block.shape[1:]
+        else:
+            kernel = functools.partial(add_kernel, offsets)
         return pl.pallas_call(
             kernel,
-            out_shape=shape(out_shape, f32),
-            in_specs=[VMEM] * 2 + [ANY] * len(after),
+            out_shape=shape(size, f32),
+            in_specs=[VMEM] * width + [ANY] * len(after),
             out_specs=VMEM,
             compiler_params=PARAMS,
             name="merge",
-        )(first, second, *after)
+        )(block, *partners, *after)
+
+    def rounds_of(most):
+        rounds = []
+        distance = devices
+        while distance > 1:
+            width = most if 2 * most <= distance <= share else 2
+            distance //= width
+            rounds.append((distance, width))
+        return rounds
+
+    rounds = rounds_of(2)
 
     def inner(subs, order, *halos):
         return pl.pallas_call(
@@ -586,12 +621,9 @@
         name="cross",
     )(own_sums, face_modes, from_before, whole_middle)
 
-    turn = 0
-    distance = devices // 2
-    while distance >= 1:
-        turn += 1
+    for turn, (distance, width) in enumerate(rounds):
         after = ()
-        if turn == 1:
+        if turn == 0:
             inner_first, basis_first, right_first, *returned = pl.pallas_call(
                 start_kernel,
                 out_shape=(
@@ -599,7 +631,7 @@
                     shape((1, 80, half + full), jnp.bfloat16),
                     shape((q + 32, half), f32),
                     shape((cut, half), f32),
-                    shape((q + 40 - cut, half), f32),
+                    shape((q + 24 + 8 - cut, half), f32),
                 ),
                 in_specs=[ANY] + [VMEM] * (6 + row_blocks),
                 out_specs=(VMEM,) * 5,
@@ -609,20 +641,15 @@
             )(block, *fields, from_before, *factor)
             after = (returned[0],)
             received = [shifted(part, -1) for part in returned]
-        elif turn == 5:
+        elif turn == len(rounds) - 1:
             inner_last, basis_last, whole_last = inner((count - 1,), block, from_next)
             after = (whole_last,)
-        partner = swapped(block, distance)
-        if distance >= share:
-            block = merged(add_kernel, block.shape, block, partner, *after)
-        else:
-            if block.ndim == 2:
-                block, partner = block[None], partner[None]
-            pair = functools.partial(pair_kernel, distance)
-            size = block.shape[0]
-            block = merged(pair, (size, 2) + block.shape[1:], block, partner, *after)
-            block = block.reshape((2 * size,) + block.shape[2:])
-        distance //= 2
+        placed = distance < share
+        if placed and block.ndim == 2:
+            block = block[None]
+        block = exchanged(block, distance, width, placed, *after)
+        if placed:
+            block = block.reshape((-1,) + block.shape[2:])
 
     projected, coeffs, sums = pl.pallas_call(
         functools.partial(combine_kernel, copies),
@@ -658,11 +685,9 @@
         name="outer",
     )(sums, match_copy, whole_middle, whole_last, right_first, coeffs, *factor)
     after = (image_proj,)
-    distance = devices // 2
-    while distance >= 1:
-        sums = merged(add_kernel, sums.shape, sums, swapped(sums, distance), *after)
+    for distance, width in rounds_of(4):
+        sums = exchanged(sums, distance, width, False, *after)
         after = ()
-        distance //= 2
 
     return pl.pallas_call(
         finish_kernel,

time: 49 us -> 46.8 us (0.955)
  waiting for transfers between devices: 13.6 us -> 10.3 us
  starting transfers between devices: 23.1 us -> 24.3 us
    ppermute x10 -> x11, waiting for transfers between devices: 13.4 us -> 10.3 us  [swapped(): return lax.ppermute(block, AXES, route)]
    ppermute x10 -> x11, starting transfers between devices: 16.9 us -> 18.1 us  [swapped(): return lax.ppermute(block, AXES, route)]
  transfers between devices with their start and end apart: 14 -> 15, of which waited for: 10 -> 10; matrix products, arithmetic and copies ran while one was open for 0% -> 0% of each run, Pallas kernels for 18% -> 19%
where the time goes in v4:
time: 46.8 us; the launch traced here: 46.5 us
  starting transfers between devices  24.3 us (52%)
  Pallas kernels  11.2 us (24%)
  waiting for transfers between devices  10.3 us (22%)
  between operations  0.78 us (2%)
    ppermute x11, starting transfers between devices, swapped(): return lax.ppermute(block, AXES, route)  18.1 us
    ppermute x11, waiting for transfers between devices, swapped(): return lax.ppermute(block, AXES, route)  10.3 us
    ppermute x4, starting transfers between devices, shifted(): return lax.ppermute(block, AXES, route)  6.21 us
    pallas_call x1, Pallas kernels, on_device(): pl.pallas_call(functools.partial(prepare_kernel, copies, share), out_shap...  2.93 us
    pallas_call x2, Pallas kernels, inner(): pl.pallas_call(functools.partial(later_kernel, subs), out_shape=(shape((l...  1.93 us
    pallas_call x1, Pallas kernels, on_device(): pl.pallas_call(outer_kernel, out_shape=(shape((count, cases, half), f32),...  1.83 us
    pallas_call x1, Pallas kernels, on_device(): pl.pallas_call(finish_kernel, out_shape=(shape((count, cases, half), f32)...  1.23 us
    pallas_call x1, Pallas kernels, on_device(): pl.pallas_call(start_kernel, out_shape=(shape((1, q, full), f32), shape((...  1.14 us
  transfers between devices with their start and end apart: 15, of which 10 were waited for; matrix products, arithmetic and copies ran while one was open for 0% of the time, Pallas kernels for 19%

profile of v4, /device:TPU:0, one launch (start us, length us, event | category | flops | bytes accessed | tf_op | source)
XLA Modules:
  0.0 46.5 jit_solution(6176328681931917663)
XLA Ops:
  0.6 1.0 %first.1 = f32[8,5376]{1,0:T(8,128)S(1)} custom-call(f32[6,4,1024]{2,1,0:T(4,128)} %bitcast.15, f32[24,768]{1,0:T(8,128)} %coarse_in.3, f32[4,32,512]{2,1,0:T(8,128)} %residual_in.3, f32[4,32,512]{2,1,0:T(8,128)} %old_in.3), custom_call_target="tpu_custom_call" | custom-call | tf_op jit(solution)/shard_map/first/pallas_call | solution.py:509
  1.7 2.4 %collective-permute-start = (f32[8,5376]{1,0:T(8,128)S(1)}, f32[8,5376]{1,0:T(8,128)S(1)}, u32[]{:S(2)}, u32[]{:S(2)}) collective-permute-start(f32[8,5376]{1,0:T(8,128)S(1)} %first.1), channel_id=1, source_target_pairs={{0,1},{1,2},{2,3},{3,4},{4,5},{5,6},{6,7},{7,8},{8,9},{9,10},{10,1... | collective-permute-start | bytes 516104 | tf_op jit(solution)/shard_map/ppermute | solution.py:22
  4.1 2.9 %prepare.1 = (f32[4,8,512]{2,1,0:T(8,128)S(1)}, f32[24,128]{1,0:T(8,128)S(1)}, f32[8,2560]{1,0:T(8,128)S(1)}, f32[4,32,512]{2,1,0:T(8,128)S(1)}, f32[4,32,512]{2...) custom-call(s32[4,512]{1,0:T(4,128)} %matching_in.1, ...), custom_call_target="tpu_custom_call" | custom-call | tf_op jit(solution)/shard_map/prepare/pallas_call | solution.py:535
  7.0 1.2 %inner_middle.1 = (f32[2,64,1024]{2,1,0:T(8,128)S(1)}, bf16[2,80,1536]{2,1,0:T(8,128)(2,1)S(1)}, f32[2,96,1024]{2,1,0:T(8,128)S(1)}) custom-call(f32[24,128]{1,0:T(8,128)S(1)} %get-tuple-element.31.order.own_sums, s32[4,512]{1,0:T(4,128)S(1)} %get-tuple-element.33.matching, f32[4,8,1024]{2,1,0:T(8,128)S(1)} %get-tuple-element.34.padded, ...), custom_call_target="tpu_custom_call" | custom-call | tf_op jit(solution)/shard_map/inner_middle/pallas_call | solution.py:600
  8.2 0.0 collective-permute-done.from_before
  8.2 0.2 cross.1.order.own
  8.4 6.1 %collective-permute-start.1 = (f32[24,128]{1,0:T(8,128)S(1)}, f32[24,128]{1,0:T(8,128)S(1)}, u32[]{:S(2)}, u32[]{:S(2)}) collective-permute-start(f32[24,128]{1,0:T(8,128)S(1)} %cross.1.order.own), channel_id=1, source_target_pairs={{0,16},{1,17},{2,18},{3,19},{4,20},{5,21},{6,22},{7,23},{8,24},{9,... | collective-permute-start | bytes 36872 | tf_op jit(solution)/shard_map/ppermute | solution.py:27
  14.5 1.1 %inner_first.1 = (f32[1,64,1024]{2,1,0:T(8,128)S(1)}, bf16[1,80,1536]{2,1,0:T(8,128)(2,1)S(1)}, f32[96,512]{1,0:T(8,128)S(1)}, f32[56,512]{1,0:T(8,128)S(1)}, f32[40,512]{1,0:T(8,128)S(1)}) custom-call(f32[24,128]{1,0:T(8,128)S(1)} %cross.1.order.own, s32[4,512]{1,0:T(4,128)S(1)} %get-tuple-element.33.matching, f32[4,8,1024]{2,1,0:T(8,128)S(1)} %get-tuple-element.34.padded, ...), custom_call_target="tpu_custom_call" | custom-call | tf_op jit(solution)/shard_map/inner_first/pallas_call | solution.py:627
  15.6 0.5 %collective-permute-done.1.others_0_ = f32[24,128]{1,0:T(8,128)S(1)} collective-permute-done((f32[24,128]{1,0:T(8,128)S(1)}, f32[24,128]{1,0:T(8,128)S(1)}, u32[]{:S(2)}, u32[]{:S(2)}) %collective-permute-start.1) | collective-permute-done | bytes 12320 | tf_op jit(solution)/shard_map/ppermute | solution.py:27
  16.2 1.9 %collective-permute-start.2 = (f32[24,128]{1,0:T(8,128)S(1)}, f32[24,128]{1,0:T(8,128)S(1)}, u32[]{:S(2)}, u32[]{:S(2)}) collective-permute-start(f32[24,128]{1,0:T(8,128)S(1)} %merge.9.own), channel_id=1, source_target_pairs={{0,8},{1,9},{2,10},{3,11},{4,12},{5,13},{6,14},{7,15},{8,0},{9,1},... | collective-permute-start | bytes 36872 | tf_op jit(solution)/shard_map/ppermute | solution.py:27
  18.1 1.3 %collective-permute-start.13 = (f32[56,512]{1,0:T(8,128)S(1)}, f32[56,512]{1,0:T(8,128)S(1)}, u32[]{:S(2)}, u32[]{:S(2)}) collective-permute-start(f32[56,512]{1,0:T(8,128)S(1)} %get-tuple-element.42.others_1_), channel_id=1, source_target_pairs={{1,0},{2,1},{3,2},{4,3},{5,4},{6,5},{7,6},{8,7},{9,8},{10,9},{11,1... | collective-permute-start | bytes 344072 | tf_op jit(solution)/shard_map/ppermute | solution.py:22
  19.4 0.5 %collective-permute-done.2.others_0_ = f32[24,128]{1,0:T(8,128)S(1)} collective-permute-done((f32[24,128]{1,0:T(8,128)S(1)}, f32[24,128]{1,0:T(8,128)S(1)}, u32[]{:S(2)}, u32[]{:S(2)}) %collective-permute-start.2) | collective-permute-done | bytes 12320 | tf_op jit(solution)/shard_map/ppermute | solution.py:27
  19.9 1.0 %collective-permute-start.3 = (f32[1,24,128]{2,1,0:T(8,128)S(1)}, f32[1,24,128]{2,1,0:T(8,128)S(1)}, u32[]{:S(2)}, u32[]{:S(2)}) collective-permute-start(f32[1,24,128]{2,1,0:T(8,128)S(1)} %bitcast.12), channel_id=1, source_target_pairs={{0,4},{1,5},{2,6},{3,7},{4,0},{5,1},{6,2},{7,3},{8,12},{9,13},{10,... | collective-permute-start | bytes 36872 | tf_op jit(solution)/shard_map/ppermute | solution.py:27
  20.8 1.3 %collective-permute-start.6 = (f32[8,2560]{1,0:T(8,128)S(1)}, f32[8,2560]{1,0:T(8,128)S(1)}, u32[]{:S(2)}, u32[]{:S(2)}) collective-permute-start(f32[8,2560]{1,0:T(8,128)S(1)} %get-tuple-element.43), channel_id=1, source_target_pairs={{1,0},{2,1},{3,2},{4,3},{5,4},{6,5},{7,6},{8,7},{9,8},{10,9},{11,1... | collective-permute-start | bytes 245768 | tf_op jit(solution)/shard_map/ppermute | solution.py:22
  22.1 1.4 %collective-permute-done.3.others_0_ = f32[1,24,128]{2,1,0:T(8,128)S(1)} collective-permute-done((f32[1,24,128]{2,1,0:T(8,128)S(1)}, f32[1,24,128]{2,1,0:T(8,128)S(1)}, u32[]{:S(2)}, u32[]{:S(2)}) %collective-permute-start.3) | collective-permute-done | bytes 12320 | tf_op jit(solution)/shard_map/ppermute | solution.py:27
  23.6 1.0 %collective-permute-start.4 = (f32[2,24,128]{2,1,0:T(8,128)S(1)}, f32[2,24,128]{2,1,0:T(8,128)S(1)}, u32[]{:S(2)}, u32[]{:S(2)}) collective-permute-start(f32[2,24,128]{2,1,0:T(8,128)S(1)} %bitcast.10), channel_id=1, source_target_pairs={{0,2},{1,3},{2,0},{3,1},{4,6},{5,7},{6,4},{7,5},{8,10},{9,11},{10,... | collective-permute-start | bytes 73736 | tf_op jit(solution)/shard_map/ppermute | solution.py:27
  24.6 1.3 %collective-permute-start.14 = (f32[40,512]{1,0:T(8,128)S(1)}, f32[40,512]{1,0:T(8,128)S(1)}, u32[]{:S(2)}, u32[]{:S(2)}) collective-permute-start(f32[40,512]{1,0:T(8,128)S(1)} %get-tuple-element.58), channel_id=1, source_target_pairs={{1,0},{2,1},{3,2},{4,3},{5,4},{6,5},{7,6},{8,7},{9,8},{10,9},{11,1... | collective-permute-start | bytes 245768 | tf_op jit(solution)/shard_map/ppermute | solution.py:22
  25.8 1.5 %collective-permute-done.4.others_0_ = f32[2,24,128]{2,1,0:T(8,128)S(1)} collective-permute-done((f32[2,24,128]{2,1,0:T(8,128)S(1)}, f32[2,24,128]{2,1,0:T(8,128)S(1)}, u32[]{:S(2)}, u32[]{:S(2)}) %collective-permute-start.4) | collective-permute-done | bytes 24608 | tf_op jit(solution)/shard_map/ppermute | solution.py:27
  27.4 0.0 collective-permute-start.5
  27.4 0.0 collective-permute-done.6.others_0_.from_next
  27.4 0.8 %inner_last.1 = (f32[1,64,1024]{2,1,0:T(8,128)S(1)}, bf16[1,80,1536]{2,1,0:T(8,128)(2,1)S(1)}, f32[1,96,1024]{2,1,0:T(8,128)S(1)}) custom-call(f32[4,24,128]{2,1,0:T(8,128)S(1)} %bitcast.7, s32[4,512]{1,0:T(4,128)S(1)} %get-tuple-element.33.matching, f32[4,8,1024]{2,1,0:T(8,128)S(1)} %get-tuple-element.34.padded, ...), custom_call_target="tpu_custom_call" | custom-call | tf_op jit(solution)/shard_map/inner_last/pallas_call | solution.py:600
  28.2 0.5 collective-permute-done.5.others_0_
  28.6 0.8 %combine.1 = (f32[4,32,512]{2,1,0:T(8,128)S(1)}, f32[56,32]{1,0:T(8,128)S(1)}, f32[8,128]{1,0:T(8,128)S(1)}) custom-call(f32[8,24,128]{2,1,0:T(8,128)S(1)} %bitcast.9, f32[8,5376]{1,0:T(8,128)S(1)} %collective-permute-done.from_before, f32[32,768]{1,0:T(8,128)S(1)} %get-tuple-element.45.coarse_rows, ...), custom_call_target="tpu_custom_call" | custom-call | tf_op jit(solution)/shard_map/combine/pallas_call | solution.py:654
  29.4 3.0 %collective-permute-start.7 = (f32[8,128]{1,0:T(8,128)S(1)}, f32[8,128]{1,0:T(8,128)S(1)}, u32[]{:S(2)}, u32[]{:S(2)}) collective-permute-start(f32[8,128]{1,0:T(8,128)S(1)} %get-tuple-element.52.order.own), channel_id=1, source_target_pairs={{0,16},{1,17},{2,18},{3,19},{4,20},{5,21},{6,22},{7,23},{8,24},{9,... | collective-permute-start | bytes 12296 | tf_op jit(solution)/shard_map/ppermute | solution.py:27
  32.4 0.0 copy-start
  32.4 0.0 copy-start.1
  32.4 1.8 %outer.1 = (f32[4,32,512]{2,1,0:T(8,128)S(1)}, f32[4,32,512]{2,1,0:T(8,128)S(1)}) custom-call(f32[8,128]{1,0:T(8,128)S(1)} %get-tuple-element.52.order.own, s32[4,512]{1,0:T(4,128)S(1)} %get-tuple-element.33.matching, f32[2,96,1024]{2,1,0:T(8,128)S(1)} %get-tuple-element.41.order.whole_middle, f32[1,96,1024]{2,1,0:T(8,128)S(1)} %get-tuple-element.44.others_1_.whole_last, ...), custom_call_target="tpu_custom_call" | custom-call | tf_op jit(solution)/shard_map/outer/pallas_call | solution.py:679
  34.2 0.0 collective-permute-done.7.others_0_
  34.2 1.7 %collective-permute-start.8 = (f32[8,128]{1,0:T(8,128)S(1)}, f32[8,128]{1,0:T(8,128)S(1)}, u32[]{:S(2)}, u32[]{:S(2)}) collective-permute-start(f32[8,128]{1,0:T(8,128)S(1)} %merge.14.own), channel_id=1, source_target_pairs={{0,8},{1,9},{2,10},{3,11},{4,12},{5,13},{6,14},{7,15},{8,0},{9,1},... | collective-permute-start | bytes 12296 | tf_op jit(solution)/shard_map/ppermute | solution.py:27
  35.9 2.0 %collective-permute-done.8.others_0_ = f32[8,128]{1,0:T(8,128)S(1)} collective-permute-done((f32[8,128]{1,0:T(8,128)S(1)}, f32[8,128]{1,0:T(8,128)S(1)}, u32[]{:S(2)}, u32[]{:S(2)}) %collective-permute-start.8) | collective-permute-done | bytes 4128 | tf_op jit(solution)/shard_map/ppermute | solution.py:27
  37.9 1.8 %collective-permute-start.11 = (f32[8,128]{1,0:T(8,128)S(1)}, f32[8,128]{1,0:T(8,128)S(1)}, u32[]{:S(2)}, u32[]{:S(2)}) collective-permute-start(f32[8,128]{1,0:T(8,128)S(1)} %merge.15.own), channel_id=1, source_target_pairs={{0,6},{1,7},{2,4},{3,5},{4,2},{5,3},{6,0},{7,1},{8,14},{9,15},{10,... | collective-permute-start | bytes 12296 | tf_op jit(solution)/shard_map/ppermute | solution.py:27
  39.7 0.7 %collective-permute-start.10 = (f32[8,128]{1,0:T(8,128)S(1)}, f32[8,128]{1,0:T(8,128)S(1)}, u32[]{:S(2)}, u32[]{:S(2)}) collective-permute-start(f32[8,128]{1,0:T(8,128)S(1)} %merge.15.own), channel_id=1, source_target_pairs={{0,4},{1,5},{2,6},{3,7},{4,0},{5,1},{6,2},{7,3},{8,12},{9,13},{10,... | collective-permute-start | bytes 12296 | tf_op jit(solution)/shard_map/ppermute | solution.py:27
  40.4 1.0 %collective-permute-start.9 = (f32[8,128]{1,0:T(8,128)S(1)}, f32[8,128]{1,0:T(8,128)S(1)}, u32[]{:S(2)}, u32[]{:S(2)}) collective-permute-start(f32[8,128]{1,0:T(8,128)S(1)} %merge.15.own), channel_id=1, source_target_pairs={{0,2},{1,3},{2,0},{3,1},{4,6},{5,7},{6,4},{7,5},{8,10},{9,11},{10,... | collective-permute-start | bytes 12296 | tf_op jit(solution)/shard_map/ppermute | solution.py:27
  41.4 1.0 %collective-permute-done.11.others_2_ = f32[8,128]{1,0:T(8,128)S(1)} collective-permute-done((f32[8,128]{1,0:T(8,128)S(1)}, f32[8,128]{1,0:T(8,128)S(1)}, u32[]{:S(2)}, u32[]{:S(2)}) %collective-permute-start.11) | collective-permute-done | bytes 4128 | tf_op jit(solution)/shard_map/ppermute | solution.py:27
  42.4 0.9 %collective-permute-done.10.others_1_ = f32[8,128]{1,0:T(8,128)S(1)} collective-permute-done((f32[8,128]{1,0:T(8,128)S(1)}, f32[8,128]{1,0:T(8,128)S(1)}, u32[]{:S(2)}, u32[]{:S(2)}) %collective-permute-start.10) | collective-permute-done | bytes 4128 | tf_op jit(solution)/shard_map/ppermute | solution.py:27
  43.3 0.7 %collective-permute-done.9.others_0_ = f32[8,128]{1,0:T(8,128)S(1)} collective-permute-done((f32[8,128]{1,0:T(8,128)S(1)}, f32[8,128]{1,0:T(8,128)S(1)}, u32[]{:S(2)}, u32[]{:S(2)}) %collective-permute-start.9) | collective-permute-done | bytes 4128 | tf_op jit(solution)/shard_map/ppermute | solution.py:27
  44.1 0.0 collective-permute-start.12
  44.1 1.2 %collective-permute-done.12.others_0_ = f32[8,128]{1,0:T(8,128)S(1)} collective-permute-done((f32[8,128]{1,0:T(8,128)S(1)}, f32[8,128]{1,0:T(8,128)S(1)}, u32[]{:S(2)}, u32[]{:S(2)}) %collective-permute-start.12) | collective-permute-done | bytes 4128 | tf_op jit(solution)/shard_map/ppermute | solution.py:27
  45.2 0.0 collective-permute-done.14.received_rest
  45.2 0.0 collective-permute-done.13.received_first
  45.2 0.0 copy-done
  45.2 0.0 copy-done.1
  45.3 1.2 %finish.1 = (f32[4,32,512]{2,1,0:T(8,128)}, f32[4,32,512]{2,1,0:T(8,128)}, f32[4,32,512]{2,1,0:T(8,128)}) custom-call(f32[8,128]{1,0:T(8,128)S(1)} %merge.17.sums, f32[1,32]{1,0:T(1,128)S(1)} %bitcast.14, f32[4,32,512]{2,1,0:T(8,128)S(1)} %copy-done, f32[4,32,512]{2,1,0:T(8,128)S(1)} %get-tuple-element.35.masked, ...), custom_call_target="tpu_custom_call" | custom-call | tf_op jit(solution)/shard_map/finish/pallas_call | solution.py:692
  (9 shorter events, 0.0 us)
Async XLA Ops:
  1.7 6.5 %collective-permute-start = (f32[8,5376]{1,0:T(8,128)S(1)}, f32[8,5376]{1,0:T(8,128)S(1)}, u32[]{:S(2)}, u32[]{:S(2)}) collective-permute-start(f32[8,5376]{1,0:T(8,128)S(1)} %first.1), channel_id=1, source_target_pairs={{0,1},{1,2},{2,3},{3,4},{4,5},{5,6},{6,7},{7,8},{8,9},{9,10},{10,1... | collective-permute-start | bytes 516104 | tf_op jit(solution)/shard_map/ppermute | solution.py:22
  8.4 7.7 %collective-permute-start.1 = (f32[24,128]{1,0:T(8,128)S(1)}, f32[24,128]{1,0:T(8,128)S(1)}, u32[]{:S(2)}, u32[]{:S(2)}) collective-permute-start(f32[24,128]{1,0:T(8,128)S(1)} %cross.1.order.own), channel_id=1, source_target_pairs={{0,16},{1,17},{2,18},{3,19},{4,20},{5,21},{6,22},{7,23},{8,24},{9,... | collective-permute-start | bytes 36872 | tf_op jit(solution)/shard_map/ppermute | solution.py:27
  16.2 3.7 %collective-permute-start.2 = (f32[24,128]{1,0:T(8,128)S(1)}, f32[24,128]{1,0:T(8,128)S(1)}, u32[]{:S(2)}, u32[]{:S(2)}) collective-permute-start(f32[24,128]{1,0:T(8,128)S(1)} %merge.9.own), channel_id=1, source_target_pairs={{0,8},{1,9},{2,10},{3,11},{4,12},{5,13},{6,14},{7,15},{8,0},{9,1},... | collective-permute-start | bytes 36872 | tf_op jit(solution)/shard_map/ppermute | solution.py:27
  18.1 27.2 %collective-permute-start.13 = (f32[56,512]{1,0:T(8,128)S(1)}, f32[56,512]{1,0:T(8,128)S(1)}, u32[]{:S(2)}, u32[]{:S(2)}) collective-permute-start(f32[56,512]{1,0:T(8,128)S(1)} %get-tuple-element.42.others_1_), channel_id=1, source_target_pairs={{1,0},{2,1},{3,2},{4,3},{5,4},{6,5},{7,6},{8,7},{9,8},{10,9},{11,1... | collective-permute-start | bytes 344072 | tf_op jit(solution)/shard_map/ppermute | solution.py:22
  19.9 3.7 %collective-permute-start.3 = (f32[1,24,128]{2,1,0:T(8,128)S(1)}, f32[1,24,128]{2,1,0:T(8,128)S(1)}, u32[]{:S(2)}, u32[]{:S(2)}) collective-permute-start(f32[1,24,128]{2,1,0:T(8,128)S(1)} %bitcast.12), channel_id=1, source_target_pairs={{0,4},{1,5},{2,6},{3,7},{4,0},{5,1},{6,2},{7,3},{8,12},{9,13},{10,... | collective-permute-start | bytes 36872 | tf_op jit(solution)/shard_map/ppermute | solution.py:27
  20.8 6.6 %collective-permute-start.6 = (f32[8,2560]{1,0:T(8,128)S(1)}, f32[8,2560]{1,0:T(8,128)S(1)}, u32[]{:S(2)}, u32[]{:S(2)}) collective-permute-start(f32[8,2560]{1,0:T(8,128)S(1)} %get-tuple-element.43), channel_id=1, source_target_pairs={{1,0},{2,1},{3,2},{4,3},{5,4},{6,5},{7,6},{8,7},{9,8},{10,9},{11,1... | collective-permute-start | bytes 245768 | tf_op jit(solution)/shard_map/ppermute | solution.py:22
  23.6 3.8 %collective-permute-start.4 = (f32[2,24,128]{2,1,0:T(8,128)S(1)}, f32[2,24,128]{2,1,0:T(8,128)S(1)}, u32[]{:S(2)}, u32[]{:S(2)}) collective-permute-start(f32[2,24,128]{2,1,0:T(8,128)S(1)} %bitcast.10), channel_id=1, source_target_pairs={{0,2},{1,3},{2,0},{3,1},{4,6},{5,7},{6,4},{7,5},{8,10},{9,11},{10,... | collective-permute-start | bytes 73736 | tf_op jit(solution)/shard_map/ppermute | solution.py:27
  24.6 20.7 %collective-permute-start.14 = (f32[40,512]{1,0:T(8,128)S(1)}, f32[40,512]{1,0:T(8,128)S(1)}, u32[]{:S(2)}, u32[]{:S(2)}) collective-permute-start(f32[40,512]{1,0:T(8,128)S(1)} %get-tuple-element.58), channel_id=1, source_target_pairs={{1,0},{2,1},{3,2},{4,3},{5,4},{6,5},{7,6},{8,7},{9,8},{10,9},{11,1... | collective-permute-start | bytes 245768 | tf_op jit(solution)/shard_map/ppermute | solution.py:22
  27.4 1.2 %collective-permute-start.5 = (f32[4,24,128]{2,1,0:T(8,128)S(1)}, f32[4,24,128]{2,1,0:T(8,128)S(1)}, u32[]{:S(2)}, u32[]{:S(2)}) collective-permute-start(f32[4,24,128]{2,1,0:T(8,128)S(1)} %bitcast.6), channel_id=1, source_target_pairs={{0,1},{1,0},{2,3},{3,2},{4,5},{5,4},{6,7},{7,6},{8,9},{9,8},{10,11... | collective-permute-start | bytes 147464 | tf_op jit(solution)/shard_map/ppermute | solution.py:27
  29.4 4.8 %collective-permute-start.7 = (f32[8,128]{1,0:T(8,128)S(1)}, f32[8,128]{1,0:T(8,128)S(1)}, u32[]{:S(2)}, u32[]{:S(2)}) collective-permute-start(f32[8,128]{1,0:T(8,128)S(1)} %get-tuple-element.52.order.own), channel_id=1, source_target_pairs={{0,16},{1,17},{2,18},{3,19},{4,20},{5,21},{6,22},{7,23},{8,24},{9,... | collective-permute-start | bytes 12296 | tf_op jit(solution)/shard_map/ppermute | solution.py:27
  32.4 12.8 %copy-start = (f32[4,32,512]{2,1,0:T(8,128)S(1)}, f32[4,32,512]{2,1,0:T(8,128)}, u32[]{:S(2)}) copy-start(f32[4,32,512]{2,1,0:T(8,128)} %multipliers.1) | copy-start | bytes 786436
  32.4 12.9 %copy-start.1 = (f32[32]{0:T(128)S(1)}, f32[32]{0:T(128)}, u32[]{:S(2)}) copy-start(f32[32]{0:T(128)} %param.11) | copy-start | bytes 388
  34.2 3.7 %collective-permute-start.8 = (f32[8,128]{1,0:T(8,128)S(1)}, f32[8,128]{1,0:T(8,128)S(1)}, u32[]{:S(2)}, u32[]{:S(2)}) collective-permute-start(f32[8,128]{1,0:T(8,128)S(1)} %merge.14.own), channel_id=1, source_target_pairs={{0,8},{1,9},{2,10},{3,11},{4,12},{5,13},{6,14},{7,15},{8,0},{9,1},... | collective-permute-start | bytes 12296 | tf_op jit(solution)/shard_map/ppermute | solution.py:27
  37.9 4.5 %collective-permute-start.11 = (f32[8,128]{1,0:T(8,128)S(1)}, f32[8,128]{1,0:T(8,128)S(1)}, u32[]{:S(2)}, u32[]{:S(2)}) collective-permute-start(f32[8,128]{1,0:T(8,128)S(1)} %merge.15.own), channel_id=1, source_target_pairs={{0,6},{1,7},{2,4},{3,5},{4,2},{5,3},{6,0},{7,1},{8,14},{9,15},{10,... | collective-permute-start | bytes 12296 | tf_op jit(solution)/shard_map/ppermute | solution.py:27
  39.7 3.6 %collective-permute-start.10 = (f32[8,128]{1,0:T(8,128)S(1)}, f32[8,128]{1,0:T(8,128)S(1)}, u32[]{:S(2)}, u32[]{:S(2)}) collective-permute-start(f32[8,128]{1,0:T(8,128)S(1)} %merge.15.own), channel_id=1, source_target_pairs={{0,4},{1,5},{2,6},{3,7},{4,0},{5,1},{6,2},{7,3},{8,12},{9,13},{10,... | collective-permute-start | bytes 12296 | tf_op jit(solution)/shard_map/ppermute | solution.py:27
  40.4 3.6 %collective-permute-start.9 = (f32[8,128]{1,0:T(8,128)S(1)}, f32[8,128]{1,0:T(8,128)S(1)}, u32[]{:S(2)}, u32[]{:S(2)}) collective-permute-start(f32[8,128]{1,0:T(8,128)S(1)} %merge.15.own), channel_id=1, source_target_pairs={{0,2},{1,3},{2,0},{3,1},{4,6},{5,7},{6,4},{7,5},{8,10},{9,11},{10,... | collective-permute-start | bytes 12296 | tf_op jit(solution)/shard_map/ppermute | solution.py:27
  44.1 1.2 %collective-permute-start.12 = (f32[8,128]{1,0:T(8,128)S(1)}, f32[8,128]{1,0:T(8,128)S(1)}, u32[]{:S(2)}, u32[]{:S(2)}) collective-permute-start(f32[8,128]{1,0:T(8,128)S(1)} %merge.16.own), channel_id=1, source_target_pairs={{0,1},{1,0},{2,3},{3,2},{4,5},{5,4},{6,7},{7,6},{8,9},{9,8},{10,11... | collective-permute-start | bytes 12296 | tf_op jit(solution)/shard_map/ppermute | solution.py:27

commit v5 on v4

--- a/solution.py
+++ b/solution.py
@@ -78,26 +78,29 @@
 
 def first_kernel(modes_in, coarse_in, residual_in, old_in, pack_next, modes, coarse, arrived):
     ranks, count, full = modes_in.shape
-    half = full // 2
-    width = coarse_in.shape[1]
-    pairs = [(modes_in, modes), (coarse_in, coarse)]
-    lane = half + width
-    for field in (residual_in, old_in):
-        for k in range(field.shape[1] // 8):
-            pairs.append(
-                (field.at[count - 1, pl.ds(8 * k, 8)], pack_next.at[:, pl.ds(lane, half)])
-            )
-            lane += half
+    _, cases, half = residual_in.shape
+    rows, width = coarse.shape
+    last = count - 1
+    pairs = [
+        (modes_in.at[:, :, pl.ds(half, half)], modes),
+        (coarse_in.at[pl.ds(coarse_in.shape[0] - rows, rows)], coarse),
+        (residual_in.at[last], pack_next.at[pl.ds(0, cases)]),
+        (old_in.at[last], pack_next.at[pl.ds(cases, cases)]),
+    ]
     fetches = [pltpu.make_async_copy(a, b, arrived.at[i]) for i, (a, b) in enumerate(pairs)]
     for fetch in fetches:
         fetch.start()
-    pack_next[:, : half + width] = jnp.zeros((8, half + width), jnp.float32)
+    row = 2 * cases
+    pack_next[row:, :] = jnp.zeros((pack_next.shape[0] - row, half), jnp.float32)
     fetches[0].wait()
-    pack_next[0:ranks, :half] = modes[:, count - 1, half:]
+    pack_next[row : row + ranks, :] = modes[:, last, :]
     fetches[1].wait()
-    pack_next[0:ranks, half : half + width] = coarse[(count - 1) * ranks : count * ranks, :]
-    for fetch in fetches[2:]:
-        fetch.wait()
+    for lane in range(0, width, half):
+        row += 8
+        part = coarse[rows - ranks :, lane : min(lane + half, width)]
+        pack_next[row : row + ranks, : part.shape[1]] = part
+    fetches[2].wait()
+    fetches[3].wait()
 
 
 def at_face_before(left, table):
@@ -188,18 +191,10 @@
 
 def cross_kernel(copies, share, ranks, own_sums, face_modes, from_before, order, out):
     lane_block = lax.axis_index(AXES) // share
-    half = face_modes.shape[2]
-    fields = from_before.shape[1] - 2 * half * (out.shape[1] // copies // 8)
-    field = unpacked(from_before, fields, out.shape[1] // copies, half)
-    cross = rows_dot(face_modes[0], field, HIGHEST)
+    cases = out.shape[1] // copies
+    cross = rows_dot(face_modes[0], from_before[0:cases], HIGHEST)
     out[...] = own_sums[...]
     out[0:ranks, :] = own_sums[0:ranks, :] - in_lane_block(cross, lane_block, copies)[0:ranks]
-
-
-def unpacked(pack, start, cases, half):
-    return jnp.concatenate(
-        [pack[:, start + k * half : start + (k + 1) * half] for k in range(cases // 8)], axis=0
-    )
 
 
 def inner_part(g, matching, padded, masked, old_masked, face_modes, held, from_before, from_next, operand):
@@ -213,10 +208,8 @@
     left_modes = padded[g, :, :half]
     right_modes = padded[g, :, half:]
     if g == 0:
-        fields = from_before.shape[1] - 2 * half * (cases // 8)
-        prior_modes = from_before[:, :half]
-        prior_res = unpacked(from_before, fields, cases, half)
-        prior_old = unpacked(from_before, fields + half * (cases // 8), cases, half)
+        prior_res, prior_old = from_before[0:cases], from_before[cases : 2 * cases]
+        prior_modes = from_before[2 * cases : 2 * cases + 8]
         left_modes = left_modes * jnp.where(me == 0, 0.0, 1.0)
     else:
         prior_modes = padded[g - 1, :, half:]
@@ -385,9 +378,13 @@
     width = coarse_rows.shape[1]
     own = gathered[...].reshape(gathered.shape[0] * gathered.shape[1], copies * cases)
     stacked = jnp.concatenate([own[:, b * cases : (b + 1) * cases] for b in range(copies)], axis=0)
+    first = 2 * cases + 8
+    prior = jnp.concatenate(
+        [from_before[k : k + 8] for k in range(first, from_before.shape[0], 8)], axis=1
+    )
     rows = jnp.concatenate(
         [
-            from_before[:, half : half + width],
+            prior[:, :width],
             coarse_rows[...],
             from_next[:, half : half + width],
             from_next[:, half + width : half + 2 * width],
@@ -432,6 +429,15 @@
     sums[...] = rows_dot(ones, high) + rows_dot(ones, low)
 
 
+def settle_kernel(order, image_proj, image_old, coeffs, received_first, received_rest, proj, old):
+    count, cases, _ = image_proj.shape
+    received = jnp.concatenate([received_first[...], received_rest[...]], axis=0)
+    basis = three_terms(received[2 * cases : 2 * cases + 24])
+    near = coeffs[8 * count : 8 * count + 24]
+    proj[...] = image_proj[count - 1] - received[0:cases] + across(near, basis)
+    old[...] = image_old[count - 1] - received[cases : 2 * cases]
+
+
 def finish_kernel(
     sums,
     old_norms,
@@ -441,9 +447,8 @@
     projected,
     image_proj,
     image_old,
-    coeffs,
-    received_first,
-    received_rest,
+    last_proj,
+    last_old,
     new_multipliers,
     new_residual,
     direction,
@@ -468,11 +473,7 @@
     for g in range(count):
         image_p, image_o = image_proj[g], image_old[g]
         if g == count - 1:
-            received = jnp.concatenate([received_first[...], received_rest[...]], axis=0)
-            basis = three_terms(received[2 * cases : 2 * cases + 24])
-            near = coeffs[8 * count : 8 * count + 24]
-            image_p = image_p - received[0:cases] + across(near, basis)
-            image_o = image_o - received[cases : 2 * cases]
+            image_p, image_o = last_proj[...], last_old[...]
         towards = projected[g] + ratio * old_masked[g]
         direction[g] = towards
         new_multipliers[g] = multipliers[g] + step_len * towards
@@ -505,16 +506,17 @@
     in_hbm = lambda *arrays: (pltpu.with_memory_space_constraint(x, pltpu.HBM) for x in arrays)
 
     modes_by_rank = rigid_modes.transpose(1, 0, 2)
-    next_width = half + coarse_width + 2 * half * (cases // 8)
+    next_rows = 2 * cases + 8 + 8 * pl.cdiv(coarse_width, half)
+    coarse_part = own_rows - (own_rows - ranks) // 8 * 8
     pack_next = pl.pallas_call(
         first_kernel,
-        out_shape=shape((8, next_width), f32),
+        out_shape=shape((next_rows, half), f32),
         in_specs=[HBM] * 4,
         out_specs=VMEM,
         scratch_shapes=[
-            pltpu.VMEM((ranks, count, full), f32),
-            pltpu.VMEM((own_rows, coarse_width), f32),
-            pltpu.SemaphoreType.DMA((2 + 2 * (cases // 8),)),
+            pltpu.VMEM((ranks, count, half), f32),
+            pltpu.VMEM((coarse_part, coarse_width), f32),
+            pltpu.SemaphoreType.DMA((4,)),
         ],
         compiler_params=PARAMS,
         name="first",
@@ -685,14 +687,25 @@
         name="outer",
     )(sums, match_copy, whole_middle, whole_last, right_first, coeffs, *factor)
     after = (image_proj,)
-    for distance, width in rounds_of(4):
+    rounds = sorted(rounds_of(4), key=lambda one: -one[1])
+    for distance, width in rounds:
+        if distance == rounds[-1][0]:
+            last_proj, last_old = pl.pallas_call(
+                settle_kernel,
+                out_shape=(shape((cases, half), f32),) * 2,
+                in_specs=[ANY] + [VMEM] * 5,
+                out_specs=(VMEM,) * 2,
+                compiler_params=PARAMS,
+                name="settle",
+            )(sums, image_proj, image_old, coeffs, *received)
+            after = (last_proj,)
         sums = exchanged(sums, distance, width, False, *after)
         after = ()
 
     return pl.pallas_call(
         finish_kernel,
         out_shape=(shape((count, cases, half), f32),) * 3,
-        in_specs=[VMEM] * 11,
+        in_specs=[VMEM] * 10,
         out_specs=(VMEM,) * 3,
         compiler_params=PARAMS,
         name="finish",
@@ -705,8 +718,8 @@
         projected,
         image_proj,
         image_old,
-        coeffs,
-        *received,
+        last_proj,
+        last_old,
     )
 
 

time: 46.8 us -> 46.5 us (level)
    pallas_call x1 -> x2, Pallas kernels: 1.04 us -> 1.14 us  [the longest x1 0.96 us: on_device(): pl.pallas_call(first_kernel, out_shape=shape((next_rows, half), f32), in_...]
where the time goes in v5:
time: 46.5 us; the launch traced here: 46.2 us
  starting transfers between devices  24.1 us (52%)
  Pallas kernels  11.2 us (24%)
  waiting for transfers between devices  10.1 us (22%)
  between operations  0.76 us (2%)
    ppermute x11, starting transfers between devices, swapped(): return lax.ppermute(block, AXES, route)  17.9 us
    ppermute x11, waiting for transfers between devices, swapped(): return lax.ppermute(block, AXES, route)  10.1 us
    ppermute x4, starting transfers between devices, shifted(): return lax.ppermute(block, AXES, route)  6.21 us
    pallas_call x1, Pallas kernels, on_device(): pl.pallas_call(functools.partial(prepare_kernel, copies, share), out_shap...  2.93 us
    pallas_call x2, Pallas kernels, inner(): pl.pallas_call(functools.partial(later_kernel, subs), out_shape=(shape((l...  1.94 us
    pallas_call x1, Pallas kernels, on_device(): pl.pallas_call(outer_kernel, out_shape=(shape((count, cases, half), f32),...  1.82 us
    pallas_call x1, Pallas kernels, on_device(): pl.pallas_call(finish_kernel, out_shape=(shape((count, cases, half), f32)...  1.22 us
    pallas_call x1, Pallas kernels, on_device(): pl.pallas_call(start_kernel, out_shape=(shape((1, q, full), f32), shape((...  1.14 us
  transfers between devices with their start and end apart: 15, of which 10 were waited for; matrix products, arithmetic and copies ran while one was open for 0% of the time, Pallas kernels for 19%

profile of v5, /device:TPU:0, one launch (start us, length us, event | category | flops | bytes accessed | tf_op | source)
XLA Modules:
  0.0 46.2 jit_solution(10593770794114718284)
XLA Ops:
  0.6 1.0 %first.1 = f32[88,512]{1,0:T(8,128)S(1)} custom-call(f32[6,4,1024]{2,1,0:T(4,128)} %bitcast.15, f32[24,768]{1,0:T(8,128)} %coarse_in.3, f32[4,32,512]{2,1,0:T(8,128)} %residual_in.3, f32[4,32,512]{2,1,0:T(8,128)} %old_in.3), custom_call_target="tpu_custom_call" | custom-call | tf_op jit(solution)/shard_map/first/pallas_call | solution.py:511
  1.6 2.4 %collective-permute-start = (f32[88,512]{1,0:T(8,128)S(1)}, f32[88,512]{1,0:T(8,128)S(1)}, u32[]{:S(2)}, u32[]{:S(2)}) collective-permute-start(f32[88,512]{1,0:T(8,128)S(1)} %first.1), channel_id=1, source_target_pairs={{0,1},{1,2},{2,3},{3,4},{4,5},{5,6},{6,7},{7,8},{8,9},{9,10},{10,1... | collective-permute-start | bytes 540680 | tf_op jit(solution)/shard_map/ppermute | solution.py:22
  4.0 2.9 %prepare.1 = (f32[4,8,512]{2,1,0:T(8,128)S(1)}, f32[24,128]{1,0:T(8,128)S(1)}, f32[8,2560]{1,0:T(8,128)S(1)}, f32[4,32,512]{2,1,0:T(8,128)S(1)}, f32[4,32,512]{2...) custom-call(s32[4,512]{1,0:T(4,128)} %matching_in.1, ...), custom_call_target="tpu_custom_call" | custom-call | tf_op jit(solution)/shard_map/prepare/pallas_call | solution.py:537
  6.9 1.2 %inner_middle.1 = (f32[2,64,1024]{2,1,0:T(8,128)S(1)}, bf16[2,80,1536]{2,1,0:T(8,128)(2,1)S(1)}, f32[2,96,1024]{2,1,0:T(8,128)S(1)}) custom-call(f32[24,128]{1,0:T(8,128)S(1)} %get-tuple-element.33.order.own_sums, s32[4,512]{1,0:T(4,128)S(1)} %get-tuple-element.35.matching, f32[4,8,1024]{2,1,0:T(8,128)S(1)} %get-tuple-element.36.padded, ...), custom_call_target="tpu_custom_call" | custom-call | tf_op jit(solution)/shard_map/inner_middle/pallas_call | solution.py:602
  8.1 0.0 collective-permute-done.from_before
  8.1 0.2 cross.1.order.own
  8.3 6.2 %collective-permute-start.1 = (f32[24,128]{1,0:T(8,128)S(1)}, f32[24,128]{1,0:T(8,128)S(1)}, u32[]{:S(2)}, u32[]{:S(2)}) collective-permute-start(f32[24,128]{1,0:T(8,128)S(1)} %cross.1.order.own), channel_id=1, source_target_pairs={{0,16},{1,17},{2,18},{3,19},{4,20},{5,21},{6,22},{7,23},{8,24},{9,... | collective-permute-start | bytes 36872 | tf_op jit(solution)/shard_map/ppermute | solution.py:27
  14.5 1.1 %inner_first.1 = (f32[1,64,1024]{2,1,0:T(8,128)S(1)}, bf16[1,80,1536]{2,1,0:T(8,128)(2,1)S(1)}, f32[96,512]{1,0:T(8,128)S(1)}, f32[56,512]{1,0:T(8,128)S(1)}, f32[40,512]{1,0:T(8,128)S(1)}) custom-call(f32[24,128]{1,0:T(8,128)S(1)} %cross.1.order.own, s32[4,512]{1,0:T(4,128)S(1)} %get-tuple-element.35.matching, f32[4,8,1024]{2,1,0:T(8,128)S(1)} %get-tuple-element.36.padded, ...), custom_call_target="tpu_custom_call" | custom-call | tf_op jit(solution)/shard_map/inner_first/pallas_call | solution.py:629
  15.6 0.5 %collective-permute-done.1.others_0_ = f32[24,128]{1,0:T(8,128)S(1)} collective-permute-done((f32[24,128]{1,0:T(8,128)S(1)}, f32[24,128]{1,0:T(8,128)S(1)}, u32[]{:S(2)}, u32[]{:S(2)}) %collective-permute-start.1) | collective-permute-done | bytes 12320 | tf_op jit(solution)/shard_map/ppermute | solution.py:27
  16.2 1.9 %collective-permute-start.2 = (f32[24,128]{1,0:T(8,128)S(1)}, f32[24,128]{1,0:T(8,128)S(1)}, u32[]{:S(2)}, u32[]{:S(2)}) collective-permute-start(f32[24,128]{1,0:T(8,128)S(1)} %merge.9.own), channel_id=1, source_target_pairs={{0,8},{1,9},{2,10},{3,11},{4,12},{5,13},{6,14},{7,15},{8,0},{9,1},... | collective-permute-start | bytes 36872 | tf_op jit(solution)/shard_map/ppermute | solution.py:27
  18.1 1.3 %collective-permute-start.13 = (f32[56,512]{1,0:T(8,128)S(1)}, f32[56,512]{1,0:T(8,128)S(1)}, u32[]{:S(2)}, u32[]{:S(2)}) collective-permute-start(f32[56,512]{1,0:T(8,128)S(1)} %get-tuple-element.44.others_1_), channel_id=1, source_target_pairs={{1,0},{2,1},{3,2},{4,3},{5,4},{6,5},{7,6},{8,7},{9,8},{10,9},{11,1... | collective-permute-start | bytes 344072 | tf_op jit(solution)/shard_map/ppermute | solution.py:22
  19.4 0.5 %collective-permute-done.2.others_0_ = f32[24,128]{1,0:T(8,128)S(1)} collective-permute-done((f32[24,128]{1,0:T(8,128)S(1)}, f32[24,128]{1,0:T(8,128)S(1)}, u32[]{:S(2)}, u32[]{:S(2)}) %collective-permute-start.2) | collective-permute-done | bytes 12320 | tf_op jit(solution)/shard_map/ppermute | solution.py:27
  19.9 1.1 %collective-permute-start.3 = (f32[1,24,128]{2,1,0:T(8,128)S(1)}, f32[1,24,128]{2,1,0:T(8,128)S(1)}, u32[]{:S(2)}, u32[]{:S(2)}) collective-permute-start(f32[1,24,128]{2,1,0:T(8,128)S(1)} %bitcast.12), channel_id=1, source_target_pairs={{0,4},{1,5},{2,6},{3,7},{4,0},{5,1},{6,2},{7,3},{8,12},{9,13},{10,... | collective-permute-start | bytes 36872 | tf_op jit(solution)/shard_map/ppermute | solution.py:27
  20.9 1.3 %collective-permute-start.6 = (f32[8,2560]{1,0:T(8,128)S(1)}, f32[8,2560]{1,0:T(8,128)S(1)}, u32[]{:S(2)}, u32[]{:S(2)}) collective-permute-start(f32[8,2560]{1,0:T(8,128)S(1)} %get-tuple-element.45), channel_id=1, source_target_pairs={{1,0},{2,1},{3,2},{4,3},{5,4},{6,5},{7,6},{8,7},{9,8},{10,9},{11,1... | collective-permute-start | bytes 245768 | tf_op jit(solution)/shard_map/ppermute | solution.py:22
  22.2 1.3 %collective-permute-done.3.others_0_ = f32[1,24,128]{2,1,0:T(8,128)S(1)} collective-permute-done((f32[1,24,128]{2,1,0:T(8,128)S(1)}, f32[1,24,128]{2,1,0:T(8,128)S(1)}, u32[]{:S(2)}, u32[]{:S(2)}) %collective-permute-start.3) | collective-permute-done | bytes 12320 | tf_op jit(solution)/shard_map/ppermute | solution.py:27
  23.6 1.0 %collective-permute-start.4 = (f32[2,24,128]{2,1,0:T(8,128)S(1)}, f32[2,24,128]{2,1,0:T(8,128)S(1)}, u32[]{:S(2)}, u32[]{:S(2)}) collective-permute-start(f32[2,24,128]{2,1,0:T(8,128)S(1)} %bitcast.10), channel_id=1, source_target_pairs={{0,2},{1,3},{2,0},{3,1},{4,6},{5,7},{6,4},{7,5},{8,10},{9,11},{10,... | collective-permute-start | bytes 73736 | tf_op jit(solution)/shard_map/ppermute | solution.py:27
  24.6 1.3 %collective-permute-start.14 = (f32[40,512]{1,0:T(8,128)S(1)}, f32[40,512]{1,0:T(8,128)S(1)}, u32[]{:S(2)}, u32[]{:S(2)}) collective-permute-start(f32[40,512]{1,0:T(8,128)S(1)} %get-tuple-element.59), channel_id=1, source_target_pairs={{1,0},{2,1},{3,2},{4,3},{5,4},{6,5},{7,6},{8,7},{9,8},{10,9},{11,1... | collective-permute-start | bytes 245768 | tf_op jit(solution)/shard_map/ppermute | solution.py:22
  25.9 1.5 %collective-permute-done.4.others_0_ = f32[2,24,128]{2,1,0:T(8,128)S(1)} collective-permute-done((f32[2,24,128]{2,1,0:T(8,128)S(1)}, f32[2,24,128]{2,1,0:T(8,128)S(1)}, u32[]{:S(2)}, u32[]{:S(2)}) %collective-permute-start.4) | collective-permute-done | bytes 24608 | tf_op jit(solution)/shard_map/ppermute | solution.py:27
  27.4 0.0 collective-permute-start.5
  27.4 0.0 collective-permute-done.6.others_0_.from_next
  27.4 0.8 %inner_last.1 = (f32[1,64,1024]{2,1,0:T(8,128)S(1)}, bf16[1,80,1536]{2,1,0:T(8,128)(2,1)S(1)}, f32[1,96,1024]{2,1,0:T(8,128)S(1)}) custom-call(f32[4,24,128]{2,1,0:T(8,128)S(1)} %bitcast.7, s32[4,512]{1,0:T(4,128)S(1)} %get-tuple-element.35.matching, f32[4,8,1024]{2,1,0:T(8,128)S(1)} %get-tuple-element.36.padded, ...), custom_call_target="tpu_custom_call" | custom-call | tf_op jit(solution)/shard_map/inner_last/pallas_call | solution.py:602
  28.2 0.5 collective-permute-done.5.others_0_
  28.6 0.8 %combine.1 = (f32[4,32,512]{2,1,0:T(8,128)S(1)}, f32[56,32]{1,0:T(8,128)S(1)}, f32[8,128]{1,0:T(8,128)S(1)}) custom-call(f32[8,24,128]{2,1,0:T(8,128)S(1)} %bitcast.9, f32[88,512]{1,0:T(8,128)S(1)} %collective-permute-done.from_before, f32[32,768]{1,0:T(8,128)S(1)} %get-tuple-element.47.coarse_rows, ...), custom_call_target="tpu_custom_call" | custom-call | tf_op jit(solution)/shard_map/combine/pallas_call | solution.py:656
  29.4 1.9 %collective-permute-start.9 = (f32[8,128]{1,0:T(8,128)S(1)}, f32[8,128]{1,0:T(8,128)S(1)}, u32[]{:S(2)}, u32[]{:S(2)}) collective-permute-start(f32[8,128]{1,0:T(8,128)S(1)} %get-tuple-element.54.order.own), channel_id=1, source_target_pairs={{0,6},{1,7},{2,4},{3,5},{4,2},{5,3},{6,0},{7,1},{8,14},{9,15},{10,... | collective-permute-start | bytes 12296 | tf_op jit(solution)/shard_map/ppermute | solution.py:27
  31.3 0.8 %collective-permute-start.8 = (f32[8,128]{1,0:T(8,128)S(1)}, f32[8,128]{1,0:T(8,128)S(1)}, u32[]{:S(2)}, u32[]{:S(2)}) collective-permute-start(f32[8,128]{1,0:T(8,128)S(1)} %get-tuple-element.54.order.own), channel_id=1, source_target_pairs={{0,4},{1,5},{2,6},{3,7},{4,0},{5,1},{6,2},{7,3},{8,12},{9,13},{10,... | collective-permute-start | bytes 12296 | tf_op jit(solution)/shard_map/ppermute | solution.py:27
  32.1 0.9 %collective-permute-start.7 = (f32[8,128]{1,0:T(8,128)S(1)}, f32[8,128]{1,0:T(8,128)S(1)}, u32[]{:S(2)}, u32[]{:S(2)}) collective-permute-start(f32[8,128]{1,0:T(8,128)S(1)} %get-tuple-element.54.order.own), channel_id=1, source_target_pairs={{0,2},{1,3},{2,0},{3,1},{4,6},{5,7},{6,4},{7,5},{8,10},{9,11},{10,... | collective-permute-start | bytes 12296 | tf_op jit(solution)/shard_map/ppermute | solution.py:27
  33.0 0.0 copy-start
  33.0 0.0 copy-start.1
  33.0 1.8 %outer.1 = (f32[4,32,512]{2,1,0:T(8,128)S(1)}, f32[4,32,512]{2,1,0:T(8,128)S(1)}) custom-call(f32[8,128]{1,0:T(8,128)S(1)} %get-tuple-element.54.order.own, s32[4,512]{1,0:T(4,128)S(1)} %get-tuple-element.35.matching, f32[2,96,1024]{2,1,0:T(8,128)S(1)} %get-tuple-element.43.order.whole_middle, f32[1,96,1024]{2,1,0:T(8,128)S(1)} %get-tuple-element.46.others_1_.whole_last, ...), custom_call_target="tpu_custom_call" | custom-call | tf_op jit(solution)/shard_map/outer/pallas_call | solution.py:681
  34.8 0.0 collective-permute-done.9.others_2_
  34.8 0.1 collective-permute-done.8.others_1_
  34.9 0.8 %collective-permute-done.7.others_0_ = f32[8,128]{1,0:T(8,128)S(1)} collective-permute-done((f32[8,128]{1,0:T(8,128)S(1)}, f32[8,128]{1,0:T(8,128)S(1)}, u32[]{:S(2)}, u32[]{:S(2)}) %collective-permute-start.7) | collective-permute-done | bytes 4128 | tf_op jit(solution)/shard_map/ppermute | solution.py:27
  35.7 2.7 %collective-permute-start.10 = (f32[8,128]{1,0:T(8,128)S(1)}, f32[8,128]{1,0:T(8,128)S(1)}, u32[]{:S(2)}, u32[]{:S(2)}) collective-permute-start(f32[8,128]{1,0:T(8,128)S(1)} %merge.14.own), channel_id=1, source_target_pairs={{0,16},{1,17},{2,18},{3,19},{4,20},{5,21},{6,22},{7,23},{8,24},{9,... | collective-permute-start | bytes 12296 | tf_op jit(solution)/shard_map/ppermute | solution.py:27
  38.4 1.8 %collective-permute-done.10.others_0_ = f32[8,128]{1,0:T(8,128)S(1)} collective-permute-done((f32[8,128]{1,0:T(8,128)S(1)}, f32[8,128]{1,0:T(8,128)S(1)}, u32[]{:S(2)}, u32[]{:S(2)}) %collective-permute-start.10) | collective-permute-done | bytes 4128 | tf_op jit(solution)/shard_map/ppermute | solution.py:27
  40.2 1.5 %collective-permute-start.11 = (f32[8,128]{1,0:T(8,128)S(1)}, f32[8,128]{1,0:T(8,128)S(1)}, u32[]{:S(2)}, u32[]{:S(2)}) collective-permute-start(f32[8,128]{1,0:T(8,128)S(1)} %merge.15.own), channel_id=1, source_target_pairs={{0,8},{1,9},{2,10},{3,11},{4,12},{5,13},{6,14},{7,15},{8,0},{9,1},... | collective-permute-start | bytes 12296 | tf_op jit(solution)/shard_map/ppermute | solution.py:27
  41.7 2.1 %collective-permute-done.11.others_0_ = f32[8,128]{1,0:T(8,128)S(1)} collective-permute-done((f32[8,128]{1,0:T(8,128)S(1)}, f32[8,128]{1,0:T(8,128)S(1)}, u32[]{:S(2)}, u32[]{:S(2)}) %collective-permute-start.11) | collective-permute-done | bytes 4128 | tf_op jit(solution)/shard_map/ppermute | solution.py:27
  43.8 0.0 collective-permute-start.12
  43.8 0.0 collective-permute-done.14.received_rest
  43.8 0.0 collective-permute-done.13.received_first
  43.8 0.2 settle.1
  44.0 1.0 %collective-permute-done.12.others_0_ = f32[8,128]{1,0:T(8,128)S(1)} collective-permute-done((f32[8,128]{1,0:T(8,128)S(1)}, f32[8,128]{1,0:T(8,128)S(1)}, u32[]{:S(2)}, u32[]{:S(2)}) %collective-permute-start.12) | collective-permute-done | bytes 4128 | tf_op jit(solution)/shard_map/ppermute | solution.py:27
  45.0 0.0 copy-done
  45.0 0.0 copy-done.1
  45.0 1.2 %finish.1 = (f32[4,32,512]{2,1,0:T(8,128)}, f32[4,32,512]{2,1,0:T(8,128)}, f32[4,32,512]{2,1,0:T(8,128)}) custom-call(f32[8,128]{1,0:T(8,128)S(1)} %merge.17.sums, f32[1,32]{1,0:T(1,128)S(1)} %bitcast.14, f32[4,32,512]{2,1,0:T(8,128)S(1)} %copy-done, f32[4,32,512]{2,1,0:T(8,128)S(1)} %get-tuple-element.37.masked, ...), custom_call_target="tpu_custom_call" | custom-call | tf_op jit(solution)/shard_map/finish/pallas_call | solution.py:705
  (9 shorter events, 0.0 us)
Async XLA Ops:
  1.6 6.5 %collective-permute-start = (f32[88,512]{1,0:T(8,128)S(1)}, f32[88,512]{1,0:T(8,128)S(1)}, u32[]{:S(2)}, u32[]{:S(2)}) collective-permute-start(f32[88,512]{1,0:T(8,128)S(1)} %first.1), channel_id=1, source_target_pairs={{0,1},{1,2},{2,3},{3,4},{4,5},{5,6},{6,7},{7,8},{8,9},{9,10},{10,1... | collective-permute-start | bytes 540680 | tf_op jit(solution)/shard_map/ppermute | solution.py:22
  8.3 7.8 %collective-permute-start.1 = (f32[24,128]{1,0:T(8,128)S(1)}, f32[24,128]{1,0:T(8,128)S(1)}, u32[]{:S(2)}, u32[]{:S(2)}) collective-permute-start(f32[24,128]{1,0:T(8,128)S(1)} %cross.1.order.own), channel_id=1, source_target_pairs={{0,16},{1,17},{2,18},{3,19},{4,20},{5,21},{6,22},{7,23},{8,24},{9,... | collective-permute-start | bytes 36872 | tf_op jit(solution)/shard_map/ppermute | solution.py:27
  16.2 3.7 %collective-permute-start.2 = (f32[24,128]{1,0:T(8,128)S(1)}, f32[24,128]{1,0:T(8,128)S(1)}, u32[]{:S(2)}, u32[]{:S(2)}) collective-permute-start(f32[24,128]{1,0:T(8,128)S(1)} %merge.9.own), channel_id=1, source_target_pairs={{0,8},{1,9},{2,10},{3,11},{4,12},{5,13},{6,14},{7,15},{8,0},{9,1},... | collective-permute-start | bytes 36872 | tf_op jit(solution)/shard_map/ppermute | solution.py:27
  18.1 25.8 %collective-permute-start.13 = (f32[56,512]{1,0:T(8,128)S(1)}, f32[56,512]{1,0:T(8,128)S(1)}, u32[]{:S(2)}, u32[]{:S(2)}) collective-permute-start(f32[56,512]{1,0:T(8,128)S(1)} %get-tuple-element.44.others_1_), channel_id=1, source_target_pairs={{1,0},{2,1},{3,2},{4,3},{5,4},{6,5},{7,6},{8,7},{9,8},{10,9},{11,1... | collective-permute-start | bytes 344072 | tf_op jit(solution)/shard_map/ppermute | solution.py:22
  19.9 3.7 %collective-permute-start.3 = (f32[1,24,128]{2,1,0:T(8,128)S(1)}, f32[1,24,128]{2,1,0:T(8,128)S(1)}, u32[]{:S(2)}, u32[]{:S(2)}) collective-permute-start(f32[1,24,128]{2,1,0:T(8,128)S(1)} %bitcast.12), channel_id=1, source_target_pairs={{0,4},{1,5},{2,6},{3,7},{4,0},{5,1},{6,2},{7,3},{8,12},{9,13},{10,... | collective-permute-start | bytes 36872 | tf_op jit(solution)/shard_map/ppermute | solution.py:27
  20.9 6.5 %collective-permute-start.6 = (f32[8,2560]{1,0:T(8,128)S(1)}, f32[8,2560]{1,0:T(8,128)S(1)}, u32[]{:S(2)}, u32[]{:S(2)}) collective-permute-start(f32[8,2560]{1,0:T(8,128)S(1)} %get-tuple-element.45), channel_id=1, source_target_pairs={{1,0},{2,1},{3,2},{4,3},{5,4},{6,5},{7,6},{8,7},{9,8},{10,9},{11,1... | collective-permute-start | bytes 245768 | tf_op jit(solution)/shard_map/ppermute | solution.py:22
  23.6 3.8 %collective-permute-start.4 = (f32[2,24,128]{2,1,0:T(8,128)S(1)}, f32[2,24,128]{2,1,0:T(8,128)S(1)}, u32[]{:S(2)}, u32[]{:S(2)}) collective-permute-start(f32[2,24,128]{2,1,0:T(8,128)S(1)} %bitcast.10), channel_id=1, source_target_pairs={{0,2},{1,3},{2,0},{3,1},{4,6},{5,7},{6,4},{7,5},{8,10},{9,11},{10,... | collective-permute-start | bytes 73736 | tf_op jit(solution)/shard_map/ppermute | solution.py:27
  24.6 19.3 %collective-permute-start.14 = (f32[40,512]{1,0:T(8,128)S(1)}, f32[40,512]{1,0:T(8,128)S(1)}, u32[]{:S(2)}, u32[]{:S(2)}) collective-permute-start(f32[40,512]{1,0:T(8,128)S(1)} %get-tuple-element.59), channel_id=1, source_target_pairs={{1,0},{2,1},{3,2},{4,3},{5,4},{6,5},{7,6},{8,7},{9,8},{10,9},{11,1... | collective-permute-start | bytes 245768 | tf_op jit(solution)/shard_map/ppermute | solution.py:22
  27.4 1.2 %collective-permute-start.5 = (f32[4,24,128]{2,1,0:T(8,128)S(1)}, f32[4,24,128]{2,1,0:T(8,128)S(1)}, u32[]{:S(2)}, u32[]{:S(2)}) collective-permute-start(f32[4,24,128]{2,1,0:T(8,128)S(1)} %bitcast.6), channel_id=1, source_target_pairs={{0,1},{1,0},{2,3},{3,2},{4,5},{5,4},{6,7},{7,6},{8,9},{9,8},{10,11... | collective-permute-start | bytes 147464 | tf_op jit(solution)/shard_map/ppermute | solution.py:27
  29.4 5.4 %collective-permute-start.9 = (f32[8,128]{1,0:T(8,128)S(1)}, f32[8,128]{1,0:T(8,128)S(1)}, u32[]{:S(2)}, u32[]{:S(2)}) collective-permute-start(f32[8,128]{1,0:T(8,128)S(1)} %get-tuple-element.54.order.own), channel_id=1, source_target_pairs={{0,6},{1,7},{2,4},{3,5},{4,2},{5,3},{6,0},{7,1},{8,14},{9,15},{10,... | collective-permute-start | bytes 12296 | tf_op jit(solution)/shard_map/ppermute | solution.py:27
  31.3 3.6 %collective-permute-start.8 = (f32[8,128]{1,0:T(8,128)S(1)}, f32[8,128]{1,0:T(8,128)S(1)}, u32[]{:S(2)}, u32[]{:S(2)}) collective-permute-start(f32[8,128]{1,0:T(8,128)S(1)} %get-tuple-element.54.order.own), channel_id=1, source_target_pairs={{0,4},{1,5},{2,6},{3,7},{4,0},{5,1},{6,2},{7,3},{8,12},{9,13},{10,... | collective-permute-start | bytes 12296 | tf_op jit(solution)/shard_map/ppermute | solution.py:27
  32.1 3.6 %collective-permute-start.7 = (f32[8,128]{1,0:T(8,128)S(1)}, f32[8,128]{1,0:T(8,128)S(1)}, u32[]{:S(2)}, u32[]{:S(2)}) collective-permute-start(f32[8,128]{1,0:T(8,128)S(1)} %get-tuple-element.54.order.own), channel_id=1, source_target_pairs={{0,2},{1,3},{2,0},{3,1},{4,6},{5,7},{6,4},{7,5},{8,10},{9,11},{10,... | collective-permute-start | bytes 12296 | tf_op jit(solution)/shard_map/ppermute | solution.py:27
  33.0 12.0 %copy-start = (f32[4,32,512]{2,1,0:T(8,128)S(1)}, f32[4,32,512]{2,1,0:T(8,128)}, u32[]{:S(2)}) copy-start(f32[4,32,512]{2,1,0:T(8,128)} %multipliers.1) | copy-start | bytes 786436
  33.0 12.0 %copy-start.1 = (f32[32]{0:T(128)S(1)}, f32[32]{0:T(128)}, u32[]{:S(2)}) copy-start(f32[32]{0:T(128)} %param.11) | copy-start | bytes 388
  35.7 4.5 %collective-permute-start.10 = (f32[8,128]{1,0:T(8,128)S(1)}, f32[8,128]{1,0:T(8,128)S(1)}, u32[]{:S(2)}, u32[]{:S(2)}) collective-permute-start(f32[8,128]{1,0:T(8,128)S(1)} %merge.14.own), channel_id=1, source_target_pairs={{0,16},{1,17},{2,18},{3,19},{4,20},{5,21},{6,22},{7,23},{8,24},{9,... | collective-permute-start | bytes 12296 | tf_op jit(solution)/shard_map/ppermute | solution.py:27
  40.2 3.6 %collective-permute-start.11 = (f32[8,128]{1,0:T(8,128)S(1)}, f32[8,128]{1,0:T(8,128)S(1)}, u32[]{:S(2)}, u32[]{:S(2)}) collective-permute-start(f32[8,128]{1,0:T(8,128)S(1)} %merge.15.own), channel_id=1, source_target_pairs={{0,8},{1,9},{2,10},{3,11},{4,12},{5,13},{6,14},{7,15},{8,0},{9,1},... | collective-permute-start | bytes 12296 | tf_op jit(solution)/shard_map/ppermute | solution.py:27
  43.8 1.2 %collective-permute-start.12 = (f32[8,128]{1,0:T(8,128)S(1)}, f32[8,128]{1,0:T(8,128)S(1)}, u32[]{:S(2)}, u32[]{:S(2)}) collective-permute-start(f32[8,128]{1,0:T(8,128)S(1)} %merge.16.order.own), channel_id=1, source_target_pairs={{0,1},{1,0},{2,3},{3,2},{4,5},{5,4},{6,7},{7,6},{8,9},{9,8},{10,11... | collective-permute-start | bytes 12296 | tf_op jit(solution)/shard_map/ppermute | solution.py:27

commit v6 on v5

--- a/solution.py
+++ b/solution.py
@@ -597,6 +597,8 @@
         return rounds
 
     rounds = rounds_of(2)
+    lane_rounds = [one for one in rounds if one[0] >= share]
+    rounds = lane_rounds[::-1] + rounds[len(lane_rounds) :]
 
     def inner(subs, order, *halos):
         return pl.pallas_call(

time: 46.5 us -> 46.6 us (level)
  no operation moved by 1% of the time
where the time goes in v6:
time: 46.6 us; the launch traced here: 46.3 us
  starting transfers between devices  23.9 us (51%)
  Pallas kernels  11.2 us (24%)
  waiting for transfers between devices  10.4 us (22%)
  between operations  0.76 us (2%)
    ppermute x11, starting transfers between devices, swapped(): return lax.ppermute(block, AXES, route)  17.7 us
    ppermute x11, waiting for transfers between devices, swapped(): return lax.ppermute(block, AXES, route)  10.4 us
    ppermute x4, starting transfers between devices, shifted(): return lax.ppermute(block, AXES, route)  6.21 us
    pallas_call x1, Pallas kernels, on_device(): pl.pallas_call(functools.partial(prepare_kernel, copies, share), out_shap...  2.93 us
    pallas_call x2, Pallas kernels, inner(): pl.pallas_call(functools.partial(later_kernel, subs), out_shape=(shape((l...  1.94 us
    pallas_call x1, Pallas kernels, on_device(): pl.pallas_call(outer_kernel, out_shape=(shape((count, cases, half), f32),...  1.82 us
    pallas_call x1, Pallas kernels, on_device(): pl.pallas_call(finish_kernel, out_shape=(shape((count, cases, half), f32)...  1.22 us
    pallas_call x1, Pallas kernels, on_device(): pl.pallas_call(start_kernel, out_shape=(shape((1, q, full), f32), shape((...  1.14 us
  transfers between devices with their start and end apart: 15, of which 10 were waited for; matrix products, arithmetic and copies ran while one was open for 0% of the time, Pallas kernels for 19%

profile of v6, /device:TPU:0, one launch (start us, length us, event | category | flops | bytes accessed | tf_op | source)
XLA Modules:
  0.0 46.3 jit_solution(12744168786471787445)
XLA Ops:
  0.6 1.0 %first.1 = f32[88,512]{1,0:T(8,128)S(1)} custom-call(f32[6,4,1024]{2,1,0:T(4,128)} %bitcast.15, f32[24,768]{1,0:T(8,128)} %coarse_in.3, f32[4,32,512]{2,1,0:T(8,128)} %residual_in.3, f32[4,32,512]{2,1,0:T(8,128)} %old_in.3), custom_call_target="tpu_custom_call" | custom-call | tf_op jit(solution)/shard_map/first/pallas_call | solution.py:511
  1.6 2.4 %collective-permute-start = (f32[88,512]{1,0:T(8,128)S(1)}, f32[88,512]{1,0:T(8,128)S(1)}, u32[]{:S(2)}, u32[]{:S(2)}) collective-permute-start(f32[88,512]{1,0:T(8,128)S(1)} %first.1), channel_id=1, source_target_pairs={{0,1},{1,2},{2,3},{3,4},{4,5},{5,6},{6,7},{7,8},{8,9},{9,10},{10,1... | collective-permute-start | bytes 540680 | tf_op jit(solution)/shard_map/ppermute | solution.py:22
  4.0 2.9 %prepare.1 = (f32[4,8,512]{2,1,0:T(8,128)S(1)}, f32[24,128]{1,0:T(8,128)S(1)}, f32[8,2560]{1,0:T(8,128)S(1)}, f32[4,32,512]{2,1,0:T(8,128)S(1)}, f32[4,32,512]{2...) custom-call(s32[4,512]{1,0:T(4,128)} %matching_in.1, ...), custom_call_target="tpu_custom_call" | custom-call | tf_op jit(solution)/shard_map/prepare/pallas_call | solution.py:537
  6.9 1.2 %inner_middle.1 = (f32[2,64,1024]{2,1,0:T(8,128)S(1)}, bf16[2,80,1536]{2,1,0:T(8,128)(2,1)S(1)}, f32[2,96,1024]{2,1,0:T(8,128)S(1)}) custom-call(f32[24,128]{1,0:T(8,128)S(1)} %get-tuple-element.33.order.own_sums, s32[4,512]{1,0:T(4,128)S(1)} %get-tuple-element.35.matching, f32[4,8,1024]{2,1,0:T(8,128)S(1)} %get-tuple-element.36.padded, ...), custom_call_target="tpu_custom_call" | custom-call | tf_op jit(solution)/shard_map/inner_middle/pallas_call | solution.py:604
  8.1 0.0 collective-permute-done.from_before
  8.1 0.2 cross.1.order.own
  8.3 5.1 %collective-permute-start.1 = (f32[24,128]{1,0:T(8,128)S(1)}, f32[24,128]{1,0:T(8,128)S(1)}, u32[]{:S(2)}, u32[]{:S(2)}) collective-permute-start(f32[24,128]{1,0:T(8,128)S(1)} %cross.1.order.own), channel_id=1, source_target_pairs={{0,8},{1,9},{2,10},{3,11},{4,12},{5,13},{6,14},{7,15},{8,0},{9,1},... | collective-permute-start | bytes 36872 | tf_op jit(solution)/shard_map/ppermute | solution.py:27
  13.5 1.1 %inner_first.1 = (f32[1,64,1024]{2,1,0:T(8,128)S(1)}, bf16[1,80,1536]{2,1,0:T(8,128)(2,1)S(1)}, f32[96,512]{1,0:T(8,128)S(1)}, f32[56,512]{1,0:T(8,128)S(1)}, f32[40,512]{1,0:T(8,128)S(1)}) custom-call(f32[24,128]{1,0:T(8,128)S(1)} %cross.1.order.own, s32[4,512]{1,0:T(4,128)S(1)} %get-tuple-element.35.matching, f32[4,8,1024]{2,1,0:T(8,128)S(1)} %get-tuple-element.36.padded, ...), custom_call_target="tpu_custom_call" | custom-call | tf_op jit(solution)/shard_map/inner_first/pallas_call | solution.py:631
  14.6 0.5 %collective-permute-done.1.others_0_ = f32[24,128]{1,0:T(8,128)S(1)} collective-permute-done((f32[24,128]{1,0:T(8,128)S(1)}, f32[24,128]{1,0:T(8,128)S(1)}, u32[]{:S(2)}, u32[]{:S(2)}) %collective-permute-start.1) | collective-permute-done | bytes 12320 | tf_op jit(solution)/shard_map/ppermute | solution.py:27
  15.2 3.0 %collective-permute-start.2 = (f32[24,128]{1,0:T(8,128)S(1)}, f32[24,128]{1,0:T(8,128)S(1)}, u32[]{:S(2)}, u32[]{:S(2)}) collective-permute-start(f32[24,128]{1,0:T(8,128)S(1)} %merge.9.own), channel_id=1, source_target_pairs={{0,16},{1,17},{2,18},{3,19},{4,20},{5,21},{6,22},{7,23},{8,24},{9,... | collective-permute-start | bytes 36872 | tf_op jit(solution)/shard_map/ppermute | solution.py:27
  18.2 1.3 %collective-permute-start.13 = (f32[56,512]{1,0:T(8,128)S(1)}, f32[56,512]{1,0:T(8,128)S(1)}, u32[]{:S(2)}, u32[]{:S(2)}) collective-permute-start(f32[56,512]{1,0:T(8,128)S(1)} %get-tuple-element.44.others_1_), channel_id=1, source_target_pairs={{1,0},{2,1},{3,2},{4,3},{5,4},{6,5},{7,6},{8,7},{9,8},{10,9},{11,1... | collective-permute-start | bytes 344072 | tf_op jit(solution)/shard_map/ppermute | solution.py:22
  19.5 0.4 collective-permute-done.2.others_0_
  19.9 1.0 %collective-permute-start.3 = (f32[1,24,128]{2,1,0:T(8,128)S(1)}, f32[1,24,128]{2,1,0:T(8,128)S(1)}, u32[]{:S(2)}, u32[]{:S(2)}) collective-permute-start(f32[1,24,128]{2,1,0:T(8,128)S(1)} %bitcast.12), channel_id=1, source_target_pairs={{0,4},{1,5},{2,6},{3,7},{4,0},{5,1},{6,2},{7,3},{8,12},{9,13},{10,... | collective-permute-start | bytes 36872 | tf_op jit(solution)/shard_map/ppermute | solution.py:27
  20.8 1.3 %collective-permute-start.6 = (f32[8,2560]{1,0:T(8,128)S(1)}, f32[8,2560]{1,0:T(8,128)S(1)}, u32[]{:S(2)}, u32[]{:S(2)}) collective-permute-start(f32[8,2560]{1,0:T(8,128)S(1)} %get-tuple-element.45), channel_id=1, source_target_pairs={{1,0},{2,1},{3,2},{4,3},{5,4},{6,5},{7,6},{8,7},{9,8},{10,9},{11,1... | collective-permute-start | bytes 245768 | tf_op jit(solution)/shard_map/ppermute | solution.py:22
  22.1 1.5 %collective-permute-done.3.others_0_ = f32[1,24,128]{2,1,0:T(8,128)S(1)} collective-permute-done((f32[1,24,128]{2,1,0:T(8,128)S(1)}, f32[1,24,128]{2,1,0:T(8,128)S(1)}, u32[]{:S(2)}, u32[]{:S(2)}) %collective-permute-start.3) | collective-permute-done | bytes 12320 | tf_op jit(solution)/shard_map/ppermute | solution.py:27
  23.6 1.1 %collective-permute-start.4 = (f32[2,24,128]{2,1,0:T(8,128)S(1)}, f32[2,24,128]{2,1,0:T(8,128)S(1)}, u32[]{:S(2)}, u32[]{:S(2)}) collective-permute-start(f32[2,24,128]{2,1,0:T(8,128)S(1)} %bitcast.10), channel_id=1, source_target_pairs={{0,2},{1,3},{2,0},{3,1},{4,6},{5,7},{6,4},{7,5},{8,10},{9,11},{10,... | collective-permute-start | bytes 73736 | tf_op jit(solution)/shard_map/ppermute | solution.py:27
  24.7 1.3 %collective-permute-start.14 = (f32[40,512]{1,0:T(8,128)S(1)}, f32[40,512]{1,0:T(8,128)S(1)}, u32[]{:S(2)}, u32[]{:S(2)}) collective-permute-start(f32[40,512]{1,0:T(8,128)S(1)} %get-tuple-element.59), channel_id=1, source_target_pairs={{1,0},{2,1},{3,2},{4,3},{5,4},{6,5},{7,6},{8,7},{9,8},{10,9},{11,1... | collective-permute-start | bytes 245768 | tf_op jit(solution)/shard_map/ppermute | solution.py:22
  26.0 1.4 %collective-permute-done.4.others_0_ = f32[2,24,128]{2,1,0:T(8,128)S(1)} collective-permute-done((f32[2,24,128]{2,1,0:T(8,128)S(1)}, f32[2,24,128]{2,1,0:T(8,128)S(1)}, u32[]{:S(2)}, u32[]{:S(2)}) %collective-permute-start.4) | collective-permute-done | bytes 24608 | tf_op jit(solution)/shard_map/ppermute | solution.py:27
  27.4 0.0 collective-permute-start.5
  27.4 0.0 collective-permute-done.6.others_0_.from_next
  27.4 0.8 %inner_last.1 = (f32[1,64,1024]{2,1,0:T(8,128)S(1)}, bf16[1,80,1536]{2,1,0:T(8,128)(2,1)S(1)}, f32[1,96,1024]{2,1,0:T(8,128)S(1)}) custom-call(f32[4,24,128]{2,1,0:T(8,128)S(1)} %bitcast.7, s32[4,512]{1,0:T(4,128)S(1)} %get-tuple-element.35.matching, f32[4,8,1024]{2,1,0:T(8,128)S(1)} %get-tuple-element.36.padded, ...), custom_call_target="tpu_custom_call" | custom-call | tf_op jit(solution)/shard_map/inner_last/pallas_call | solution.py:604
  28.2 0.5 collective-permute-done.5.others_0_
  28.6 0.8 %combine.1 = (f32[4,32,512]{2,1,0:T(8,128)S(1)}, f32[56,32]{1,0:T(8,128)S(1)}, f32[8,128]{1,0:T(8,128)S(1)}) custom-call(f32[8,24,128]{2,1,0:T(8,128)S(1)} %bitcast.9, f32[88,512]{1,0:T(8,128)S(1)} %collective-permute-done.from_before, f32[32,768]{1,0:T(8,128)S(1)} %get-tuple-element.47.coarse_rows, ...), custom_call_target="tpu_custom_call" | custom-call | tf_op jit(solution)/shard_map/combine/pallas_call | solution.py:658
  29.4 2.0 %collective-permute-start.9 = (f32[8,128]{1,0:T(8,128)S(1)}, f32[8,128]{1,0:T(8,128)S(1)}, u32[]{:S(2)}, u32[]{:S(2)}) collective-permute-start(f32[8,128]{1,0:T(8,128)S(1)} %get-tuple-element.54.order.own), channel_id=1, source_target_pairs={{0,6},{1,7},{2,4},{3,5},{4,2},{5,3},{6,0},{7,1},{8,14},{9,15},{10,... | collective-permute-start | bytes 12296 | tf_op jit(solution)/shard_map/ppermute | solution.py:27
  31.4 0.8 %collective-permute-start.8 = (f32[8,128]{1,0:T(8,128)S(1)}, f32[8,128]{1,0:T(8,128)S(1)}, u32[]{:S(2)}, u32[]{:S(2)}) collective-permute-start(f32[8,128]{1,0:T(8,128)S(1)} %get-tuple-element.54.order.own), channel_id=1, source_target_pairs={{0,4},{1,5},{2,6},{3,7},{4,0},{5,1},{6,2},{7,3},{8,12},{9,13},{10,... | collective-permute-start | bytes 12296 | tf_op jit(solution)/shard_map/ppermute | solution.py:27
  32.2 0.8 %collective-permute-start.7 = (f32[8,128]{1,0:T(8,128)S(1)}, f32[8,128]{1,0:T(8,128)S(1)}, u32[]{:S(2)}, u32[]{:S(2)}) collective-permute-start(f32[8,128]{1,0:T(8,128)S(1)} %get-tuple-element.54.order.own), channel_id=1, source_target_pairs={{0,2},{1,3},{2,0},{3,1},{4,6},{5,7},{6,4},{7,5},{8,10},{9,11},{10,... | collective-permute-start | bytes 12296 | tf_op jit(solution)/shard_map/ppermute | solution.py:27
  33.0 0.0 copy-start
  33.0 0.0 copy-start.1
  33.0 1.8 %outer.1 = (f32[4,32,512]{2,1,0:T(8,128)S(1)}, f32[4,32,512]{2,1,0:T(8,128)S(1)}) custom-call(f32[8,128]{1,0:T(8,128)S(1)} %get-tuple-element.54.order.own, s32[4,512]{1,0:T(4,128)S(1)} %get-tuple-element.35.matching, f32[2,96,1024]{2,1,0:T(8,128)S(1)} %get-tuple-element.43.order.whole_middle, f32[1,96,1024]{2,1,0:T(8,128)S(1)} %get-tuple-element.46.others_1_.whole_last, ...), custom_call_target="tpu_custom_call" | custom-call | tf_op jit(solution)/shard_map/outer/pallas_call | solution.py:683
  34.8 0.0 collective-permute-done.9.others_2_
  34.8 0.2 collective-permute-done.8.others_1_
  35.0 0.8 %collective-permute-done.7.others_0_ = f32[8,128]{1,0:T(8,128)S(1)} collective-permute-done((f32[8,128]{1,0:T(8,128)S(1)}, f32[8,128]{1,0:T(8,128)S(1)}, u32[]{:S(2)}, u32[]{:S(2)}) %collective-permute-start.7) | collective-permute-done | bytes 4128 | tf_op jit(solution)/shard_map/ppermute | solution.py:27
  35.8 2.4 %collective-permute-start.10 = (f32[8,128]{1,0:T(8,128)S(1)}, f32[8,128]{1,0:T(8,128)S(1)}, u32[]{:S(2)}, u32[]{:S(2)}) collective-permute-start(f32[8,128]{1,0:T(8,128)S(1)} %merge.14.own), channel_id=1, source_target_pairs={{0,16},{1,17},{2,18},{3,19},{4,20},{5,21},{6,22},{7,23},{8,24},{9,... | collective-permute-start | bytes 12296 | tf_op jit(solution)/shard_map/ppermute | solution.py:27
  38.2 2.1 %collective-permute-done.10.others_0_ = f32[8,128]{1,0:T(8,128)S(1)} collective-permute-done((f32[8,128]{1,0:T(8,128)S(1)}, f32[8,128]{1,0:T(8,128)S(1)}, u32[]{:S(2)}, u32[]{:S(2)}) %collective-permute-start.10) | collective-permute-done | bytes 4128 | tf_op jit(solution)/shard_map/ppermute | solution.py:27
  40.3 1.6 %collective-permute-start.11 = (f32[8,128]{1,0:T(8,128)S(1)}, f32[8,128]{1,0:T(8,128)S(1)}, u32[]{:S(2)}, u32[]{:S(2)}) collective-permute-start(f32[8,128]{1,0:T(8,128)S(1)} %merge.15.own), channel_id=1, source_target_pairs={{0,8},{1,9},{2,10},{3,11},{4,12},{5,13},{6,14},{7,15},{8,0},{9,1},... | collective-permute-start | bytes 12296 | tf_op jit(solution)/shard_map/ppermute | solution.py:27
  41.9 2.0 %collective-permute-done.11.others_0_ = f32[8,128]{1,0:T(8,128)S(1)} collective-permute-done((f32[8,128]{1,0:T(8,128)S(1)}, f32[8,128]{1,0:T(8,128)S(1)}, u32[]{:S(2)}, u32[]{:S(2)}) %collective-permute-start.11) | collective-permute-done | bytes 4128 | tf_op jit(solution)/shard_map/ppermute | solution.py:27
  43.9 0.0 collective-permute-start.12
  43.9 0.0 collective-permute-done.14.received_rest
  43.9 0.0 collective-permute-done.13.received_first
  44.0 0.2 settle.1
  44.1 1.0 %collective-permute-done.12.others_0_ = f32[8,128]{1,0:T(8,128)S(1)} collective-permute-done((f32[8,128]{1,0:T(8,128)S(1)}, f32[8,128]{1,0:T(8,128)S(1)}, u32[]{:S(2)}, u32[]{:S(2)}) %collective-permute-start.12) | collective-permute-done | bytes 4128 | tf_op jit(solution)/shard_map/ppermute | solution.py:27
  45.1 0.0 copy-done
  45.1 0.0 copy-done.1
  45.1 1.2 %finish.1 = (f32[4,32,512]{2,1,0:T(8,128)}, f32[4,32,512]{2,1,0:T(8,128)}, f32[4,32,512]{2,1,0:T(8,128)}) custom-call(f32[8,128]{1,0:T(8,128)S(1)} %merge.17.sums, f32[1,32]{1,0:T(1,128)S(1)} %bitcast.14, f32[4,32,512]{2,1,0:T(8,128)S(1)} %copy-done, f32[4,32,512]{2,1,0:T(8,128)S(1)} %get-tuple-element.37.masked, ...), custom_call_target="tpu_custom_call" | custom-call | tf_op jit(solution)/shard_map/finish/pallas_call | solution.py:707
  (9 shorter events, 0.0 us)
Async XLA Ops:
  1.6 6.5 %collective-permute-start = (f32[88,512]{1,0:T(8,128)S(1)}, f32[88,512]{1,0:T(8,128)S(1)}, u32[]{:S(2)}, u32[]{:S(2)}) collective-permute-start(f32[88,512]{1,0:T(8,128)S(1)} %first.1), channel_id=1, source_target_pairs={{0,1},{1,2},{2,3},{3,4},{4,5},{5,6},{6,7},{7,8},{8,9},{9,10},{10,1... | collective-permute-start | bytes 540680 | tf_op jit(solution)/shard_map/ppermute | solution.py:22
  8.3 6.8 %collective-permute-start.1 = (f32[24,128]{1,0:T(8,128)S(1)}, f32[24,128]{1,0:T(8,128)S(1)}, u32[]{:S(2)}, u32[]{:S(2)}) collective-permute-start(f32[24,128]{1,0:T(8,128)S(1)} %cross.1.order.own), channel_id=1, source_target_pairs={{0,8},{1,9},{2,10},{3,11},{4,12},{5,13},{6,14},{7,15},{8,0},{9,1},... | collective-permute-start | bytes 36872 | tf_op jit(solution)/shard_map/ppermute | solution.py:27
  15.2 4.7 %collective-permute-start.2 = (f32[24,128]{1,0:T(8,128)S(1)}, f32[24,128]{1,0:T(8,128)S(1)}, u32[]{:S(2)}, u32[]{:S(2)}) collective-permute-start(f32[24,128]{1,0:T(8,128)S(1)} %merge.9.own), channel_id=1, source_target_pairs={{0,16},{1,17},{2,18},{3,19},{4,20},{5,21},{6,22},{7,23},{8,24},{9,... | collective-permute-start | bytes 36872 | tf_op jit(solution)/shard_map/ppermute | solution.py:27
  18.2 25.8 %collective-permute-start.13 = (f32[56,512]{1,0:T(8,128)S(1)}, f32[56,512]{1,0:T(8,128)S(1)}, u32[]{:S(2)}, u32[]{:S(2)}) collective-permute-start(f32[56,512]{1,0:T(8,128)S(1)} %get-tuple-element.44.others_1_), channel_id=1, source_target_pairs={{1,0},{2,1},{3,2},{4,3},{5,4},{6,5},{7,6},{8,7},{9,8},{10,9},{11,1... | collective-permute-start | bytes 344072 | tf_op jit(solution)/shard_map/ppermute | solution.py:22
  19.9 3.7 %collective-permute-start.3 = (f32[1,24,128]{2,1,0:T(8,128)S(1)}, f32[1,24,128]{2,1,0:T(8,128)S(1)}, u32[]{:S(2)}, u32[]{:S(2)}) collective-permute-start(f32[1,24,128]{2,1,0:T(8,128)S(1)} %bitcast.12), channel_id=1, source_target_pairs={{0,4},{1,5},{2,6},{3,7},{4,0},{5,1},{6,2},{7,3},{8,12},{9,13},{10,... | collective-permute-start | bytes 36872 | tf_op jit(solution)/shard_map/ppermute | solution.py:27
  20.8 6.6 %collective-permute-start.6 = (f32[8,2560]{1,0:T(8,128)S(1)}, f32[8,2560]{1,0:T(8,128)S(1)}, u32[]{:S(2)}, u32[]{:S(2)}) collective-permute-start(f32[8,2560]{1,0:T(8,128)S(1)} %get-tuple-element.45), channel_id=1, source_target_pairs={{1,0},{2,1},{3,2},{4,3},{5,4},{6,5},{7,6},{8,7},{9,8},{10,9},{11,1... | collective-permute-start | bytes 245768 | tf_op jit(solution)/shard_map/ppermute | solution.py:22
  23.6 3.8 %collective-permute-start.4 = (f32[2,24,128]{2,1,0:T(8,128)S(1)}, f32[2,24,128]{2,1,0:T(8,128)S(1)}, u32[]{:S(2)}, u32[]{:S(2)}) collective-permute-start(f32[2,24,128]{2,1,0:T(8,128)S(1)} %bitcast.10), channel_id=1, source_target_pairs={{0,2},{1,3},{2,0},{3,1},{4,6},{5,7},{6,4},{7,5},{8,10},{9,11},{10,... | collective-permute-start | bytes 73736 | tf_op jit(solution)/shard_map/ppermute | solution.py:27
  24.7 19.3 %collective-permute-start.14 = (f32[40,512]{1,0:T(8,128)S(1)}, f32[40,512]{1,0:T(8,128)S(1)}, u32[]{:S(2)}, u32[]{:S(2)}) collective-permute-start(f32[40,512]{1,0:T(8,128)S(1)} %get-tuple-element.59), channel_id=1, source_target_pairs={{1,0},{2,1},{3,2},{4,3},{5,4},{6,5},{7,6},{8,7},{9,8},{10,9},{11,1... | collective-permute-start | bytes 245768 | tf_op jit(solution)/shard_map/ppermute | solution.py:22
  27.4 1.2 %collective-permute-start.5 = (f32[4,24,128]{2,1,0:T(8,128)S(1)}, f32[4,24,128]{2,1,0:T(8,128)S(1)}, u32[]{:S(2)}, u32[]{:S(2)}) collective-permute-start(f32[4,24,128]{2,1,0:T(8,128)S(1)} %bitcast.6), channel_id=1, source_target_pairs={{0,1},{1,0},{2,3},{3,2},{4,5},{5,4},{6,7},{7,6},{8,9},{9,8},{10,11... | collective-permute-start | bytes 147464 | tf_op jit(solution)/shard_map/ppermute | solution.py:27
  29.4 5.4 %collective-permute-start.9 = (f32[8,128]{1,0:T(8,128)S(1)}, f32[8,128]{1,0:T(8,128)S(1)}, u32[]{:S(2)}, u32[]{:S(2)}) collective-permute-start(f32[8,128]{1,0:T(8,128)S(1)} %get-tuple-element.54.order.own), channel_id=1, source_target_pairs={{0,6},{1,7},{2,4},{3,5},{4,2},{5,3},{6,0},{7,1},{8,14},{9,15},{10,... | collective-permute-start | bytes 12296 | tf_op jit(solution)/shard_map/ppermute | solution.py:27
  31.4 3.6 %collective-permute-start.8 = (f32[8,128]{1,0:T(8,128)S(1)}, f32[8,128]{1,0:T(8,128)S(1)}, u32[]{:S(2)}, u32[]{:S(2)}) collective-permute-start(f32[8,128]{1,0:T(8,128)S(1)} %get-tuple-element.54.order.own), channel_id=1, source_target_pairs={{0,4},{1,5},{2,6},{3,7},{4,0},{5,1},{6,2},{7,3},{8,12},{9,13},{10,... | collective-permute-start | bytes 12296 | tf_op jit(solution)/shard_map/ppermute | solution.py:27
  32.2 3.6 %collective-permute-start.7 = (f32[8,128]{1,0:T(8,128)S(1)}, f32[8,128]{1,0:T(8,128)S(1)}, u32[]{:S(2)}, u32[]{:S(2)}) collective-permute-start(f32[8,128]{1,0:T(8,128)S(1)} %get-tuple-element.54.order.own), channel_id=1, source_target_pairs={{0,2},{1,3},{2,0},{3,1},{4,6},{5,7},{6,4},{7,5},{8,10},{9,11},{10,... | collective-permute-start | bytes 12296 | tf_op jit(solution)/shard_map/ppermute | solution.py:27
  33.0 12.2 %copy-start = (f32[4,32,512]{2,1,0:T(8,128)S(1)}, f32[4,32,512]{2,1,0:T(8,128)}, u32[]{:S(2)}) copy-start(f32[4,32,512]{2,1,0:T(8,128)} %multipliers.1) | copy-start | bytes 786436
  33.0 12.2 %copy-start.1 = (f32[32]{0:T(128)S(1)}, f32[32]{0:T(128)}, u32[]{:S(2)}) copy-start(f32[32]{0:T(128)} %param.11) | copy-start | bytes 388
  35.8 4.5 %collective-permute-start.10 = (f32[8,128]{1,0:T(8,128)S(1)}, f32[8,128]{1,0:T(8,128)S(1)}, u32[]{:S(2)}, u32[]{:S(2)}) collective-permute-start(f32[8,128]{1,0:T(8,128)S(1)} %merge.14.own), channel_id=1, source_target_pairs={{0,16},{1,17},{2,18},{3,19},{4,20},{5,21},{6,22},{7,23},{8,24},{9,... | collective-permute-start | bytes 12296 | tf_op jit(solution)/shard_map/ppermute | solution.py:27
  40.3 3.6 %collective-permute-start.11 = (f32[8,128]{1,0:T(8,128)S(1)}, f32[8,128]{1,0:T(8,128)S(1)}, u32[]{:S(2)}, u32[]{:S(2)}) collective-permute-start(f32[8,128]{1,0:T(8,128)S(1)} %merge.15.own), channel_id=1, source_target_pairs={{0,8},{1,9},{2,10},{3,11},{4,12},{5,13},{6,14},{7,15},{8,0},{9,1},... | collective-permute-start | bytes 12296 | tf_op jit(solution)/shard_map/ppermute | solution.py:27
  43.9 1.2 %collective-permute-start.12 = (f32[8,128]{1,0:T(8,128)S(1)}, f32[8,128]{1,0:T(8,128)S(1)}, u32[]{:S(2)}, u32[]{:S(2)}) collective-permute-start(f32[8,128]{1,0:T(8,128)S(1)} %merge.16.order.own), channel_id=1, source_target_pairs={{0,1},{1,0},{2,3},{3,2},{4,5},{5,4},{6,7},{7,6},{8,9},{9,8},{10,11... | collective-permute-start | bytes 12296 | tf_op jit(solution)/shard_map/ppermute | solution.py:27
